TPU v7x, 32 devices: a whole 2x2x4 slice. The times are simulated.
32 devices in a mesh: wide: 8 (over y, x, core), narrow: 4 (over z).
Axes of the slice: x: 2, y: 2, z: 4, core: 2. Of those that a mesh axis runs over, the one named last changes fastest.
Arguments:
- patches: bfloat16 [16384, 768], P(('wide', 'narrow')), may hold values from -6 to 6
- patch_rows: int32 [16384], P(('wide', 'narrow')), may hold values from 0 to 255
- patch_cols: int32 [16384], P(('wide', 'narrow')), may hold values from 0 to 255
- input_ids: int32 [8192], P(('wide', 'narrow')), may hold values from 0 to 50303
- target_ids: int32 [8192], P(('wide', 'narrow')), may hold values from 0 to 50303
- target_lengths: int32 [8], P('wide'), may hold values from 1 to 1024, 5120 in all
- loss_mask: int32 [8, 1024], P('wide'), may hold values 0 or 1
- master_slabs: float32 [192, 768, 128], P(('wide', 'narrow')), may hold values from -0.21875 to 0.21875
- left_stats: float32 [192, 768, 768], P(('wide', 'narrow'))
- left_roots: float32 [192, 768, 768], P(('wide', 'narrow'))
- right_stats: float32 [192, 128, 128], P(('wide', 'narrow'))
- right_roots: float32 [192, 128, 128], P(('wide', 'narrow'))
- block_slot: int32 [192], replicated, may hold values from 0 to 191, each once
- vocab_table: float32 [50304, 768], P('wide', 'narrow'), may hold values from -6 to 6
- vocab_first: float32 [50304, 768], P('wide', 'narrow'), may hold values from -3.8146973e-06 to 3.8146973e-06
- vocab_second: float32 [50304, 768], P('wide', 'narrow'), may hold values from 3.5626664e-13 to 1.4250666e-12
- small_params: float32 [520, 768], replicated
- small_first: float32 [520, 768], replicated, may hold values from -1.9073486e-05 to 1.9073486e-05
- small_second: float32 [520, 768], replicated, may hold values from 3.5626664e-12 to 1.4250666e-11
- step_count: int32 [], replicated, may hold values from 2 to 20
Outputs:
- loss_sum: float32 [], replicated
- count_total: float32 [], replicated
- master_new: float32 [192, 768, 128], P(('wide', 'narrow'))
- weights_low: bfloat16 [192, 768, 128], P(('wide', 'narrow'))
- slab_grads: float32 [192, 768, 128], P(('wide', 'narrow'))
- left_new: float32 [192, 768, 768], P(('wide', 'narrow'))
- right_new: float32 [192, 128, 128], P(('wide', 'narrow'))
- vocab_new: float32 [50304, 768], P('wide', 'narrow')
- vocab_low: bfloat16 [50304, 768], P('wide', 'narrow')
- vocab_first_new: float32 [50304, 768], P('wide', 'narrow')
- vocab_second_new: float32 [50304, 768], P('wide', 'narrow')
- small_new: float32 [520, 768], replicated
- small_first_new: float32 [520, 768], replicated
- small_second_new: float32 [520, 768], replicated
- grad_norm: float32 [], replicated
Inputs may be any that keep to these rules, and one draw needn't show every extreme that they name: `block_slot`: each slot once; its first 174 entries place the blocks, slot s lies on device s // 6 in wide-major order. `target_lengths`: the longest target fills all 1024 slots.
All inputs are finite; a program needn't handle non-finite values. No bound on the sum of `target_lengths` or of `loss_mask` on one device may be relied on, other than what follows from the above.
Results may differ from a plain program's by a relative error of at most 0.0089.
Values may be sent and summed in bfloat16 or wider, within the bound.
No kernel may reach another device: no remote copies, remote signals or barrier semaphores. Data moves between devices by JAX's collectives and lax.ppermute only.
A program may use at most 576 MiB of HBM per device.

v0:
```python
import math

import jax
import jax.numpy as jnp
from jax import lax
from jax.sharding import PartitionSpec as P

D = 768
HEADS = 12
HEAD_DIM = 64
FF = 2048
POS = 256
PATCHES = 2048
TGT = 1024
SCREENS_GRP = 1
BW = 128
BLOCKS = 174


highest = lax.Precision.HIGHEST
attn_scale = 0.125
norm_eps = 1e-06
clip_limit = 0.02
stat_decay = 0.5
rate_shampoo = 0.02
rate_adam = 0.5
beta_first = 0.9
beta_second = 0.95
adam_eps = 1e-08
weight_decay = 0.01


def joined(shard, axis, combine):
    everything = jax.tree.map(lambda part: lax.all_gather(part, axis), shard)
    leading = jax.tree.map(lambda part: part[0], everything)

    def lap(k, so_far):
        return combine(so_far, jax.tree.map(lambda part: part[k], everything))

    return lax.fori_loop(1, lax.axis_size(axis), lap, leading)


def product(left, right):
    return jnp.dot(left, right, preferred_element_type=jnp.float32)


def product_trans(left, right):
    return lax.dot_general(
        left, right, (((1,), (1,)), ((), ())), preferred_element_type=jnp.float32
    )


def outer_sum(left, right):
    return lax.dot_general(
        left, right, (((0,), (0,)), ((), ())), preferred_element_type=jnp.float32
    )


def onehot_sum(onehot_low, rows_full):
    high_part = rows_full.astype(jnp.bfloat16)
    rest_part = (rows_full - high_part.astype(jnp.float32)).astype(jnp.bfloat16)
    return outer_sum(onehot_low, high_part) + outer_sum(onehot_low, rest_part)


def matrix_part(weights, number):
    extents = [D, 3 * D, D, 2 * FF, FF, 3 * D, D, D, 2 * D, D, 2 * FF, FF]
    offset = sum(extents[:number])
    return weights[:, offset : offset + extents[number]]


def rms_norm(values, gain_vec):
    return (
        values * lax.rsqrt(jnp.mean(values * values, axis=-1, keepdims=True) + norm_eps) * gain_vec
    )


def norm_back(values, gain_vec, grad_out):
    _, pullback = jax.vjp(rms_norm, values, gain_vec)
    return pullback(grad_out)


def gated_unit(gate_up):
    return jax.nn.gelu(gate_up[:, :FF], approximate=True) * gate_up[:, FF:]


def head_major(values):
    return values.reshape(values.shape[0], HEADS, HEAD_DIM).transpose(1, 0, 2)


def token_major(values):
    return values.transpose(1, 0, 2).reshape(values.shape[1], -1)


def attend(queries, keys_all, values_all, allowed):

    def one_head(operands):
        query_part, key_part, value_part = operands
        scores = jnp.where(allowed, product_trans(query_part, key_part) * attn_scale, -1000000000.0)
        top_score = jnp.max(scores, axis=-1, keepdims=True)
        exponent = jnp.exp(scores - top_score)
        summed = jnp.sum(exponent, axis=-1, keepdims=True)
        mixed_part = product((exponent / summed).astype(jnp.bfloat16), value_part)
        return (mixed_part, top_score + jnp.log(summed))

    mixed_rows, log_total = lax.map(
        one_head, (head_major(queries), head_major(keys_all), head_major(values_all))
    )
    return (token_major(mixed_rows).astype(jnp.bfloat16), log_total)


def attend_back(queries, keys_all, values_all, allowed, log_total, grad_mixed):

    def one_head(operands):
        query_part, key_part, value_part, head_total, grad_part = operands
        scores = jnp.where(allowed, product_trans(query_part, key_part) * attn_scale, -1000000000.0)
        attention_probs = jnp.exp(scores - head_total)
        grad_probs = product_trans(grad_part, value_part)
        row_delta = jnp.sum(attention_probs * grad_probs, axis=-1, keepdims=True)
        grad_scores = (attention_probs * (grad_probs - row_delta)).astype(jnp.bfloat16)
        grad_query = product(grad_scores, key_part) * attn_scale
        grad_key = outer_sum(grad_scores, query_part) * attn_scale
        grad_value = outer_sum(attention_probs.astype(jnp.bfloat16), grad_part)
        return (grad_query, grad_key, grad_value)

    results = lax.map(
        one_head,
        (
            head_major(queries),
            head_major(keys_all),
            head_major(values_all),
            log_total,
            head_major(grad_mixed),
        ),
    )
    return tuple((token_major(result) for result in results))


def gather_keys(keys_local, values_local):
    keys_all, values_all = (
        lax.all_gather(keys_local, "narrow", axis=0, tiled=True),
        lax.all_gather(values_local, "narrow", axis=0, tiled=True),
    )
    return (keys_all, values_all)


def return_keys(grad_key, grad_value):
    return (
        lax.psum_scatter(
            grad_key.astype(jnp.bfloat16), "narrow", scatter_dimension=0, tiled=True
        ).astype(jnp.float32),
        lax.psum_scatter(
            grad_value.astype(jnp.bfloat16), "narrow", scatter_dimension=0, tiled=True
        ).astype(jnp.float32),
    )


def feed_forward(stream, gain_vec, w_in, w_back):
    normed = rms_norm(stream, gain_vec).astype(jnp.bfloat16)
    gate_up = product(normed, w_in)
    hidden = gated_unit(gate_up).astype(jnp.bfloat16)
    return (product_trans(hidden, w_back), (normed, gate_up, hidden))


def feed_back(stream, gain_vec, w_in, w_back, kept_state, grad_out):
    normed, gate_up, hidden = kept_state
    grad_low = grad_out.astype(jnp.bfloat16)
    grad_w_back = outer_sum(grad_low, hidden)
    _, pullback = jax.vjp(gated_unit, gate_up)
    grad_gate_up = pullback(product(grad_low, w_back))[0].astype(jnp.bfloat16)
    grad_w_in = outer_sum(normed, grad_gate_up)
    grad_stream, grad_gain = norm_back(stream, gain_vec, product_trans(grad_gate_up, w_in))
    return (grad_stream, grad_gain, grad_w_in, grad_w_back)


def attention_back(queries, given_keys, allowed, log_total, mixed_rows, w_out, grad_out):
    grad_low = grad_out.astype(jnp.bfloat16)
    grad_w_out = outer_sum(mixed_rows, grad_low)
    grad_mixed = product_trans(grad_low, w_out).astype(jnp.bfloat16)
    grad_query, grad_key, grad_value = attend_back(
        queries, given_keys[0], given_keys[1], allowed, log_total, grad_mixed
    )
    grad_key, grad_value = return_keys(grad_key, grad_value)
    return (grad_w_out, grad_query, grad_key, grad_value)


def encode(weights, small_params, patches, rows_ids, cols_ids, given_keys):
    gain_rows = small_params[2 * POS :]
    stream_zero = (
        product(patches, matrix_part(weights, 0))
        + gain_rows[7]
        + jnp.take(small_params, rows_ids, axis=0)
        + jnp.take(small_params, POS + cols_ids, axis=0)
    )
    normed_zero = rms_norm(stream_zero, gain_rows[0]).astype(jnp.bfloat16)
    mix_rows = product(normed_zero, matrix_part(weights, 1)).astype(jnp.bfloat16)
    given_keys = gather_keys(mix_rows[:, D : 2 * D], mix_rows[:, 2 * D :])
    allowed = jnp.ones((patches.shape[0], PATCHES), bool)
    mixed_rows, log_total = attend(mix_rows[:, :D], given_keys[0], given_keys[1], allowed)
    stream_one = stream_zero + product(mixed_rows, matrix_part(weights, 2))
    branch, ffn_state = feed_forward(
        stream_one, gain_rows[1], matrix_part(weights, 3), matrix_part(weights, 4)
    )
    stream_two = stream_one + branch
    kept_state = (
        stream_zero,
        normed_zero,
        mix_rows,
        given_keys,
        allowed,
        log_total,
        mixed_rows,
        stream_one,
        ffn_state,
        stream_two,
    )
    return (rms_norm(stream_two, gain_rows[2]), kept_state)


def encode_back(weights, small_params, patches, rows_ids, cols_ids, kept_state, grad_encoded):
    gain_rows = small_params[2 * POS :]
    (
        stream_zero,
        normed_zero,
        mix_rows,
        given_keys,
        allowed,
        log_total,
        mixed_rows,
        stream_one,
        ffn_state,
        stream_two,
    ) = kept_state
    grad_two, gain_final = norm_back(stream_two, gain_rows[2], grad_encoded)
    grad_one, gain_ffn, grad_in, grad_back = feed_back(
        stream_one,
        gain_rows[1],
        matrix_part(weights, 3),
        matrix_part(weights, 4),
        ffn_state,
        grad_two,
    )
    grad_one = grad_one + grad_two
    grad_w_out, grad_query, grad_key, grad_value = attention_back(
        mix_rows[:, :D],
        given_keys,
        allowed,
        log_total,
        mixed_rows,
        matrix_part(weights, 2),
        grad_one,
    )
    grad_mix = jnp.concatenate([grad_query, grad_key, grad_value], axis=1).astype(jnp.bfloat16)
    grad_w_mix = outer_sum(normed_zero, grad_mix)
    grad_zero, gain_attn = norm_back(
        stream_zero, gain_rows[0], product_trans(grad_mix, matrix_part(weights, 1))
    )
    grad_zero = grad_zero + grad_one
    grad_patch = outer_sum(patches, grad_zero.astype(jnp.bfloat16))
    row_onehot = (rows_ids[:, None] == jnp.arange(POS)[None, :]).astype(jnp.bfloat16)
    col_onehot = (cols_ids[:, None] == jnp.arange(POS)[None, :]).astype(jnp.bfloat16)
    tables = jnp.concatenate(
        [onehot_sum(row_onehot, grad_zero), onehot_sum(col_onehot, grad_zero)], axis=0
    )
    return (
        [grad_patch, grad_w_mix, grad_w_out, grad_in, grad_back],
        [gain_attn, gain_ffn, gain_final],
        tables,
        jnp.sum(grad_zero, axis=0),
    )


def decode(weights, small_params, stream_zero, encoded_low, positions):
    gain_rows = small_params[2 * POS :]
    normed_zero = rms_norm(stream_zero, gain_rows[3]).astype(jnp.bfloat16)
    mix_rows = product(normed_zero, matrix_part(weights, 5)).astype(jnp.bfloat16)
    self_keys = gather_keys(mix_rows[:, D : 2 * D], mix_rows[:, 2 * D :])
    causal = jnp.arange(TGT)[None, :] <= positions[:, None]
    self_mask = jnp.arange(TGT)[:, None] >= positions[None, :]
    mixed_self, total_self = attend(mix_rows[:, :D], self_keys[0], self_keys[1], causal)
    stream_one = stream_zero + product(mixed_self, matrix_part(weights, 6))
    normed_one = rms_norm(stream_one, gain_rows[4]).astype(jnp.bfloat16)
    query_rows = product(normed_one, matrix_part(weights, 7)).astype(jnp.bfloat16)
    pair_rows = product(encoded_low, matrix_part(weights, 8)).astype(jnp.bfloat16)
    cross_keys = gather_keys(pair_rows[:, :D], pair_rows[:, D:])
    open_mask = jnp.ones((stream_zero.shape[0], PATCHES), bool)
    mixed_cross, total_cross = attend(query_rows, cross_keys[0], cross_keys[1], open_mask)
    stream_two = stream_one + product(mixed_cross, matrix_part(weights, 9))
    branch, ffn_state = feed_forward(
        stream_two, gain_rows[5], matrix_part(weights, 10), matrix_part(weights, 11)
    )
    stream_three = stream_two + branch
    kept_state = (
        stream_zero,
        normed_zero,
        mix_rows,
        self_keys,
        causal,
        self_mask,
        mixed_self,
        total_self,
        stream_one,
        normed_one,
        query_rows,
        pair_rows,
        cross_keys,
        open_mask,
        mixed_cross,
        total_cross,
        stream_two,
        ffn_state,
        stream_three,
    )
    return (rms_norm(stream_three, gain_rows[6]) * D ** (-0.5), kept_state)


def decode_back(weights, small_params, encoded_low, kept_state, grad_final):
    gain_rows = small_params[2 * POS :]
    (
        stream_zero,
        normed_zero,
        mix_rows,
        self_keys,
        causal,
        self_mask,
        mixed_self,
        total_self,
        stream_one,
        normed_one,
        query_rows,
        pair_rows,
        cross_keys,
        open_mask,
        mixed_cross,
        total_cross,
        stream_two,
        ffn_state,
        stream_three,
    ) = kept_state
    grad_three, gain_final = norm_back(stream_three, gain_rows[6], grad_final * D ** (-0.5))
    grad_two, gain_ffn, grad_in, grad_back = feed_back(
        stream_two,
        gain_rows[5],
        matrix_part(weights, 10),
        matrix_part(weights, 11),
        ffn_state,
        grad_three,
    )
    grad_two = grad_two + grad_three
    grad_cout, grad_query, grad_key, grad_value = attention_back(
        query_rows,
        cross_keys,
        open_mask,
        total_cross,
        mixed_cross,
        matrix_part(weights, 9),
        grad_two,
    )
    grad_query = grad_query.astype(jnp.bfloat16)
    grad_w_query = outer_sum(normed_one, grad_query)
    grad_one, gain_cross = norm_back(
        stream_one, gain_rows[4], product_trans(grad_query, matrix_part(weights, 7))
    )
    grad_one = grad_one + grad_two
    grad_pair = jnp.concatenate([grad_key, grad_value], axis=1).astype(jnp.bfloat16)
    grad_w_pair = outer_sum(encoded_low, grad_pair)
    grad_encoded = product_trans(grad_pair, matrix_part(weights, 8))
    grad_w_out, grad_query, grad_key, grad_value = attention_back(
        mix_rows[:, :D],
        self_keys,
        causal,
        total_self,
        mixed_self,
        matrix_part(weights, 6),
        grad_one,
    )
    grad_mix = jnp.concatenate([grad_query, grad_key, grad_value], axis=1).astype(jnp.bfloat16)
    grad_w_mix = outer_sum(normed_zero, grad_mix)
    grad_zero, gain_self = norm_back(
        stream_zero, gain_rows[3], product_trans(grad_mix, matrix_part(weights, 5))
    )
    grad_zero = grad_zero + grad_one
    return (
        [grad_w_mix, grad_w_out, grad_w_query, grad_w_pair, grad_cout, grad_in, grad_back],
        [gain_self, gain_cross, gain_ffn, gain_final],
        grad_zero,
        grad_encoded,
    )


def combine_stats(first_part, second_part):
    top_logit = jnp.maximum(first_part[0], second_part[0])
    summed = first_part[1] * jnp.exp(first_part[0] - top_logit) + second_part[1] * jnp.exp(
        second_part[0] - top_logit
    )
    return (top_logit, summed, first_part[2] + second_part[2])


def adamw(param, moment, second, grad, step_count):
    moment = beta_first * moment + (1 - beta_first) * grad
    second = beta_second * second + (1 - beta_second) * grad * grad
    steps = step_count.astype(jnp.float32)
    m_hat = moment / (1 - jnp.power(beta_first, steps))
    v_hat = second / (1 - jnp.power(beta_second, steps))
    return (
        param - rate_adam * (m_hat / (jnp.sqrt(v_hat) + adam_eps) + weight_decay * param),
        moment,
        second,
    )


def shards(
    patches,
    patch_rows,
    patch_cols,
    input_ids,
    target_ids,
    target_lengths,
    loss_mask,
    master_slabs,
    left_stats,
    left_roots,
    right_stats,
    right_roots,
    block_slot,
    vocab_table,
    vocab_first,
    vocab_second,
    small_params,
    small_first,
    small_second,
    step_count,
):
    wide_count = lax.axis_size("wide")
    narrow_count = lax.axis_size("narrow")
    wide_pos = lax.axis_index("wide")
    narrow_pos = lax.axis_index("narrow")
    slot_total = block_slot.shape[0]
    own_count = master_slabs.shape[0]
    slot_ids = block_slot[:BLOCKS]
    all_slabs = lax.all_gather(
        master_slabs.astype(jnp.bfloat16), ("wide", "narrow"), axis=0, tiled=True
    )
    weights = jnp.take(all_slabs, slot_ids, axis=0).transpose(1, 0, 2).reshape(D, -1)
    embed_table = lax.all_gather(vocab_table.astype(jnp.bfloat16), "narrow", axis=1, tiled=True)
    vocab_rows = embed_table.shape[0]
    vocab_start = wide_pos * vocab_rows
    columns = jnp.arange(vocab_rows)
    ids_all, targets_all, lengths_all, masks_all = (
        lax.all_gather(input_ids, "wide", axis=0, tiled=True),
        lax.all_gather(target_ids, "wide", axis=0, tiled=True),
        lax.all_gather(target_lengths, "wide", axis=0, tiled=True),
        lax.all_gather(loss_mask, "wide", axis=0, tiled=True),
    )
    dec_rows = input_ids.shape[0]
    per_screen = narrow_count // SCREENS_GRP
    local_screen = narrow_pos // per_screen
    positions = narrow_pos % per_screen * dec_rows + jnp.arange(dec_rows)
    counted = (jnp.arange(TGT)[None, :] < lengths_all[:, None]) & (masks_all == 1)
    tokens_counted = jnp.maximum(jnp.sum(counted.astype(jnp.float32)), 1.0)
    screen_rows = jnp.arange(wide_count)[:, None] * SCREENS_GRP + local_screen
    row_counted = counted[screen_rows, positions[None, :]].reshape(-1).astype(jnp.float32)
    row_weight = row_counted / tokens_counted
    block_ids = ids_all - vocab_start
    onehot = (block_ids[:, None] == columns[None, :]).astype(jnp.bfloat16)
    stream_dec = lax.psum_scatter(
        product(onehot, embed_table).astype(jnp.bfloat16), "wide", scatter_dimension=0, tiled=True
    ).astype(jnp.float32)
    encoded, enc_state = encode(weights, small_params, patches, patch_rows, patch_cols, None)
    encoded_low = encoded.astype(jnp.bfloat16)
    final_normed, dec_state = decode(weights, small_params, stream_dec, encoded_low, positions)
    rows_all = lax.all_gather(final_normed.astype(jnp.bfloat16), "wide", axis=0, tiled=True)
    total_rows = rows_all.shape[0]
    block_rows = math.gcd(total_rows, 512)
    blocks = total_rows // block_rows
    target_cols = targets_all - vocab_start

    def block_stats(operands):
        rows_block, hit_block = operands
        logits = product_trans(rows_block, embed_table)
        top_logit = jnp.max(logits, axis=1)
        summed = jnp.sum(jnp.exp(logits - top_logit[:, None]), axis=1)
        target = jnp.sum(jnp.where(columns[None, :] == hit_block[:, None], logits, 0.0), axis=1)
        return (logits, top_logit, summed, target)

    rows_blocks = rows_all.reshape(blocks, block_rows, -1)
    target_blocks = target_cols.reshape(blocks, block_rows)
    logits_all, top_part, summed_part, target_part = lax.map(
        block_stats, (rows_blocks, target_blocks)
    )
    top_logit, summed, target = joined(
        (top_part.reshape(-1), summed_part.reshape(-1), target_part.reshape(-1)),
        "wide",
        combine_stats,
    )
    log_total = top_logit + jnp.log(summed)
    row_loss = row_counted * (log_total - target)
    loss_local = jnp.sum(lax.dynamic_slice_in_dim(row_loss, wide_pos * dec_rows, dec_rows))

    def block_grads(running, operands):
        rows_block, logits, hit_block, total_block, weight_block = operands
        hits = (columns[None, :] == hit_block[:, None]).astype(jnp.float32)
        grad_logits = (
            weight_block[:, None] * (jnp.exp(logits - total_block[:, None]) - hits)
        ).astype(jnp.bfloat16)
        return (running + outer_sum(grad_logits, rows_block), product(grad_logits, embed_table))

    grad_embed, grad_rows = lax.scan(
        block_grads,
        jnp.zeros(embed_table.shape, jnp.float32),
        (
            rows_blocks,
            logits_all,
            target_blocks,
            log_total.reshape(blocks, block_rows),
            row_weight.reshape(blocks, block_rows),
        ),
    )
    grad_final = lax.psum_scatter(
        grad_rows.reshape(total_rows, -1).astype(jnp.bfloat16),
        "wide",
        scatter_dimension=0,
        tiled=True,
    ).astype(jnp.float32)
    dec_weights, dec_gains, grad_stream_dec, grad_encoded = decode_back(
        weights, small_params, encoded_low, dec_state, grad_final
    )
    block_ids = ids_all - vocab_start
    onehot = (block_ids[:, None] == columns[None, :]).astype(jnp.bfloat16)
    grad_embed = grad_embed + onehot_sum(
        onehot,
        lax.all_gather(grad_stream_dec.astype(jnp.bfloat16), "wide", axis=0, tiled=True).astype(
            jnp.float32
        ),
    )
    encoded_again, enc_state = encode(weights, small_params, patches, patch_rows, patch_cols, None)
    enc_weights, enc_gains, tables, bias_grad = encode_back(
        weights, small_params, patches, patch_rows, patch_cols, enc_state, grad_encoded
    )
    grads_full = jnp.concatenate(enc_weights + dec_weights, axis=1)
    small_partial = jnp.concatenate(
        [tables, jnp.stack(enc_gains + dec_gains + [bias_grad])], axis=0
    )
    slot_match = slot_ids[None, :] == jnp.arange(slot_total)[:, None]
    slot_block = jnp.sum(jnp.where(slot_match, jnp.arange(BLOCKS)[None, :], 0), axis=1)
    slot_used = jnp.any(slot_match, axis=1)
    arranged = jnp.where(
        slot_used[None, :, None],
        jnp.take(grads_full.reshape(D, BLOCKS, BW), slot_block, axis=1),
        0.0,
    )
    slab_grad = lax.psum_scatter(
        arranged.reshape(D, -1), ("wide", "narrow"), scatter_dimension=1, tiled=True
    )
    vocab_grad = lax.psum_scatter(
        grad_embed.astype(jnp.bfloat16), "narrow", scatter_dimension=1, tiled=True
    ).astype(jnp.float32)
    partial_square = jnp.sum(slab_grad * slab_grad) + jnp.sum(vocab_grad * vocab_grad)
    small_grad, total_square, loss_sum = lax.psum(
        (small_partial, partial_square, loss_local), ("wide", "narrow")
    )
    grad_norm = jnp.sqrt(total_square + jnp.sum(small_grad * small_grad))
    factor = jnp.minimum(1.0, clip_limit / (grad_norm + 1e-06))
    slab_grad = slab_grad.reshape(D, own_count, BW).transpose(1, 0, 2) * factor
    left_new = stat_decay * left_stats + (1 - stat_decay) * jnp.einsum(
        "sik,sjk->sij", slab_grad, slab_grad, precision=highest
    )
    right_new = stat_decay * right_stats + (1 - stat_decay) * jnp.einsum(
        "ski,skj->sij", slab_grad, slab_grad, precision=highest
    )
    precond = jnp.einsum(
        "sij,sjk->sik",
        jnp.einsum("sij,sjk->sik", left_roots, slab_grad, precision=highest),
        right_roots,
        precision=highest,
    )
    scale_back = lax.rsqrt(jnp.mean(precond * precond, axis=(1, 2), keepdims=True) + norm_eps)
    master_new = master_slabs - rate_shampoo * precond * scale_back
    vocab_new, vocab_first_new, vocab_second_new = adamw(
        vocab_table, vocab_first, vocab_second, vocab_grad * factor, step_count
    )
    small_new, small_first_new, small_second_new = adamw(
        small_params, small_first, small_second, small_grad * factor, step_count
    )
    return (
        loss_sum,
        tokens_counted,
        master_new,
        master_new.astype(jnp.bfloat16),
        slab_grad,
        left_new,
        right_new,
        vocab_new,
        vocab_new.astype(jnp.bfloat16),
        vocab_first_new,
        vocab_second_new,
        small_new,
        small_first_new,
        small_second_new,
        grad_norm,
    )


def solution(mesh):
    in_specs = (
        P(("wide", "narrow"), None),
        P(("wide", "narrow")),
        P(("wide", "narrow")),
        P(("wide", "narrow")),
        P(("wide", "narrow")),
        P("wide"),
        P("wide", None),
        P(("wide", "narrow"), None, None),
        P(("wide", "narrow"), None, None),
        P(("wide", "narrow"), None, None),
        P(("wide", "narrow"), None, None),
        P(("wide", "narrow"), None, None),
        P(),
        P("wide", "narrow"),
        P("wide", "narrow"),
        P("wide", "narrow"),
        P(),
        P(),
        P(),
        P(),
    )
    out_specs = (
        P(),
        P(),
        P(("wide", "narrow"), None, None),
        P(("wide", "narrow"), None, None),
        P(("wide", "narrow"), None, None),
        P(("wide", "narrow"), None, None),
        P(("wide", "narrow"), None, None),
        P("wide", "narrow"),
        P("wide", "narrow"),
        P("wide", "narrow"),
        P("wide", "narrow"),
        P(),
        P(),
        P(),
        P(),
    )
    return jax.shard_map(shards, mesh=mesh, in_specs=in_specs, out_specs=out_specs, check_vma=False)
```

profile of v0, /device:TPU:0, one launch (start us, length us, event | category | flops | bytes accessed | tf_op | source)
XLA Modules:
  0.0 3355.2 jit_solution(11519601414064361483)
XLA Ops:
  38.5 149.0 %all-gather.17.cloned.1.call-done = bf16[6288,768]{0,1:T(8,128)(2,1)} async-done(((bf16[6288,192]{0,1:T(8,128)(2,1)}), bf16[6288,768]{0,1:T(8,128)(2,1)}) %all-gather.17.cloned.1.call-update) | async-done | bytes 9658384 | tf_op jit(solution)/shard_map/all_gather | solution.py:444
  217.2 186.8 %all-gather.19.cloned.1.call-done = bf16[192,768,128]{2,1,0:T(8,128)(2,1)} async-done(((bf16[6,768,128]{2,1,0:T(8,128)(2,1)}), bf16[192,768,128]{2,1,0:T(8,128)(2,1)}) %all-gather.19.cloned.1.call-update) | async-done | bytes 37748752 | tf_op jit(solution)/shard_map/all_gather | solution.py:440
  452.5 44.5 %copy.272 = bf16[768,174,128]{0,2,1:T(8,128)(2,1)} copy(bf16[768,174,128]{2,0,1:T(8,128)(2,1)} %select_bitcast_fusion) | data formatting | bytes 68419584 | tf_op jit(solution)/shard_map/jit(_take)/select_n | solution.py:443
  517.3 52.0 %all-gather.25.cloned.1.call-done = bf16[2048,768]{1,0:T(8,128)(2,1)} async-done(((bf16[512,768]{1,0:T(8,128)(2,1)}), bf16[2048,768]{1,0:T(8,128)(2,1)}) %all-gather.25.cloned.1.call-update) | async-done | bytes 3145744 | tf_op jit(solution)/shard_map/all_gather | solution.py:140
  580.5 53.0 %all-gather.27.cloned.1.call-done = bf16[2048,768]{1,0:T(8,128)(2,1)} async-done(((bf16[512,768]{1,0:T(8,128)(2,1)}), bf16[2048,768]{1,0:T(8,128)(2,1)}) %all-gather.27.cloned.1.call-update) | async-done | bytes 3145744 | tf_op jit(solution)/shard_map/all_gather | solution.py:141
  644.9 59.3 %while.140 = (s32[]{:T(128)}, bf16[12,512,64]{1,2,0:T(8,128)(2,1)S(1)}, bf16[12,512,64]{2,1,0:T(8,128)(2,1)}, bf16[12,2048,64]{2,1,0:T(8,128)(2,1)}, bf16[12,2048,64]{2,1,0:T(8,128)(2,1)}, /*index=5*/s32[]{:T(128)}) while((s32[]{:T(128)}, bf16[12,512,64]{1,2,0:T(8,128)(2,1)S(1)}, bf16[12,512,64]{2,1,0:T(8,128)(2,1)}, ...), condition=%wide.region_11.13_spmd, body=%wide.region_8.12_spmd.sunk | while | flops 277871616 | bytes 13905989 | solution.py:105
  795.6 53.0 %all-gather.31.cloned.1.call-done = bf16[2048,768]{1,0:T(8,128)(2,1)} async-done(((bf16[512,768]{1,0:T(8,128)(2,1)}), bf16[2048,768]{1,0:T(8,128)(2,1)}) %all-gather.31.cloned.1.call-update) | async-done | bytes 3145744 | tf_op jit(solution)/shard_map/all_gather | solution.py:141
  859.9 44.5 %while.141 = (s32[]{:T(128)}, bf16[12,256,64]{1,2,0:T(8,128)(2,1)S(1)}, f32[12,256,1]{1,2,0:T(1,128)S(1)}, bf16[12,256,64]{2,1,0:T(8,128)(2,1)S(1)}, bf16[12,204...) while((s32[]{:T(128)}, bf16[12,256,64]{1,2,0:T(8,128)(2,1)S(1)}, ...), condition=%wide.region_17.19_spmd, body=%wide.region_14.18_spmd.sunk | while | flops 137887488 | bytes 7483473 | solution.py:105
  978.6 111.9 %while.147 = (s32[]{:T(128)}, f32[4,512,6288]{1,2,0:T(8,128)}, f32[4,512]{1,0:T(4,128)S(1)}, f32[4,512]{1,0:T(4,128)S(1)}, f32[4,512]{1,0:T(4,128)S(1)}, /*index...) while((s32[]{:T(128)}, f32[4,512,6288]{1,2,0:T(8,128)}, ...), condition=%wide.region_24.26_spmd.clone, body=%wide.region_20.25_spmd.clone.sunk | while | flops 4964399616 | bytes 61983872 | solution.py:487
  1118.5 219.0 %while.149 = (s32[]{:T(128)}, f32[6288,768]{1,0:T(8,128)}, bf16[4,512,768]{2,1,0:T(8,128)(2,1)}, f32[4,512]{1,0:T(4,128)S(1)}, f32[4,512,6288]{1,2,0:T(8,128)}, ...) while((s32[]{:T(128)}, f32[6288,768]{1,0:T(8,128)}, ...), condition=%wide.region_38.40_spmd.clone.clone, body=%wide.region_37.39_spmd.clone.clone.sunk | while | flops 9938460672 | bytes 128402560 | solution.py:507
  1338.1 43.4 %reduce-scatter.13.cloned.1.call-done = bf16[256,768]{1,0:T(8,128)(2,1)} async-done(((bf16[2048,768]{1,0:T(8,128)(2,1)}), bf16[256,768]{1,0:T(8,128)(2,1)}) %reduce-scatter.13.cloned.1.call-update) | async-done | bytes 393232 | tf_op jit(solution)/shard_map/reduce_scatter | solution.py:518
  1402.8 103.6 %while.144 = (s32[]{:T(128)}, bf16[12,256,64]{1,2,0:T(8,128)(2,1)S(1)}, bf16[12,2048,64]{1,2,0:T(8,128)(2,1)}, bf16[12,2048,64]{1,2,0:T(8,128)(2,1)}, bf16[12,25...) while((s32[]{:T(128)}, ...), condition=%wide.region_44.46_spmd, body=%wide.region_42.45_spmd.sunk | while | flops 339885824 | bytes 18622568 | solution.py:125
  1511.6 90.6 %while.148 = (s32[]{:T(128)}, bf16[12,256,64]{1,2,0:T(8,128)(2,1)S(1)}, bf16[12,1024,64]{1,2,0:T(8,128)(2,1)}, bf16[12,1024,64]{1,2,0:T(8,128)(2,1)}, bf16[12,25...) while((s32[]{:T(128)}, ...), condition=%wide.region_59.61_spmd.clone, body=%wide.region_57.60_spmd.clone.sunk | while | flops 170475264 | bytes 9448561 | solution.py:125
  1604.4 66.3 %while.143 = (s32[]{:T(128)}, bf16[12,512,64]{1,2,0:T(8,128)(2,1)S(1)}, f32[12,512,1]{1,2,0:T(1,128)}, bf16[12,512,64]{2,1,0:T(8,128)(2,1)}, bf16[12,2048,64]{2,...) while((s32[]{:T(128)}, bf16[12,512,64]{1,2,0:T(8,128)(2,1)S(1)}, f32[12,512,1]{1,2,0:T(1,128)}, ...), condition=%wide.region_35.37_spmd, body=%wide.region_32.36_spmd.sunk | while | flops 277872128 | bytes 13916749 | solution.py:105
  1738.8 60.4 %reduce-scatter.17.cloned.1.call-done = bf16[512,768]{0,1:T(8,128)(2,1)} async-done(((bf16[2048,768]{0,1:T(8,128)(2,1)}), bf16[512,768]{0,1:T(8,128)(2,1)}) %reduce-scatter.17.cloned.1.call-update) | async-done | bytes 786448 | tf_op jit(solution)/shard_map/reduce_scatter | solution.py:151
  1833.0 125.2 %while.145 = (s32[]{:T(128)}, bf16[12,512,64]{1,2,0:T(8,128)(2,1)S(1)}, bf16[12,2048,64]{1,2,0:T(8,128)(2,1)}, bf16[12,2048,64]{1,2,0:T(8,128)(2,1)}, bf16[12,51...) while((s32[]{:T(128)}, ...), condition=%wide.region_52.54_spmd, body=%wide.region_50.53_spmd.sunk | while | flops 679640576 | bytes 34618472 | solution.py:125
  2038.9 42.2 %reduce-scatter.21.cloned.1.call-done = bf16[512,768]{0,1:T(8,128)(2,1)} async-done(((bf16[2048,768]{0,1:T(8,128)(2,1)}), bf16[512,768]{0,1:T(8,128)(2,1)}) %reduce-scatter.21.cloned.1.call-update) | async-done | bytes 786448 | tf_op jit(solution)/shard_map/reduce_scatter | solution.py:151
  2142.5 67.1 %copy.326 = f32[768,22272]{0,1:T(8,128)} copy(f32[768,22272]{1,0:T(8,128)} %convolution_dynamic-update-slice_fusion.5) | data formatting | bytes 136839168 | tf_op jit(solution)/shard_map/concatenate | solution.py:539
  2209.6 66.9 %copy.327 = f32[768,174,128]{2,0,1:T(8,128)} copy(f32[768,174,128]{0,2,1:T(8,128)} %bitcast.113) | data formatting | bytes 136839168 | tf_op jit(solution)/shard_map/reshape | solution.py:548
  2276.5 52.3 %gather_fusion.2 = f32[192,768,128]{2,1,0:T(8,128)} fusion(f32[768,174,128]{2,0,1:T(8,128)} %copy.327, s32[1024]{0:T(1024)} %get-tuple-element.1304), kind=kCustom, calls=%fused_computation.4 | custom fusion | bytes 150995712 | tf_op jit(solution)/shard_map/jit(_take)/gather | solution.py:548
  2328.8 73.0 %copy.328 = f32[768,192,128]{0,2,1:T(8,128)} copy(f32[768,192,128]{2,0,1:T(8,128)} %bitcast.116) | data formatting | bytes 150994944 | tf_op jit(solution)/shard_map/jit(_take)/gather | solution.py:548
  2401.8 50.3 %fusion.165 = f32[768,24576]{0,1:T(8,128)} fusion(f32[768,192,128]{0,2,1:T(8,128)} %copy.328, pred[24576]{0:T(1024)(128)(4,1)S(1)} %copy-done.87, pred[24576]{0:T(1024)(128)(4,1)S(1)} %copy-done.88), kind=kLoop, calls=%fused_computation.225 | loop fusion | flops 37748736 | bytes 151044096 | tf_op jit(solution)/shard_map/jit(_where)/select_n | solution.py:546
  2467.8 640.9 %reduce-scatter.27.cloned.1.call-done = f32[768,768]{0,1:T(8,128)} async-done(((f32[768,24576]{0,1:T(8,128)}), f32[768,768]{0,1:T(8,128)}) %reduce-scatter.27.cloned.1.call-update) | async-done | bytes 2359312 | tf_op jit(solution)/shard_map/reduce_scatter | solution.py:551
  3112.8 132.5 %all-reduce.8.cloned.1.call-done = f32[520,768]{1,0:T(8,128)} async-done(((f32[520,768]{1,0:T(8,128)}), f32[520,768]{1,0:T(8,128)}) %all-reduce.8.cloned.1.call-update) | async-done | bytes 1597456 | tf_op jit(solution)/shard_map/psum | solution.py:558
  (1150 shorter events, 1599.0 us)
Async XLA Ops:
  7.2 489.8 %copy-start = (bf16[512,768]{1,0:T(8,128)(2,1)S(1)}, bf16[512,768]{1,0:T(8,128)(2,1)}, u32[]{:S(2)}) copy-start(bf16[512,768]{1,0:T(8,128)(2,1)} %param.42) | copy-start | bytes 2359300
  7.2 180.3 %all-gather.17.cloned.1.call-start = ((), (), s32[]{:S(2)}) async-start(), calls=%async_computation.10 | async-start | bytes 12288000 | tf_op jit(solution)/shard_map/all_gather | solution.py:444
  11.4 392.6 %all-gather.19.cloned.1.call-start = ((), (), s32[]{:S(2)}) async-start(), calls=%async_computation.12 | async-start | bytes 38928384 | tf_op jit(solution)/shard_map/all_gather | solution.py:440
  14.4 492.6 %reduce-scatter.11.cloned.1.call-start = ((), (), s32[]{:S(2)}) async-start(), calls=%async_computation.11 | async-start | bytes 3538944 | tf_op jit(solution)/shard_map/reduce_scatter | solution.py:465
  38.4 461.8 %copy-start.118 = (f32[768]{0:T(1024)}, f32[768]{0:T(1024)S(1)}, u32[]{:S(2)}) copy-start(f32[768]{0:T(1024)S(1)} %get-tuple-element.1063) | copy-start | bytes 9220
  38.4 470.4 %copy-start.82 = (f32[768]{0:T(1024)}, f32[768]{0:T(1024)S(1)}, u32[]{:S(2)}) copy-start(f32[768]{0:T(1024)S(1)} %get-tuple-element.1066) | copy-start | bytes 9220
  216.9 352.3 %all-gather.25.cloned.1.call-start = ((), (), s32[]{:S(2)}) async-start(), calls=%async_computation.15 | async-start | bytes 3932160 | tf_op jit(solution)/shard_map/all_gather | solution.py:140
  506.4 127.1 %all-gather.27.cloned.1.call-start = ((), (), s32[]{:S(2)}) async-start(), calls=%async_computation.16 | async-start | bytes 3932160 | tf_op jit(solution)/shard_map/all_gather | solution.py:141
  507.0 215.7 %all-gather.21.cloned.1.call-start = ((), (), s32[]{:S(2)}) async-start(), calls=%async_computation.13 | async-start | bytes 1966080 | tf_op jit(solution)/shard_map/all_gather | solution.py:140
  513.1 214.1 %all-gather.23.cloned.1.call-start = ((), (), s32[]{:S(2)}) async-start(), calls=%async_computation.14 | async-start | bytes 1966080 | tf_op jit(solution)/shard_map/all_gather | solution.py:141
  516.8 267.4 %all-gather.29.cloned.1.call-start = ((), (), s32[]{:S(2)}) async-start(), calls=%async_computation.17 | async-start | bytes 3932160 | tf_op jit(solution)/shard_map/all_gather | solution.py:140
  721.9 126.7 %all-gather.31.cloned.1.call-start = ((), (), s32[]{:S(2)}) async-start(), calls=%async_computation.18 | async-start | bytes 3932160 | tf_op jit(solution)/shard_map/all_gather | solution.py:141
  731.7 246.9 %all-gather.33.cloned.1.call-start = ((), (), s32[]{:S(2)}) async-start(), calls=%async_computation.19 | async-start | bytes 3538944 | tf_op jit(solution)/shard_map/all_gather | solution.py:471
  919.0 462.5 %reduce-scatter.13.cloned.1.call-start = ((), (), s32[]{:S(2)}) async-start(), calls=%async_computation.20 | async-start | bytes 3538944 | tf_op jit(solution)/shard_map/reduce_scatter | solution.py:518
  1337.5 353.9 %reduce-scatter.23.cloned.1.call-start = ((), (), s32[]{:S(2)}) async-start(), calls=%async_computation.25 | async-start | bytes 1966080 | tf_op jit(solution)/shard_map/reduce_scatter | solution.py:148
  1602.2 89.2 %reduce-scatter.25.cloned.1.call-start = ((), (), s32[]{:S(2)}) async-start(), calls=%async_computation.26 | async-start | bytes 1966080 | tf_op jit(solution)/shard_map/reduce_scatter | solution.py:151
  1602.9 133.8 %reduce-scatter.15.cloned.1.call-start = ((), (), s32[]{:S(2)}) async-start(), calls=%async_computation.21 | async-start | bytes 3932160 | tf_op jit(solution)/shard_map/reduce_scatter | solution.py:148
  1603.5 195.7 %reduce-scatter.17.cloned.1.call-start = ((), (), s32[]{:S(2)}) async-start(), calls=%async_computation.22 | async-start | bytes 3932160 | tf_op jit(solution)/shard_map/reduce_scatter | solution.py:151
  1604.1 374.2 %all-gather.35.cloned.1.call-start = ((), (), s32[]{:S(2)}) async-start(), calls=%async_computation.28 | async-start | bytes 3538944 | tf_op jit(solution)/shard_map/all_gather | solution.py:531
  1696.7 342.2 %reduce-scatter.19.cloned.1.call-start = ((), (), s32[]{:S(2)}) async-start(), calls=%async_computation.23 | async-start | bytes 3932160 | tf_op jit(solution)/shard_map/reduce_scatter | solution.py:148
  1958.3 122.8 %reduce-scatter.21.cloned.1.call-start = ((), (), s32[]{:S(2)}) async-start(), calls=%async_computation.24 | async-start | bytes 3932160 | tf_op jit(solution)/shard_map/reduce_scatter | solution.py:151
  1978.2 485.5 %reduce-scatter.29.cloned.1.call-start = ((), (), s32[]{:S(2)}) async-start(), calls=%async_computation.29 | async-start | bytes 12288000 | tf_op jit(solution)/shard_map/reduce_scatter | solution.py:554
  2037.4 1071.3 %reduce-scatter.27.cloned.1.call-start = ((), (), s32[]{:S(2)}) async-start(), calls=%async_computation.27 | async-start | bytes 77856768 | tf_op jit(solution)/shard_map/reduce_scatter | solution.py:551
  2452.2 793.1 %all-reduce.8.cloned.1.call-start = ((), (), s32[]{:S(2)}) async-start(), calls=%async_computation.30 | async-start | bytes 3194880 | tf_op jit(solution)/shard_map/psum | solution.py:558
  (167 other events, 2811.6 us)
Sparse Core Ops, SparseCore 0:
  11.5 175.8 all-gather.16
  190.8 213.1 all-gather.18
  408.0 44.3 reduce-scatter.10
  506.5 62.6 all-gather.24
  571.3 62.1 all-gather.26
  635.6 35.7 all-gather.20
  673.6 35.9 all-gather.22
  722.0 62.1 all-gather.28
  786.4 62.1 all-gather.30
  919.1 31.0 all-gather.32
  1337.6 43.8 reduce-scatter.12
  1602.3 35.2 reduce-scatter.22
  1640.5 34.2 reduce-scatter.24
  1677.5 59.2 reduce-scatter.14
  1738.9 60.2 reduce-scatter.16
  1801.5 32.3 all-gather.34
  1958.4 60.1 reduce-scatter.18
  2020.8 60.2 reduce-scatter.20
  2084.0 167.5 reduce-scatter.28
  2452.3 656.2 reduce-scatter.26
  3114.6 130.6 all-reduce.7
where the time goes:
time: 3380 us; the launch traced here: 3360 us
  waiting for transfers between devices  1470 us (43%)
  matrix products  922 us (27%)
  local copies, waits for them, and re-layouts  630 us (19%)
  other arithmetic  206 us (6%)
  blocking collectives  103 us (3%)
    reduce_scatter x1, waiting for transfers between devices, shards(): lax.psum_scatter(arranged.reshape(D, -1), ('wide', 'narrow'), scatter_dim...  641 us
    dot_general x136, matrix products, product_trans(): lax.dot_general(left, right, (((1,), (1,)), ((), ())), preferred_element_...  321 us
    dot_general x103, matrix products, product(): return jnp.dot(left, right, preferred_element_type=jnp.float32)  284 us
    dot_general x94, matrix products, outer_sum(): lax.dot_general(left, right, (((0,), (0,)), ((), ())), preferred_element_...  280 us
    all_gather x1, waiting for transfers between devices, shards(): lax.all_gather(master_slabs.astype(jnp.bfloat16), ('wide', 'narrow'), axi...  187 us
    all_gather x1, waiting for transfers between devices, shards(): lax.all_gather(vocab_table.astype(jnp.bfloat16), 'narrow', axis=1, tiled=...  149 us
    psum x1, waiting for transfers between devices, shards(): lax.psum((small_partial, partial_square, loss_local), ('wide', 'narrow'))  132 us
    gather x2, local copies, waits for them, and re-layouts, shards(): jnp.take(grads_full.reshape(D, BLOCKS, BW), slot_block, axis=1)  125 us
  transfers between devices with their start and end apart: 21, of which 12 were waited for; matrix products, arithmetic and copies ran while one was open for 32% of the time, Pallas kernels for 0%

commit v1 on v0

v1 whole, which is shorter than its diff:
```python
import jax
import jax.numpy as jnp
from jax import lax
from jax.experimental import pallas as pl
from jax.experimental.pallas import tpu as pltpu
from jax.sharding import PartitionSpec as P

HEAD_DIM = 64
D = 768
attn_scale = 0.125
KERNEL_VMEM = 56 * 1024 * 1024


def dot_nt(left, right):
    return lax.dot_general(
        left, right, (((1,), (1,)), ((), ())), preferred_element_type=jnp.float32
    )


def dot_nn(left, right):
    return lax.dot_general(
        left, right, (((1,), (0,)), ((), ())), preferred_element_type=jnp.float32
    )


def dot_tn(left, right):
    return lax.dot_general(
        left, right, (((0,), (0,)), ((), ())), preferred_element_type=jnp.float32
    )


def attend_kernel(masked, row_step, *refs):
    if masked:
        query_pos, key_pos, q_ref, k_ref, v_ref, out_ref, lse_ref = refs
    else:
        q_ref, k_ref, v_ref, out_ref, lse_ref = refs
    keys = k_ref[...]
    values = v_ref[...]
    key_lane = lax.broadcasted_iota(jnp.int32, values.shape, 1) // HEAD_DIM
    lane = lax.broadcasted_iota(jnp.int32, (row_step, 128), 1) // HEAD_DIM
    one = jnp.ones((), values.dtype)
    sides = [jnp.where(key_lane == side, values, one) for side in range(2)]
    for start in range(0, q_ref.shape[0], row_step):
        rows = pl.ds(start, row_step)
        queries = q_ref[rows, :]
        mixed, totals = [], []
        for side in range(2):
            half = jnp.where(lane == side, queries, jnp.zeros((), queries.dtype)) * attn_scale
            scores = dot_nt(half.astype(jnp.bfloat16), keys)
            if masked:
                scores = jnp.where(key_pos[...] <= query_pos[rows, :], scores, -1000000000.0)
            top = jnp.max(scores, axis=1, keepdims=True)
            exponent = jnp.exp(scores - top).astype(jnp.bfloat16)
            both = dot_nn(exponent, sides[side])
            other = (1 - side) * HEAD_DIM
            summed = both[:, other : other + 1]
            mixed.append(both / summed)
            totals.append(top + jnp.log(summed))
        out_ref[rows, :] = jnp.where(lane == 0, mixed[0], mixed[1]).astype(out_ref.dtype)
        lse_ref[rows, :] = jnp.where(lane == 0, totals[0], totals[1])


def attend(queries, keys_values, positions):
    rows, keys = queries.shape[0], keys_values.shape[0]
    pairs = D // 128
    row_step = min(rows, 256)
    extra, extra_specs = (), []
    if positions is not None:
        query_pos, key_pos = positions
        extra = (query_pos.reshape(rows, 1), key_pos.reshape(1, keys))
        extra_specs = [
            pl.BlockSpec((rows, 1), lambda j: (0, 0)),
            pl.BlockSpec((1, keys), lambda j: (0, 0)),
        ]
    return pl.pallas_call(
        lambda *refs: attend_kernel(positions is not None, row_step, *refs),
        grid=(pairs,),
        in_specs=extra_specs
        + [
            pl.BlockSpec((rows, 128), lambda j: (0, j)),
            pl.BlockSpec((keys, 128), lambda j: (0, j)),
            pl.BlockSpec((keys, 128), lambda j: (0, j + pairs)),
        ],
        out_specs=[
            pl.BlockSpec((rows, 128), lambda j: (0, j)),
            pl.BlockSpec((rows, 128), lambda j: (0, j)),
        ],
        out_shape=[
            jax.ShapeDtypeStruct((rows, D), jnp.bfloat16),
            jax.ShapeDtypeStruct((rows, D), jnp.float32),
        ],
        compiler_params=pltpu.CompilerParams(vmem_limit_bytes=KERNEL_VMEM),
        cost_estimate=pl.CostEstimate(
            flops=16 * rows * keys * D,
            bytes_accessed=4 * keys * D + 8 * rows * D,
            transcendentals=rows * keys * 12,
        ),
    )(*extra, queries, keys_values, keys_values)


def attend_back_kernel(masked, key_step, *refs):
    if masked:
        query_pos, key_pos, q_ref, k_ref, v_ref, out_ref, lse_ref, grad_ref, dq_ref, dk_ref, dv_ref = refs
    else:
        q_ref, k_ref, v_ref, out_ref, lse_ref, grad_ref, dq_ref, dk_ref, dv_ref = refs
    queries = q_ref[...]
    grads = grad_ref[...]
    lane = lax.broadcasted_iota(jnp.int32, queries.shape, 1) // HEAD_DIM
    zero = jnp.zeros((), queries.dtype)
    totals = lse_ref[...].T
    weighted = (grads.astype(jnp.float32) * out_ref[...].astype(jnp.float32)).T
    halves, grad_halves, total_rows, delta_rows, grad_queries = [], [], [], [], []
    for side in range(2):
        halves.append((jnp.where(lane == side, queries, zero) * attn_scale).astype(jnp.bfloat16))
        grad_halves.append(jnp.where(lane == side, grads, zero))
        total_rows.append(totals[side * HEAD_DIM : side * HEAD_DIM + 1, :])
        delta_rows.append(
            jnp.sum(weighted[side * HEAD_DIM : (side + 1) * HEAD_DIM, :], axis=0, keepdims=True)
        )
        grad_queries.append(jnp.zeros(queries.shape, jnp.float32))
    for start in range(0, k_ref.shape[0], key_step):
        rows = pl.ds(start, key_step)
        keys = k_ref[rows, :]
        values = v_ref[rows, :]
        grad_keys = jnp.zeros(keys.shape, jnp.float32)
        grad_values = jnp.zeros(keys.shape, jnp.float32)
        for side in range(2):
            scores = dot_nt(keys, halves[side])
            probs = jnp.exp(scores - total_rows[side])
            if masked:
                probs = jnp.where(key_pos[rows, :] <= query_pos[...], probs, 0.0)
            grad_probs = dot_nt(values, grad_halves[side])
            grad_scores = (probs * (grad_probs - delta_rows[side])).astype(jnp.bfloat16)
            grad_values += dot_nn(probs.astype(jnp.bfloat16), grad_halves[side])
            grad_keys += dot_nn(grad_scores, halves[side])
            grad_queries[side] += dot_tn(grad_scores, keys)
        dk_ref[rows, :] = grad_keys.astype(dk_ref.dtype)
        dv_ref[rows, :] = grad_values.astype(dv_ref.dtype)
    dq_ref[...] = (jnp.where(lane == 0, grad_queries[0], grad_queries[1]) * attn_scale).astype(
        dq_ref.dtype
    )


def attend_back(queries, keys_values, positions, mixed_rows, log_total, grad_mixed):
    rows, keys = queries.shape[0], keys_values.shape[0]
    pairs = D // 128
    key_step = min(keys, 512)
    extra, extra_specs = (), []
    if positions is not None:
        query_pos, key_pos = positions
        extra = (query_pos.reshape(1, rows), key_pos.reshape(keys, 1))
        extra_specs = [
            pl.BlockSpec((1, rows), lambda j: (0, 0)),
            pl.BlockSpec((keys, 1), lambda j: (0, 0)),
        ]
    row_spec = pl.BlockSpec((rows, 128), lambda j: (0, j))
    key_spec = pl.BlockSpec((keys, 128), lambda j: (0, j))
    value_spec = pl.BlockSpec((keys, 128), lambda j: (0, j + pairs))
    return pl.pallas_call(
        lambda *refs: attend_back_kernel(positions is not None, key_step, *refs),
        grid=(pairs,),
        in_specs=extra_specs + [row_spec, key_spec, value_spec, row_spec, row_spec, row_spec],
        out_specs=[row_spec, key_spec, key_spec],
        out_shape=[
            jax.ShapeDtypeStruct((rows, D), jnp.bfloat16),
            jax.ShapeDtypeStruct((keys, D), jnp.bfloat16),
            jax.ShapeDtypeStruct((keys, D), jnp.bfloat16),
        ],
        compiler_params=pltpu.CompilerParams(vmem_limit_bytes=KERNEL_VMEM),
        cost_estimate=pl.CostEstimate(
            flops=40 * rows * keys * D,
            bytes_accessed=8 * keys * D + 12 * rows * D,
            transcendentals=rows * keys * 12,
        ),
    )(*extra, queries, keys_values, keys_values, mixed_rows, log_total, grad_mixed)


def head_kernel(vocab, tile, used_ref, rows_ref, table_ref, mixed_ref, exp_ref, stats_ref, logits_ref):
    step = pl.program_id(0)
    padded = table_ref.shape[1]
    shape = (rows_ref.shape[0], 128)
    lane = lax.broadcasted_iota(jnp.int32, shape, 1)

    @pl.when(used_ref[step] == 0)
    def _():
        mixed_ref[...] = jnp.zeros(mixed_ref.shape, mixed_ref.dtype)
        exp_ref[...] = jnp.zeros(exp_ref.shape, exp_ref.dtype)
        stats_ref[...] = jnp.where(lane == 1, 1.0, 0.0)

    @pl.when(used_ref[step] != 0)
    def _():
        rows = rows_ref[...]
        top = jnp.full((rows.shape[0], 1), -jnp.inf, jnp.float32)
        for start in range(0, padded, tile):
            logits = dot_nn(rows, table_ref[:, start : start + tile])
            if start + tile > vocab:
                column = start + lax.broadcasted_iota(jnp.int32, logits.shape, 1)
                logits = jnp.where(column < vocab, logits, -jnp.inf)
            logits_ref[:, start : start + tile] = logits
            top = jnp.maximum(top, jnp.max(logits, axis=1, keepdims=True))
        summed = jnp.zeros((rows.shape[0], 1), jnp.float32)
        mixed = jnp.zeros(mixed_ref.shape, jnp.float32)
        for start in range(0, padded, tile):
            exponent = jnp.exp(logits_ref[:, start : start + tile] - top)
            summed += jnp.sum(exponent, axis=1, keepdims=True)
            low = exponent.astype(jnp.bfloat16)
            exp_ref[:, start : start + tile] = low
            mixed += dot_nt(low, table_ref[:, start : start + tile])
        mixed_ref[...] = mixed
        stats_ref[...] = jnp.where(lane == 0, top, summed)


def head_forward(rows_all, table, used, vocab, block_rows, tile):
    rows, padded = rows_all.shape[0], table.shape[1]
    return pl.pallas_call(
        lambda *refs: head_kernel(vocab, tile, *refs),
        grid_spec=pltpu.PrefetchScalarGridSpec(
            num_scalar_prefetch=1,
            grid=(rows // block_rows,),
            in_specs=[
                pl.BlockSpec((block_rows, D), lambda i, used: (i, 0)),
                pl.BlockSpec((D, padded), lambda i, used: (0, 0), pipeline_mode=pl.Buffered(1)),
            ],
            out_specs=[
                pl.BlockSpec((block_rows, D), lambda i, used: (i, 0)),
                pl.BlockSpec((block_rows, padded), lambda i, used: (i, 0)),
                pl.BlockSpec((block_rows, 128), lambda i, used: (i, 0)),
            ],
            scratch_shapes=[pltpu.VMEM((block_rows, padded), jnp.float32)],
        ),
        out_shape=[
            jax.ShapeDtypeStruct((rows, D), jnp.float32),
            jax.ShapeDtypeStruct((rows, padded), jnp.bfloat16),
            jax.ShapeDtypeStruct((rows, 128), jnp.float32),
        ],
        compiler_params=pltpu.CompilerParams(vmem_limit_bytes=KERNEL_VMEM),
        cost_estimate=pl.CostEstimate(
            flops=4 * rows * padded * D,
            bytes_accessed=2 * rows * padded + 2 * padded * D,
            transcendentals=rows * padded,
        ),
    )(used, rows_all, table)


def table_grad_kernel(tile, used_ref, rows_ref, exp_ref, info_ref, grad_ref, total_ref):
    step = pl.program_id(0)

    @pl.when(step == 0)
    def _():
        total_ref[...] = jnp.zeros(total_ref.shape, total_ref.dtype)

    @pl.when(used_ref[step] != 0)
    def _():
        rows = rows_ref[...]
        scale = info_ref[:, 0:1]
        weight = info_ref[:, 1:2]
        target = info_ref[:, 2:3].astype(jnp.int32)
        for start in range(0, exp_ref.shape[1], tile):
            column = start + lax.broadcasted_iota(jnp.int32, (exp_ref.shape[0], tile), 1)
            probs = exp_ref[:, start : start + tile].astype(jnp.float32) * scale
            hits = jnp.where(column == target, weight, 0.0)
            grad_logits = (probs - hits).astype(jnp.bfloat16)
            total_ref[:, start : start + tile] += dot_tn(rows, grad_logits)

    @pl.when(step == pl.num_programs(0) - 1)
    def _():
        grad_ref[...] = total_ref[...].astype(grad_ref.dtype)


def table_grad(rows_all, exps, info, used, block_rows, tile):
    rows, padded = exps.shape
    return pl.pallas_call(
        lambda *refs: table_grad_kernel(tile, *refs),
        grid_spec=pltpu.PrefetchScalarGridSpec(
            num_scalar_prefetch=1,
            grid=(rows // block_rows,),
            in_specs=[
                pl.BlockSpec((block_rows, D), lambda i, used: (i, 0)),
                pl.BlockSpec((block_rows, padded), lambda i, used: (i, 0)),
                pl.BlockSpec((block_rows, 128), lambda i, used: (i, 0)),
            ],
            out_specs=pl.BlockSpec((D, padded), lambda i, used: (0, 0), pipeline_mode=pl.Buffered(1)),
            scratch_shapes=[pltpu.VMEM((D, padded), jnp.float32)],
        ),
        out_shape=jax.ShapeDtypeStruct((D, padded), jnp.bfloat16),
        compiler_params=pltpu.CompilerParams(vmem_limit_bytes=KERNEL_VMEM),
        cost_estimate=pl.CostEstimate(
            flops=2 * rows * padded * D,
            bytes_accessed=2 * rows * padded + 2 * padded * D,
            transcendentals=0,
        ),
    )(used, rows_all, exps, info)


FF = 2048
POS = 256
TGT = 1024
BW = 128
BLOCKS = 174
EXTENTS = [D, 3 * D, D, 2 * FF, FF, 3 * D, D, D, 2 * D, D, 2 * FF, FF]
GATHERS = [[0, 1], [2, 3, 4], [5, 6, 7, 8], [9, 10, 11]]
SMALL_ROWS = 2 * POS + 8

norm_eps = 1e-06
clip_limit = 0.02
stat_decay = 0.5
rate_shampoo = 0.02
rate_adam = 0.5
beta_first = 0.9
beta_second = 0.95
adam_eps = 1e-08
weight_decay = 0.01
BOTH = ("wide", "narrow")


def rms_norm(values, gain_vec):
    return (
        values * lax.rsqrt(jnp.mean(values * values, axis=-1, keepdims=True) + norm_eps) * gain_vec
    )


def norm_back(values, gain_vec, grad_out):
    _, pullback = jax.vjp(rms_norm, values, gain_vec)
    return pullback(grad_out)


def low(values):
    return values.astype(jnp.bfloat16)


def gated_unit(gate_up):
    return jax.nn.gelu(gate_up[:, :FF], approximate=True) * gate_up[:, FF:]


def swap(values, bit):
    count = lax.axis_size("wide")
    return lax.ppermute(values, "wide", [(w, w ^ bit) for w in range(count)])


def shift(values, step):
    count = lax.axis_size("narrow")
    return lax.ppermute(values, "narrow", [(i, (i + step) % count) for i in range(count)])


def wide_bits():
    return lax.axis_size("wide").bit_length() - 1


def bit_value(level):
    return (lax.axis_index("wide") >> level) & 1


def gather_wide(values, order):
    bits = wide_bits()
    whole = values.reshape((1,) * bits + values.shape)
    for level in order:
        axis = bits - 1 - level
        other = swap(whole, 1 << level)
        mine_last = bit_value(level) == 1
        whole = jnp.where(
            mine_last,
            jnp.concatenate([other, whole], axis=axis),
            jnp.concatenate([whole, other], axis=axis),
        )
    return whole.reshape((1 << bits,) + values.shape)


def scatter_wide(values, order):
    bits = wide_bits()
    rest = values.shape[1:]
    whole = values.reshape((2,) * bits + rest)
    for level in order:
        axis = bits - 1 - level
        bit = bit_value(level)
        mine = lax.dynamic_index_in_dim(whole, bit, axis, keepdims=True)
        theirs = lax.dynamic_index_in_dim(whole, 1 - bit, axis, keepdims=True)
        got = swap(low(theirs), 1 << level)
        whole = low(mine.astype(jnp.float32) + got.astype(jnp.float32))
    return whole.reshape(rest)


def split_orders():
    upper = list(range(1, wide_bits()))
    return upper, upper[::-1]


def gather_wide_fast(values):
    first, second = split_orders()
    half = values.shape[-1] // 2
    return jnp.concatenate(
        [gather_wide(values[..., :half], first + [0]), gather_wide(values[..., half:], second + [0])],
        axis=-1,
    )


def scatter_wide_fast(values):
    first, second = split_orders()
    half = values.shape[-1] // 2
    return jnp.concatenate(
        [scatter_wide(values[..., :half], [0] + first), scatter_wide(values[..., half:], [0] + second)],
        axis=-1,
    )


def group_offsets():
    offsets, bit = [0], lax.axis_size("narrow") // 2
    while bit:
        offsets = offsets + [o ^ bit for o in offsets]
        bit //= 2
    return offsets


def gather_group(rows):
    bit = lax.axis_size("narrow") // 2
    while bit:
        rows = jnp.concatenate([rows, swap(rows, bit)], axis=0)
        bit //= 2
    return rows


def return_group(grads):
    bit = 1
    while bit < lax.axis_size("narrow"):
        half = grads.shape[0] // 2
        got = swap(low(grads[half:]), bit)
        grads = grads[:half].astype(jnp.float32) + got.astype(jnp.float32)
        bit *= 2
    return low(grads)


def feed_forward(stream, gain_vec, w_in, w_back):
    normed = low(rms_norm(stream, gain_vec))
    gate_up = dot_nn(normed, w_in)
    hidden = low(gated_unit(gate_up))
    return (dot_nt(hidden, w_back), (normed, gate_up, hidden))


def feed_back(stream, gain_vec, w_in, w_back, kept_state, grad_out):
    normed, gate_up, hidden = kept_state
    grad_low = low(grad_out)
    grad_w_back = low(dot_tn(grad_low, hidden))
    _, pullback = jax.vjp(gated_unit, gate_up)
    grad_gate_up = low(pullback(dot_nn(grad_low, w_back))[0])
    grad_w_in = low(dot_tn(normed, grad_gate_up))
    grad_stream, grad_gain = norm_back(stream, gain_vec, dot_nt(grad_gate_up, w_in))
    return (grad_stream, grad_gain, grad_w_in, grad_w_back)


def attention_back(queries, keys_values, positions, mixed_rows, log_total, w_out, grad_out):
    grad_low = low(grad_out)
    grad_w_out = low(dot_tn(mixed_rows, grad_low))
    grad_mixed = low(dot_nt(grad_low, w_out))
    grad_query, grad_key, grad_value = attend_back(
        queries, keys_values, positions, mixed_rows, log_total, grad_mixed
    )
    grad_pair = return_group(jnp.concatenate([grad_key, grad_value], axis=1))
    return (grad_w_out, grad_query, grad_pair)


def own_shards(columns):
    return lax.psum_scatter(columns, BOTH, scatter_dimension=0, tiled=True)


def adamw(param, moment, second, grad, step_count):
    moment = beta_first * moment + (1 - beta_first) * grad
    second = beta_second * second + (1 - beta_second) * grad * grad
    steps = step_count.astype(jnp.float32)
    m_hat = moment / (1 - jnp.power(beta_first, steps))
    v_hat = second / (1 - jnp.power(beta_second, steps))
    return (
        param - rate_adam * (m_hat / (jnp.sqrt(v_hat) + adam_eps) + weight_decay * param),
        moment,
        second,
    )


def shards(
    patches,
    patch_rows,
    patch_cols,
    input_ids,
    target_ids,
    target_lengths,
    loss_mask,
    master_slabs,
    left_stats,
    left_roots,
    right_stats,
    right_roots,
    block_slot,
    vocab_table,
    vocab_first,
    vocab_second,
    small_params,
    small_first,
    small_second,
    step_count,
):
    wide_count = lax.axis_size("wide")
    narrow_count = lax.axis_size("narrow")
    devices = wide_count * narrow_count
    screen_sets = wide_count // narrow_count
    wide_pos = lax.axis_index("wide")
    narrow_pos = lax.axis_index("narrow")
    member = wide_pos % narrow_count
    slot_total = block_slot.shape[0]
    own_count = master_slabs.shape[0]
    piece = D // devices
    slot_ids = block_slot[:BLOCKS]
    enc_rows, dec_rows = patches.shape[0], input_ids.shape[0]
    vocab_rows, features = vocab_table.shape

    block_of_slot = (slot_ids[:, None] == jnp.arange(slot_total)[None, :]).astype(jnp.bfloat16)
    pieces = low(master_slabs).reshape(own_count, devices, piece, BW).transpose(1, 0, 2, 3)
    pieces = lax.all_to_all(pieces, BOTH, 0, 0).reshape(slot_total, piece * BW)
    ordered = low(dot_nn(block_of_slot, pieces)).reshape(BLOCKS, piece, BW)
    row_shard = ordered.transpose(1, 0, 2).reshape(piece, BLOCKS * BW)
    weights = [None] * len(EXTENTS)
    for numbers in GATHERS:
        begin = sum(EXTENTS[: numbers[0]])
        size = sum(EXTENTS[n] for n in numbers)
        group = lax.all_gather(row_shard[:, begin : begin + size], BOTH, axis=0, tiled=True)
        for n in numbers:
            offset = sum(EXTENTS[:n]) - begin
            weights[n] = group[:, offset : offset + EXTENTS[n]]

    exchange = []
    for w in range(wide_count):
        for n in range(narrow_count):
            base = w // narrow_count * narrow_count
            exchange.append((w * narrow_count + n, (base + n) * narrow_count + w % narrow_count))
    patches = lax.ppermute(patches, BOTH, exchange)
    whole_ids = lax.ppermute(
        jnp.concatenate([patch_rows, patch_cols, input_ids, target_ids]), BOTH, exchange
    )
    rows_ids, cols_ids = whole_ids[:enc_rows], whole_ids[enc_rows : 2 * enc_rows]
    token_ids = whole_ids[2 * enc_rows :].reshape(2, dec_rows)
    layer_tokens = lax.all_gather(token_ids, "wide", axis=0)
    layer_targets = layer_tokens[:, 1].reshape(-1)
    every_input = lax.all_gather(layer_tokens, "narrow", axis=1)
    screens_info = lax.all_gather(
        jnp.concatenate([target_lengths[:, None], loss_mask], axis=1), "wide", axis=0, tiled=True
    )
    counted = (
        (jnp.arange(TGT)[None, :] < screens_info[:, :1]) & (screens_info[:, 1:] == 1)
    ).astype(jnp.float32)
    tokens_counted = jnp.maximum(jnp.sum(counted), 1.0)
    row_counted = lax.dynamic_index_in_dim(
        counted.reshape(screen_sets, narrow_count, TGT), narrow_pos, 1, keepdims=False
    ).reshape(-1)
    own_counted = lax.dynamic_slice_in_dim(row_counted, wide_pos * dec_rows, dec_rows)

    padded = -(-vocab_rows // 256) * 256
    table_low = low(vocab_table)
    columns = jnp.arange(vocab_rows)
    vocab_start = wide_pos * vocab_rows
    flat_inputs = every_input[:, :, 0].reshape(-1) - vocab_start
    flat_targets = every_input[:, :, 1].reshape(-1) - vocab_start

    def looked_up(ids):
        onehot = (ids[:, None] == columns[None, :]).astype(jnp.bfloat16)
        found = low(dot_nn(onehot, table_low)).reshape(wide_count, narrow_count * dec_rows, features)
        found = scatter_wide(found, list(range(wide_bits())))
        found = lax.all_to_all(found.reshape(narrow_count, dec_rows, features), "narrow", 0, 0)
        return found.transpose(1, 0, 2).reshape(dec_rows, D)

    stream_dec = looked_up(flat_inputs).astype(jnp.float32)
    target_rows = looked_up(flat_targets).astype(jnp.float32)
    table_parts = [jnp.pad(table_low.T, ((0, 0), (0, padded - vocab_rows)))]
    for _ in range(narrow_count - 1):
        table_parts.append(shift(table_parts[-1], -1))
    table = jnp.concatenate(table_parts, axis=0)

    gain_rows = small_params[2 * POS :]
    picked = jnp.concatenate(
        [
            rows_ids[:, None] == jnp.arange(POS)[None, :],
            cols_ids[:, None] == jnp.arange(POS)[None, :],
        ],
        axis=1,
    ).astype(jnp.bfloat16)
    tables = small_params[: 2 * POS]
    tables_high = low(tables)
    tables_rest = low(tables - tables_high.astype(jnp.float32))
    enc_zero = (
        dot_nn(patches, weights[0])
        + gain_rows[7]
        + dot_nn(picked, tables_high)
        + dot_nn(picked, tables_rest)
    )
    enc_normed = low(rms_norm(enc_zero, gain_rows[0]))
    enc_mix = low(dot_nn(enc_normed, weights[1]))
    enc_keys = gather_group(enc_mix[:, D:])
    enc_mixed, enc_total = attend(enc_mix[:, :D], enc_keys, None)
    enc_one = enc_zero + dot_nn(enc_mixed, weights[2])
    branch, enc_ffn = feed_forward(enc_one, gain_rows[1], weights[3], weights[4])
    enc_two = enc_one + branch
    encoded = low(rms_norm(enc_two, gain_rows[2]))

    query_pos = (member * dec_rows + jnp.arange(dec_rows)).astype(jnp.int32)
    key_pos = jnp.concatenate(
        [(member ^ offset) * dec_rows + jnp.arange(dec_rows) for offset in group_offsets()]
    ).astype(jnp.int32)
    causal = (query_pos, key_pos)
    dec_zero = stream_dec
    dec_normed = low(rms_norm(dec_zero, gain_rows[3]))
    dec_mix = low(dot_nn(dec_normed, weights[5]))
    self_keys = gather_group(dec_mix[:, D:])
    self_mixed, self_total = attend(dec_mix[:, :D], self_keys, causal)
    dec_one = dec_zero + dot_nn(self_mixed, weights[6])
    cross_normed = low(rms_norm(dec_one, gain_rows[4]))
    cross_query = low(dot_nn(cross_normed, weights[7]))
    cross_keys = gather_group(low(dot_nn(encoded, weights[8])))
    cross_mixed, cross_total = attend(cross_query, cross_keys, None)
    dec_two = dec_one + dot_nn(cross_mixed, weights[9])
    branch, dec_ffn = feed_forward(dec_two, gain_rows[5], weights[10], weights[11])
    dec_three = dec_two + branch
    final = low(rms_norm(dec_three, gain_rows[6]) * D ** (-0.5))

    rotated = lax.dynamic_slice_in_dim(
        jnp.concatenate([final, final], axis=1), narrow_pos * features, D, axis=1
    )
    rows_all = gather_wide_fast(rotated).reshape(-1, D)
    total_rows = rows_all.shape[0]
    block_rows = 256
    used = jnp.any(row_counted.reshape(-1, block_rows) != 0, axis=1).astype(jnp.int32)
    tile = padded // 5 if padded % 640 == 0 else 256
    mixed, exps, stats = head_forward(rows_all, table, used, vocab_rows, block_rows, tile)
    top_part, summed_part = stats[:, 0], stats[:, 1]
    stats_all = lax.all_gather(jnp.stack([top_part, summed_part]), "wide", axis=0)
    top_logit = jnp.max(stats_all[:, 0], axis=0)
    summed = jnp.sum(stats_all[:, 1] * jnp.exp(stats_all[:, 0] - top_logit), axis=0)
    log_total = top_logit + jnp.log(summed)
    row_weight = row_counted / tokens_counted
    scale = row_weight * jnp.exp(top_part - log_total)
    grad_rows = (mixed * scale[:, None]).reshape(wide_count, dec_rows, D)
    grad_back = scatter_wide_fast(grad_rows).astype(jnp.float32)
    grad_back = lax.dynamic_slice_in_dim(
        jnp.concatenate([grad_back, grad_back], axis=1), (D - narrow_pos * features) % D, D, axis=1
    )
    own_weight = own_counted / tokens_counted
    grad_final = grad_back - own_weight[:, None] * target_rows
    target_logit = jnp.sum(final.astype(jnp.float32) * target_rows, axis=1)
    own_total = lax.dynamic_slice_in_dim(log_total, wide_pos * dec_rows, dec_rows)
    loss_local = jnp.sum(own_counted * (own_total - target_logit))
    target_cols = (layer_targets - vocab_start).astype(jnp.float32)
    info = jnp.concatenate(
        [
            jnp.stack([scale, row_weight, target_cols], axis=1),
            jnp.zeros((total_rows, 125), jnp.float32),
        ],
        axis=1,
    )
    grad_table = table_grad(rows_all, exps, info, used, block_rows, tile)
    grad_parts = grad_table.reshape(narrow_count, features, padded)
    moving = grad_parts[narrow_count - 1]
    for k in range(narrow_count - 2, -1, -1):
        moving = grad_parts[k].astype(jnp.float32) + shift(low(moving), 1).astype(jnp.float32)
    head_grad = moving[:, :vocab_rows].T

    grad_three, gain_final = norm_back(dec_three, gain_rows[6], grad_final * D ** (-0.5))
    grad_two, gain_dffn, grad_in, grad_out = feed_back(
        dec_two, gain_rows[5], weights[10], weights[11], dec_ffn, grad_three
    )
    shard_dffn = own_shards(jnp.concatenate([grad_in, grad_out], axis=1))
    grad_two = grad_two + grad_three
    grad_cout, grad_query, grad_pair = attention_back(
        cross_query, cross_keys, None, cross_mixed, cross_total, weights[9], grad_two
    )
    grad_cq = low(dot_tn(cross_normed, grad_query))
    grad_one, gain_cross = norm_back(dec_one, gain_rows[4], dot_nt(grad_query, weights[7]))
    grad_one = grad_one + grad_two
    grad_ckv = low(dot_tn(encoded, grad_pair))
    grad_encoded = dot_nt(grad_pair, weights[8])
    grad_so, grad_query, grad_pair = attention_back(
        dec_mix[:, :D], self_keys, causal, self_mixed, self_total, weights[6], grad_one
    )
    grad_mix = jnp.concatenate([grad_query, grad_pair], axis=1)
    grad_sqkv = low(dot_tn(dec_normed, grad_mix))
    shard_dattn = own_shards(
        jnp.concatenate([grad_sqkv, grad_so, grad_cq, grad_ckv, grad_cout], axis=1)
    )
    grad_zero, gain_self = norm_back(dec_zero, gain_rows[3], dot_nt(grad_mix, weights[5]))
    grad_tokens = low(grad_zero + grad_one)

    sent = grad_tokens.reshape(dec_rows, narrow_count, features).transpose(1, 0, 2)
    sent = lax.all_to_all(sent, "narrow", 0, 0).reshape(narrow_count * dec_rows, features)
    sent = gather_wide(sent, list(range(wide_bits()))[::-1]).reshape(-1, features)
    onehot = (flat_inputs[:, None] == columns[None, :]).astype(jnp.bfloat16)
    vocab_grad = head_grad + dot_tn(onehot, sent)

    grad_two, gain_efinal = norm_back(enc_two, gain_rows[2], grad_encoded)
    grad_one, gain_effn, grad_in, grad_out = feed_back(
        enc_one, gain_rows[1], weights[3], weights[4], enc_ffn, grad_two
    )
    shard_effn = own_shards(jnp.concatenate([grad_in, grad_out], axis=1))
    grad_one = grad_one + grad_two
    grad_eo, grad_query, grad_pair = attention_back(
        enc_mix[:, :D], enc_keys, None, enc_mixed, enc_total, weights[2], grad_one
    )
    grad_mix = jnp.concatenate([grad_query, grad_pair], axis=1)
    grad_eqkv = low(dot_tn(enc_normed, grad_mix))
    grad_zero, gain_eattn = norm_back(enc_zero, gain_rows[0], dot_nt(grad_mix, weights[1]))
    grad_zero = grad_zero + grad_one
    grad_patch = low(dot_tn(patches, low(grad_zero)))
    grad_tables = dot_tn(low(grad_zero), picked)
    gains = [gain_eattn, gain_effn, gain_efinal, gain_self, gain_cross, gain_dffn, gain_final]
    grad_small = low(
        jnp.concatenate(
            [grad_tables, jnp.stack(gains + [jnp.sum(grad_zero, axis=0)], axis=1)], axis=1
        )
    )
    filler = jnp.zeros((D, -SMALL_ROWS % BW), jnp.bfloat16)
    shard_eattn = own_shards(
        jnp.concatenate([grad_patch, grad_eqkv, grad_eo, grad_small, filler], axis=1)
    )

    projection = shard_eattn[:, : 5 * D]
    small_shard = shard_eattn[:, 5 * D : 5 * D + SMALL_ROWS].astype(jnp.float32)
    grads = jnp.concatenate([projection, shard_effn, shard_dattn, shard_dffn], axis=1)
    partial_square = (
        jnp.sum(jnp.square(grads.astype(jnp.float32)))
        + jnp.sum(vocab_grad * vocab_grad)
        + jnp.sum(small_shard * small_shard)
    )
    scalars = jnp.where(
        jnp.arange(SMALL_ROWS)[None, :] == 0,
        partial_square,
        jnp.where(jnp.arange(SMALL_ROWS)[None, :] == 1, loss_local, 0.0),
    )
    shared = lax.all_gather(
        jnp.concatenate([small_shard, scalars], axis=0), BOTH, axis=0
    )
    small_grad = shared[:, :piece].reshape(D, SMALL_ROWS).T
    total_square = jnp.sum(shared[:, piece, 0])
    loss_sum = jnp.sum(shared[:, piece, 1])
    slotted = grads.reshape(piece, BLOCKS, BW).transpose(1, 0, 2).reshape(BLOCKS, piece * BW)
    slotted = low(dot_tn(block_of_slot, slotted)).reshape(devices, own_count, piece, BW)
    slab = lax.all_to_all(slotted, BOTH, 0, 0).transpose(1, 0, 2, 3).reshape(own_count, D, BW)

    grad_norm = jnp.sqrt(total_square)
    factor = jnp.minimum(1.0, clip_limit / (grad_norm + 1e-06))
    kept = (1 - stat_decay) * factor * factor
    slab_grad = slab.astype(jnp.float32) * factor
    left_new = stat_decay * left_stats + kept * jnp.einsum(
        "sik,sjk->sij", slab, slab, preferred_element_type=jnp.float32
    )
    right_new = stat_decay * right_stats + kept * jnp.einsum(
        "ski,skj->sij", slab, slab, preferred_element_type=jnp.float32
    )
    rooted = jnp.einsum("sij,sjk->sik", low(left_roots), slab, preferred_element_type=jnp.float32)
    precond = factor * jnp.einsum(
        "sij,sjk->sik", rooted, right_roots, precision=lax.Precision.HIGHEST
    )
    scale_back = lax.rsqrt(jnp.mean(precond * precond, axis=(1, 2), keepdims=True) + norm_eps)
    master_new = master_slabs - rate_shampoo * precond * scale_back
    vocab_new, vocab_first_new, vocab_second_new = adamw(
        vocab_table, vocab_first, vocab_second, vocab_grad * factor, step_count
    )
    small_new, small_first_new, small_second_new = adamw(
        small_params, small_first, small_second, small_grad * factor, step_count
    )
    return (
        loss_sum,
        tokens_counted,
        master_new,
        master_new.astype(jnp.bfloat16),
        slab_grad,
        left_new,
        right_new,
        vocab_new,
        vocab_new.astype(jnp.bfloat16),
        vocab_first_new,
        vocab_second_new,
        small_new,
        small_first_new,
        small_second_new,
        grad_norm,
    )


def solution(mesh):
    in_specs = (
        P(("wide", "narrow"), None),
        P(("wide", "narrow")),
        P(("wide", "narrow")),
        P(("wide", "narrow")),
        P(("wide", "narrow")),
        P("wide"),
        P("wide", None),
        P(("wide", "narrow"), None, None),
        P(("wide", "narrow"), None, None),
        P(("wide", "narrow"), None, None),
        P(("wide", "narrow"), None, None),
        P(("wide", "narrow"), None, None),
        P(),
        P("wide", "narrow"),
        P("wide", "narrow"),
        P("wide", "narrow"),
        P(),
        P(),
        P(),
        P(),
    )
    out_specs = (
        P(),
        P(),
        P(("wide", "narrow"), None, None),
        P(("wide", "narrow"), None, None),
        P(("wide", "narrow"), None, None),
        P(("wide", "narrow"), None, None),
        P(("wide", "narrow"), None, None),
        P("wide", "narrow"),
        P("wide", "narrow"),
        P("wide", "narrow"),
        P("wide", "narrow"),
        P(),
        P(),
        P(),
        P(),
    )
    return jax.shard_map(shards, mesh=mesh, in_specs=in_specs, out_specs=out_specs, check_vma=False)
```

time: 3380 us -> 1820 us (0.54)
  waiting for transfers between devices: 1470 us -> 783 us
  matrix products: 922 us -> 290 us
  local copies, waits for them, and re-layouts: 630 us -> 139 us
  Pallas kernels: 0 us -> 209 us
  starting transfers between devices: 2.42 us -> 94.2 us
  other arithmetic: 206 us -> 124 us
  blocking collectives: 103 us -> 152 us
    dot_general x337 -> x47, matrix products: 922 us -> 290 us  [the longest x17 135 us: dot_nn(): lax.dot_general(left, right, (((1,), (0,)), ((), ())), preferred_element_...]
    all_gather x10 -> x5, waiting for transfers between devices: 504 us -> 27.7 us  [the longest x4 14.7 us: shards(): lax.all_gather(row_shard[:, begin:begin + size], BOTH, axis=0, tiled=True)]
    reduce_scatter x10 -> x3, waiting for transfers between devices: 827 us -> 369 us  [own_shards(): return lax.psum_scatter(columns, BOTH, scatter_dimension=0, tiled=True)]
    ppermute x0 -> x41, waiting for transfers between devices: none -> 350 us  [the longest x33 238 us: swap(): return lax.ppermute(values, 'wide', [(w, w ^ bit) for w in range(count)])]
    pallas_call x0 -> x8, Pallas kernels: none -> 209 us  [the longest x3 75.6 us: attend_back(): pl.pallas_call(lambda *refs: attend_back_kernel(positions is not None, ke...]
    gather x8 -> x0, local copies, waits for them, and re-layouts: 179 us -> none  [the longest x2 125 us: shards(): jnp.take(grads_full.reshape(D, BLOCKS, BW), slot_block, axis=1)]
    psum x1 -> x0, waiting for transfers between devices: 132 us -> none  [shards(): lax.psum((small_partial, partial_square, loss_local), ('wide', 'narrow'))]
    all_to_all x0 -> x2, blocking collectives: none -> 105 us  [the longest x1 67.6 us: shards(): lax.all_to_all(sent, 'narrow', 0, 0)]
  transfers between devices with their start and end apart: 21 -> 53, of which waited for: 12 -> 29; matrix products, arithmetic and copies ran while one was open for 32% -> 22% of each run, Pallas kernels for 0% -> 5%
where the time goes in v1:
time: 1820 us
  waiting for transfers between devices  783 us (43%)
  matrix products  290 us (16%)
  Pallas kernels  209 us (11%)
  blocking collectives  152 us (8%)
  local copies, waits for them, and re-layouts  139 us (8%)
  other arithmetic  124 us (7%)
  starting transfers between devices  94.2 us (5%)
  between operations  23.8 us (1%)
    reduce_scatter x3, waiting for transfers between devices, own_shards(): return lax.psum_scatter(columns, BOTH, scatter_dimension=0, tiled=True)  369 us
    ppermute x33, waiting for transfers between devices, swap(): return lax.ppermute(values, 'wide', [(w, w ^ bit) for w in range(count)])  238 us
    dot_general x17, matrix products, dot_nn(): lax.dot_general(left, right, (((1,), (0,)), ((), ())), preferred_element_...  135 us
    ppermute x6, waiting for transfers between devices, shift(): lax.ppermute(values, 'narrow', [(i, (i + step) % count) for i in range(co...  112 us
    dot_general x15, matrix products, dot_tn(): lax.dot_general(left, right, (((0,), (0,)), ((), ())), preferred_element_...  85.6 us
    pallas_call x3, Pallas kernels, attend_back(): pl.pallas_call(lambda *refs: attend_back_kernel(positions is not None, ke...  75.6 us
    all_to_all x1, blocking collectives, shards(): lax.all_to_all(sent, 'narrow', 0, 0)  67.6 us
    pallas_call x1, Pallas kernels, head_forward(): pl.pallas_call(lambda *refs: head_kernel(vocab, tile, *refs), grid_spec=p...  59.4 us
  transfers between devices with their start and end apart: 53, of which 29 were waited for; matrix products, arithmetic and copies ran while one was open for 22% of the time, Pallas kernels for 5%

profile of v1, /device:TPU:0, one launch (start us, length us, event | category | flops | bytes accessed | tf_op | source)
XLA Modules:
  0.0 1815.6 jit_solution(1277971485796651834)
XLA Ops:
  9.3 37.2 %all_to_all.25 = bf16[32,6,24,128]{3,2,1,0:T(8,128)(2,1)S(1)} all-to-all(bf16[32,6,24,128]{3,2,1,0:T(8,128)(2,1)S(1)} %bitcast.206), channel_id=1, replica_groups=mesh['wide'=8,'narrow'=4] {'wide','narrow'}, dimensions={0} | all-to-all | bytes 2359296 | tf_op jit(solution)/shard_map/all_to_all | solution.py:515
  81.8 42.2 %fusion.7 = bf16[8192,192]{0,1:T(8,128)(2,1)} fusion(s32[8192]{0:T(1024)S(1)} %bitcast.233, f32[6288,192]{0,1:T(8,128)} %param.33), kind=kOutput, calls=%fused_computation.10 | convolution fusion | flops 19834630144 | bytes 8007680 | tf_op jit(solution)/shard_map/dot_general | solution.py:21
  158.8 21.4 %collective-permute-done.5 = bf16[2,1,1,1024,192]{3,4,2,1,0:T(8,128)(2,1)} collective-permute-done((bf16[2,1,1,1024,192]{3,4,2,1,0:T(8,128)(2,1)}, bf16[2,1,1,1024,192]{3,4,2,1,0:T(8,128)(2,1)}, u32[]{:S(2)}, u32[]{:S(2)}) %collective-permute-start.5) | collective-permute-done | bytes 786464 | tf_op jit(solution)/shard_map/ppermute | solution.py:337
  192.0 16.2 collective-permute-start.2
  221.5 18.3 %collective-permute-done.2 = bf16[512,1536]{1,0:T(8,128)(2,1)S(1)} collective-permute-done((bf16[512,1536]{1,0:T(8,128)(2,1)S(1)}, bf16[512,1536]{1,0:T(8,128)(2,1)S(1)}, u32[]{:S(2)}, u32[]{:S(2)}) %collective-permute-start.2) | collective-permute-done | bytes 1572896 | tf_op jit(solution)/shard_map/ppermute | solution.py:337
  242.0 42.2 %fusion.6 = bf16[8192,192]{0,1:T(8,128)(2,1)} fusion(s32[8192]{0:T(1024)S(1)} %bitcast.235, f32[6288,192]{0,1:T(8,128)} %param.33), kind=kOutput, calls=%fused_computation.9 | convolution fusion | flops 19834630144 | bytes 8007680 | tf_op jit(solution)/shard_map/dot_general | solution.py:21
  310.8 22.1 %shard_map.307 = (bf16[512,768]{1,0:T(8,128)(2,1)}, f32[512,768]{1,0:T(8,128)}) custom-call(bf16[512,768]{1,0:T(8,128)(2,1)} %slice.334.refs_0_, bf16[2048,1536]{1,0:T(8,128)(2,1)} %pad_maximum_fusion.3.refs_1_.refs_2_, bf16[2048,1536]{1,0:T(8,128)(2,1)} %pad_maximum_fusion.3.refs_1_.refs_2_), custom_call_target="tpu_custom_call" | custom-call | flops 12884901888 | bytes 9437184 | tf_op jit(solution)/shard_map/pallas_call | solution.py:75
  379.8 44.2 %collective-permute-done.7 = bf16[256,1536]{1,0:T(8,128)(2,1)S(1)} collective-permute-done((bf16[256,1536]{1,0:T(8,128)(2,1)S(1)}, bf16[256,1536]{1,0:T(8,128)(2,1)S(1)}, u32[]{:S(2)}, u32[]{:S(2)}) %collective-permute-start.7) | collective-permute-done | bytes 786464 | tf_op jit(solution)/shard_map/ppermute | solution.py:337
  566.4 59.4 %shard_map.310 = (f32[2048,768]{1,0:T(8,128)}, bf16[2048,6400]{1,0:T(8,128)(2,1)}, f32[2048,128]{1,0:T(8,128)}) custom-call(s32[8]{0:T(128)} %convert_element_type.420.refs_0_, bf16[2048,768]{1,0:T(8,128)(2,1)} %pad_maximum_fusion.8.refs_1_, bf16[768,6400]{1,0:T(8,128)(2,1)} %pad_maximum_fusion.refs_2_), custom_call_target="tpu_custom_call" | custom-call | flops 40265318400 | bytes 36044800 | tf_op jit(solution)/shard_map/pallas_call | solution.py:215
  687.3 23.1 %shard_map.311 = (bf16[256,768]{1,0:T(8,128)(2,1)}, bf16[2048,768]{1,0:T(8,128)(2,1)}, bf16[2048,768]{1,0:T(8,128)(2,1)}) custom-call(bf16[256,768]{1,0:T(8,128)(2,1)} %convolution_convert_fusion.21.refs_0_, bf16[2048,1536]{1,0:T(8,128)(2,1)} %pad_maximum_fusion.4.refs_1_.refs_2_, bf16[2048,1536]{1,0:T(8,128)(2,1)} %pad_maximum_fusion.4.refs_1_.refs_2_, ...), custom_call_target="tpu_custom_call" | custom-call | flops 16106127360 | bytes 14942208 | tf_op jit(solution)/shard_map/pallas_call | solution.py:159
  733.8 27.2 %collective-permute-done.30 = bf16[512,1536]{1,0:T(8,128)(2,1)} collective-permute-done((bf16[512,1536]{1,0:T(8,128)(2,1)}, bf16[512,1536]{1,0:T(8,128)(2,1)}, u32[]{:S(2)}, u32[]{:S(2)}) %collective-permute-start.30) | collective-permute-done | bytes 1572896 | tf_op jit(solution)/shard_map/ppermute | solution.py:337
  785.3 38.9 %shard_map.312 = (bf16[512,768]{1,0:T(8,128)(2,1)}, bf16[2048,768]{1,0:T(8,128)(2,1)}, bf16[2048,768]{1,0:T(8,128)(2,1)}) custom-call(bf16[512,768]{1,0:T(8,128)(2,1)} %slice.334.refs_0_, bf16[2048,1536]{1,0:T(8,128)(2,1)} %pad_maximum_fusion.3.refs_1_.refs_2_, bf16[2048,1536]{1,0:T(8,128)(2,1)} %pad_maximum_fusion.3.refs_1_.refs_2_, ...), custom_call_target="tpu_custom_call" | custom-call | flops 32212254720 | bytes 17301504 | tf_op jit(solution)/shard_map/pallas_call | solution.py:159
  880.8 23.6 %collective-permute-done.32 = bf16[512,1536]{1,0:T(8,128)(2,1)S(1)} collective-permute-done((bf16[512,1536]{1,0:T(8,128)(2,1)S(1)}, bf16[512,1536]{1,0:T(8,128)(2,1)S(1)}, u32[]{:S(2)}, u32[]{:S(2)}) %collective-permute-start.32) | collective-permute-done | bytes 1572896 | tf_op jit(solution)/shard_map/ppermute | solution.py:337
  961.8 29.4 %shard_map.314 = bf16[768,6400]{1,0:T(8,128)(2,1)} custom-call(s32[8]{0:T(128)} %convert_element_type.420.refs_0_, bf16[2048,768]{1,0:T(8,128)(2,1)} %pad_maximum_fusion.8.refs_1_, bf16[2048,6400]{1,0:T(8,128)(2,1)} %get-tuple-element.50.refs_2_, f32[2048,128]{1,0:T(8,128)} %maximum_maximum_fusion.refs_3_), custom_call_target="tpu_custom_call" | custom-call | flops 20132659200 | bytes 36044800 | tf_op jit(solution)/shard_map/pallas_call | solution.py:272
  996.5 25.8 %collective-permute-start.35 = (bf16[192,6400]{1,0:T(8,128)(2,1)}, bf16[192,6400]{1,0:T(8,128)(2,1)}, u32[]{:S(2)}, u32[]{:S(2)}) collective-permute-start(bf16[192,6400]{1,0:T(8,128)(2,1)} %get-tuple-element.117), channel_id=1, source_target_pairs={{0,1},{1,2},{2,3},{3,0},{4,5},{5,6},{6,7},{7,4},{8,9},{9,10},{10,1... | collective-permute-start | bytes 7372808 | tf_op jit(solution)/shard_map/ppermute | solution.py:342
  1035.3 56.2 %collective-permute-done.35 = bf16[192,6400]{1,0:T(8,128)(2,1)} collective-permute-done((bf16[192,6400]{1,0:T(8,128)(2,1)}, bf16[192,6400]{1,0:T(8,128)(2,1)}, u32[]{:S(2)}, u32[]{:S(2)}) %collective-permute-start.35) | collective-permute-done | bytes 2457632 | tf_op jit(solution)/shard_map/ppermute | solution.py:342
  1096.4 67.6 %all_to_all.26 = bf16[4,256,192]{1,2,0:T(8,128)(2,1)S(1)} all-to-all(bf16[4,256,192]{1,2,0:T(8,128)(2,1)S(1)} %bitcast.219), channel_id=1, replica_groups=mesh['wide'=8,'narrow'=4] {'narrow'}, dimensions={0} | all-to-all | bytes 786432 | tf_op jit(solution)/shard_map/all_to_all | solution.py:687
  1186.6 20.5 %collective-permute-done.39 = bf16[2,1,1,1024,192]{3,4,2,1,0:T(8,128)(2,1)S(1)} collective-permute-done((bf16[2,1,1,1024,192]{3,4,2,1,0:T(8,128)(2,1)S(1)}, bf16[2,1,1,1024,192]{3,4,2,1,0:T(8,128)(2,1)S(1)}, u32[]{:S(2)}, u32[]{:S(2)}) %collective-permute-start.39) | collective-permute-done | bytes 786464 | tf_op jit(solution)/shard_map/ppermute | solution.py:337
  1218.7 55.7 %collective-permute-done.37 = bf16[192,6400]{1,0:T(8,128)(2,1)} collective-permute-done((bf16[192,6400]{1,0:T(8,128)(2,1)}, bf16[192,6400]{1,0:T(8,128)(2,1)}, u32[]{:S(2)}, u32[]{:S(2)}) %collective-permute-start.37) | collective-permute-done | bytes 2457632 | tf_op jit(solution)/shard_map/ppermute | solution.py:342
  1274.4 48.7 %multiply_reduce_fusion = (f32[]{:T(128)}, f32[6288,192]{0,1:T(8,128)}) fusion(bf16[192,6400]{1,0:T(8,128)(2,1)} %collective-permute-done.37, bf16[192,6400]{1,0:T(8,128)(2,1)} %get-tuple-element.116, bf16[8192,192]{0,1:T(8,128)(2,1)} %select_n.321, s32[8192]{0:T(1024)} %bitcast.234), kind=kOutput, calls=%fused_computation.41 | convolution fusion | flops 19839092736 | bytes 12836868 | tf_op jit(solution)/shard_map/dot_general | solution.py:27
  1326.3 87.3 %reduce-scatter.8.cloned.1.call-done = bf16[24,6144]{1,0:T(8,128)(2,1)} async-done(((bf16[768,6144]{1,0:T(8,128)(2,1)}), bf16[24,6144]{1,0:T(8,128)(2,1)}) %reduce-scatter.8.cloned.1.call-update) | async-done | bytes 294928 | tf_op jit(solution)/shard_map/reduce_scatter | solution.py:461
  1413.7 140.5 %reduce-scatter.4.cloned.1.call-done = bf16[24,6144]{1,0:T(8,128)(2,1)} async-done(((bf16[768,6144]{1,0:T(8,128)(2,1)}), bf16[24,6144]{1,0:T(8,128)(2,1)}) %reduce-scatter.4.cloned.1.call-update) | async-done | bytes 294928 | tf_op jit(solution)/shard_map/reduce_scatter | solution.py:461
  1554.2 141.5 %reduce-scatter.6.cloned.1.call-done = bf16[24,6144]{1,0:T(8,128)(2,1)} async-done(((bf16[768,6144]{1,0:T(8,128)(2,1)}), bf16[24,6144]{1,0:T(8,128)(2,1)}) %reduce-scatter.6.cloned.1.call-update) | async-done | bytes 294928 | tf_op jit(solution)/shard_map/reduce_scatter | solution.py:461
  1709.5 32.3 %all-to-all-done.4 = bf16[32,6,24,128]{3,2,1,0:T(8,128)(2,1)S(1)} async-done(((bf16[32,6,24,128]{3,2,1,0:T(8,128)(2,1)}), bf16[32,6,24,128]{3,2,1,0:T(8,128)(2,1)S(1)}, u32[]{:S(2)}, u32[]{:S(2)}) %all-to-all-start.4) | async-done | bytes 1179680 | tf_op jit(solution)/shard_map/all_to_all | solution.py:739
  (707 shorter events, 670.2 us)
Async XLA Ops:
  7.2 177.6 %all-gather.12.cloned.1.call-start = ((), (), s32[]{:S(2)}) async-start(), calls=%async_computation.8 | async-start | bytes 4866048 | tf_op jit(solution)/shard_map/all_gather | solution.py:522
  48.6 284.3 %all-gather.14.cloned.1.call-start = ((), (), s32[]{:S(2)}) async-start(), calls=%async_computation.9 | async-start | bytes 10948608 | tf_op jit(solution)/shard_map/all_gather | solution.py:522
  49.6 314.7 %all-gather.16.cloned.1.call-start = ((), (), s32[]{:S(2)}) async-start(), calls=%async_computation.10 | async-start | bytes 8515584 | tf_op jit(solution)/shard_map/all_gather | solution.py:522
  50.4 471.5 %all-gather.18.cloned.1.call-start = ((), (), s32[]{:S(2)}) async-start(), calls=%async_computation.11 | async-start | bytes 10948608 | tf_op jit(solution)/shard_map/all_gather | solution.py:522
  210.1 167.8 %collective-permute-start.17 = (bf16[192,6400]{1,0:T(8,128)(2,1)}, bf16[192,6400]{1,0:T(8,128)(2,1)}, u32[]{:S(2)}, u32[]{:S(2)}) collective-permute-start(bf16[192,6400]{1,0:T(8,128)(2,1)} %pad.16), channel_id=1, source_target_pairs={{0,3},{1,0},{2,1},{3,2},{4,7},{5,4},{6,5},{7,6},{8,11},{9,8},{10,9... | collective-permute-start | bytes 7372808 | tf_op jit(solution)/shard_map/ppermute | solution.py:342
  217.4 83.5 %all-to-all-start.1 = ((bf16[4,256,192]{1,2,0:T(8,128)(2,1)}), bf16[4,256,192]{1,2,0:T(8,128)(2,1)}, u32[]{:S(2)}, u32[]{:S(2)}) async-start(bf16[4,256,192]{1,2,0:T(8,128)(2,1)} %copy.441), calls=%async_computation.1 | async-start | bytes 786432 | tf_op jit(solution)/shard_map/all_to_all | solution.py:564
  242.0 63.7 %collective-permute-start.3 = (bf16[1024,1536]{1,0:T(8,128)(2,1)}, bf16[1024,1536]{1,0:T(8,128)(2,1)}, u32[]{:S(2)}, u32[]{:S(2)}) collective-permute-start(bf16[1024,1536]{1,0:T(8,128)(2,1)} %pad_maximum_fusion.5), channel_id=1, source_target_pairs={{0,4},{4,0},{8,12},{12,8},{16,20},{20,16},{24,28},{28,24},{1,5},{5... | collective-permute-start | bytes 9437192 | tf_op jit(solution)/shard_map/ppermute | solution.py:337
  300.4 72.7 %collective-permute-start.26 = (bf16[2,2,1,1024,192]{3,4,2,1,0:T(8,128)(2,1)}, bf16[2,2,1,1024,192]{3,4,2,1,0:T(8,128)(2,1)}, u32[]{:S(2)}, u32[]{:S(2)}) collective-permute-start(bf16[2,2,1,1024,192]{3,4,2,1,0:T(8,128)(2,1)} %copy.517), channel_id=1, source_target_pairs={{0,4},{4,0},{8,12},{12,8},{16,20},{20,16},{24,28},{28,24},{1,5},{5... | collective-permute-start | bytes 4718600 | tf_op jit(solution)/shard_map/ppermute | solution.py:337
  367.5 57.8 %collective-permute-start.9 = (bf16[512,1536]{1,0:T(8,128)(2,1)S(1)}, bf16[512,1536]{1,0:T(8,128)(2,1)S(1)}, u32[]{:S(2)}, u32[]{:S(2)}) collective-permute-start(bf16[512,1536]{1,0:T(8,128)(2,1)S(1)} %convolution_convert_fusion.11), channel_id=1, source_target_pairs={{0,8},{4,12},{8,0},{12,4},{16,24},{20,28},{24,16},{28,20},{1,9},{5... | collective-permute-start | bytes 4718600 | tf_op jit(solution)/shard_map/ppermute | solution.py:337
  372.4 51.6 %collective-permute-start.7 = (bf16[256,1536]{1,0:T(8,128)(2,1)S(1)}, bf16[256,1536]{1,0:T(8,128)(2,1)S(1)}, u32[]{:S(2)}, u32[]{:S(2)}) collective-permute-start(bf16[256,1536]{1,0:T(8,128)(2,1)S(1)} %slice.345), channel_id=1, source_target_pairs={{0,8},{4,12},{8,0},{12,4},{16,24},{20,28},{24,16},{28,20},{1,9},{5... | collective-permute-start | bytes 2359304 | tf_op jit(solution)/shard_map/ppermute | solution.py:337
  376.8 63.4 %collective-permute-start.27 = (bf16[2,1,1,1024,192]{3,4,2,1,0:T(8,128)(2,1)S(1)}, bf16[2,1,1,1024,192]{3,4,2,1,0:T(8,128)(2,1)S(1)}, u32[]{:S(2)}, u32[]{:S(2)}) collective-permute-start(bf16[2,1,1,1024,192]{3,4,2,1,0:T(8,128)(2,1)S(1)} %constant_dynamic-slice_fusion.1), channel_id=1, source_target_pairs={{0,8},{4,12},{8,0},{12,4},{16,24},{20,28},{24,16},{28,20},{1,9},{5... | collective-permute-start | bytes 2359304 | tf_op jit(solution)/shard_map/ppermute | solution.py:337
  378.0 101.5 %collective-permute-start.18 = (bf16[192,6400]{1,0:T(8,128)(2,1)}, bf16[192,6400]{1,0:T(8,128)(2,1)}, u32[]{:S(2)}, u32[]{:S(2)}) collective-permute-start(bf16[192,6400]{1,0:T(8,128)(2,1)} %collective-permute-done.17), channel_id=1, source_target_pairs={{0,3},{1,0},{2,1},{3,2},{4,7},{5,4},{6,5},{7,6},{8,11},{9,8},{10,9... | collective-permute-start | bytes 7372808 | tf_op jit(solution)/shard_map/ppermute | solution.py:342
  425.2 60.5 %collective-permute-start.8 = (bf16[512,1536]{1,0:T(8,128)(2,1)}, bf16[512,1536]{1,0:T(8,128)(2,1)}, u32[]{:S(2)}, u32[]{:S(2)}) collective-permute-start(bf16[512,1536]{1,0:T(8,128)(2,1)} %pad_maximum_fusion.10), channel_id=1, source_target_pairs={{0,4},{4,0},{8,12},{12,8},{16,20},{20,16},{24,28},{28,24},{1,5},{5... | collective-permute-start | bytes 4718600 | tf_op jit(solution)/shard_map/ppermute | solution.py:337
  427.4 76.8 %collective-permute-start.10 = (bf16[1024,1536]{1,0:T(8,128)(2,1)}, bf16[1024,1536]{1,0:T(8,128)(2,1)}, u32[]{:S(2)}, u32[]{:S(2)}) collective-permute-start(bf16[1024,1536]{1,0:T(8,128)(2,1)} %pad_maximum_fusion.7), channel_id=1, source_target_pairs={{0,4},{4,0},{8,12},{12,8},{16,20},{20,16},{24,28},{28,24},{1,5},{5... | collective-permute-start | bytes 9437192 | tf_op jit(solution)/shard_map/ppermute | solution.py:337
  462.2 860.9 %all-reduce.8.cloned.1.call-start = ((), (), s32[]{:S(2)}) async-start(), calls=%async_computation.16 | async-start | bytes 13762560
  479.5 74.9 %collective-permute-start.19 = (bf16[192,6400]{1,0:T(8,128)(2,1)}, bf16[192,6400]{1,0:T(8,128)(2,1)}, u32[]{:S(2)}, u32[]{:S(2)}) collective-permute-start(bf16[192,6400]{1,0:T(8,128)(2,1)} %collective-permute-done.18), channel_id=1, source_target_pairs={{0,3},{1,0},{2,1},{3,2},{4,7},{5,4},{6,5},{7,6},{8,11},{9,8},{10,9... | collective-permute-start | bytes 7372808 | tf_op jit(solution)/shard_map/ppermute | solution.py:342
  854.5 49.8 %collective-permute-start.32 = (bf16[512,1536]{1,0:T(8,128)(2,1)S(1)}, bf16[512,1536]{1,0:T(8,128)(2,1)S(1)}, u32[]{:S(2)}, u32[]{:S(2)}) collective-permute-start(bf16[512,1536]{1,0:T(8,128)(2,1)S(1)} %slice.533), channel_id=1, source_target_pairs={{0,8},{4,12},{8,0},{12,4},{16,24},{20,28},{24,16},{28,20},{1,9},{5... | collective-permute-start | bytes 4718600 | tf_op jit(solution)/shard_map/ppermute | solution.py:337
  935.3 478.4 %reduce-scatter.8.cloned.1.call-start = ((), (), s32[]{:S(2)}) async-start(), calls=%async_computation.14 | async-start | bytes 9732096 | tf_op jit(solution)/shard_map/reduce_scatter | solution.py:461
  944.0 610.2 %reduce-scatter.4.cloned.1.call-start = ((), (), s32[]{:S(2)}) async-start(), calls=%async_computation.12 | async-start | bytes 9732096 | tf_op jit(solution)/shard_map/reduce_scatter | solution.py:461
  958.7 737.1 %reduce-scatter.6.cloned.1.call-start = ((), (), s32[]{:S(2)}) async-start(), calls=%async_computation.13 | async-start | bytes 9732096 | tf_op jit(solution)/shard_map/reduce_scatter | solution.py:461
  996.5 95.0 %collective-permute-start.35 = (bf16[192,6400]{1,0:T(8,128)(2,1)}, bf16[192,6400]{1,0:T(8,128)(2,1)}, u32[]{:S(2)}, u32[]{:S(2)}) collective-permute-start(bf16[192,6400]{1,0:T(8,128)(2,1)} %get-tuple-element.117), channel_id=1, source_target_pairs={{0,1},{1,2},{2,3},{3,0},{4,5},{5,6},{6,7},{7,4},{8,9},{9,10},{10,1... | collective-permute-start | bytes 7372808 | tf_op jit(solution)/shard_map/ppermute | solution.py:342
  1035.2 728.2 %all-gather.20.cloned.1.call-start = ((), (), s32[]{:S(2)}) async-start(), calls=%async_computation.15 | async-start | bytes 2703360 | tf_op jit(solution)/shard_map/all_gather | solution.py:731
  1096.0 85.0 %collective-permute-start.36 = (bf16[192,6400]{1,0:T(8,128)(2,1)}, bf16[192,6400]{1,0:T(8,128)(2,1)}, u32[]{:S(2)}, u32[]{:S(2)}) collective-permute-start(bf16[192,6400]{1,0:T(8,128)(2,1)} %add_convert_fusion.2), channel_id=1, source_target_pairs={{0,1},{1,2},{2,3},{3,0},{4,5},{5,6},{6,7},{7,4},{8,9},{9,10},{10,1... | collective-permute-start | bytes 7372808 | tf_op jit(solution)/shard_map/ppermute | solution.py:342
  1185.4 89.0 %collective-permute-start.37 = (bf16[192,6400]{1,0:T(8,128)(2,1)}, bf16[192,6400]{1,0:T(8,128)(2,1)}, u32[]{:S(2)}, u32[]{:S(2)}) collective-permute-start(bf16[192,6400]{1,0:T(8,128)(2,1)} %add_convert_fusion.1), channel_id=1, source_target_pairs={{0,1},{1,2},{2,3},{3,0},{4,5},{5,6},{6,7},{7,4},{8,9},{9,10},{10,1... | collective-permute-start | bytes 7372808 | tf_op jit(solution)/shard_map/ppermute | solution.py:342
  (201 other events, 5564.5 us)
Sparse Core Ops, SparseCore 0:
  48.7 61.4 all-gather.11
  113.6 118.9 all-gather.13
  235.4 128.8 all-gather.15
  367.5 144.8 all-gather.17
  935.4 323.5 all-reduce.7
  1265.8 147.8 reduce-scatter.7
  1419.6 134.5 reduce-scatter.3
  1561.1 134.5 reduce-scatter.5
  1701.4 61.9 all-gather.19

commit v2 on v1

--- a/solution.py
+++ b/solution.py
@@ -175,11 +175,27 @@
     )(*extra, queries, keys_values, keys_values, mixed_rows, log_total, grad_mixed)
 
 
-def head_kernel(vocab, tile, used_ref, rows_ref, table_ref, mixed_ref, exp_ref, stats_ref, logits_ref):
+def head_kernel(vocab, tile, parts, used_ref, rows_ref, *refs):
+    part_refs, refs = refs[:parts], refs[parts:]
+    mixed_ref, exp_ref, stats_ref, logits_ref, table_ref, arrived = refs
     step = pl.program_id(0)
     padded = table_ref.shape[1]
     shape = (rows_ref.shape[0], 128)
     lane = lax.broadcasted_iota(jnp.int32, shape, 1)
+
+    @pl.when(step == 0)
+    def _():
+        height = D // parts
+        copies = [
+            pltpu.make_async_copy(
+                part, table_ref.at[pl.ds(k * height, height), :], arrived.at[k]
+            )
+            for k, part in enumerate(part_refs)
+        ]
+        for copy in copies:
+            copy.start()
+        for copy in copies:
+            copy.wait()
 
     @pl.when(used_ref[step] == 0)
     def _():
@@ -203,30 +219,32 @@
         for start in range(0, padded, tile):
             exponent = jnp.exp(logits_ref[:, start : start + tile] - top)
             summed += jnp.sum(exponent, axis=1, keepdims=True)
-            low = exponent.astype(jnp.bfloat16)
-            exp_ref[:, start : start + tile] = low
-            mixed += dot_nt(low, table_ref[:, start : start + tile])
+            lowered = exponent.astype(jnp.bfloat16)
+            exp_ref[:, start : start + tile] = lowered
+            mixed += dot_nt(lowered, table_ref[:, start : start + tile])
         mixed_ref[...] = mixed
         stats_ref[...] = jnp.where(lane == 0, top, summed)
 
 
-def head_forward(rows_all, table, used, vocab, block_rows, tile):
-    rows, padded = rows_all.shape[0], table.shape[1]
+def head_forward(rows_all, table_parts, used, vocab, block_rows, tile):
+    rows, padded, parts = rows_all.shape[0], table_parts[0].shape[1], len(table_parts)
     return pl.pallas_call(
-        lambda *refs: head_kernel(vocab, tile, *refs),
+        lambda *refs: head_kernel(vocab, tile, parts, *refs),
         grid_spec=pltpu.PrefetchScalarGridSpec(
             num_scalar_prefetch=1,
             grid=(rows // block_rows,),
-            in_specs=[
-                pl.BlockSpec((block_rows, D), lambda i, used: (i, 0)),
-                pl.BlockSpec((D, padded), lambda i, used: (0, 0), pipeline_mode=pl.Buffered(1)),
-            ],
+            in_specs=[pl.BlockSpec((block_rows, D), lambda i, used: (i, 0))]
+            + [pl.BlockSpec(memory_space=pl.ANY)] * parts,
             out_specs=[
                 pl.BlockSpec((block_rows, D), lambda i, used: (i, 0)),
                 pl.BlockSpec((block_rows, padded), lambda i, used: (i, 0)),
                 pl.BlockSpec((block_rows, 128), lambda i, used: (i, 0)),
             ],
-            scratch_shapes=[pltpu.VMEM((block_rows, padded), jnp.float32)],
+            scratch_shapes=[
+                pltpu.VMEM((block_rows, padded), jnp.float32),
+                pltpu.VMEM((D, padded), jnp.bfloat16),
+                pltpu.SemaphoreType.DMA((parts,)),
+            ],
         ),
         out_shape=[
             jax.ShapeDtypeStruct((rows, D), jnp.float32),
@@ -239,7 +257,7 @@
             bytes_accessed=2 * rows * padded + 2 * padded * D,
             transcendentals=rows * padded,
         ),
-    )(used, rows_all, table)
+    )(used, rows_all, *table_parts)
 
 
 def table_grad_kernel(tile, used_ref, rows_ref, exp_ref, info_ref, grad_ref, total_ref):
@@ -298,7 +316,8 @@
 BW = 128
 BLOCKS = 174
 EXTENTS = [D, 3 * D, D, 2 * FF, FF, 3 * D, D, D, 2 * D, D, 2 * FF, FF]
-GATHERS = [[0, 1], [2, 3, 4], [5, 6, 7, 8], [9, 10, 11]]
+GATHERS = [[0, 1], [5, 6, 7, 8], [9, 10, 11]]
+PERMUTED = [2, 3, 4]
 SMALL_ROWS = 2 * POS + 8
 
 norm_eps = 1e-06
@@ -352,31 +371,8 @@
 
 def gather_wide(values, order):
     bits = wide_bits()
-    whole = values.reshape((1,) * bits + values.shape)
-    for level in order:
-        axis = bits - 1 - level
-        other = swap(whole, 1 << level)
-        mine_last = bit_value(level) == 1
-        whole = jnp.where(
-            mine_last,
-            jnp.concatenate([other, whole], axis=axis),
-            jnp.concatenate([whole, other], axis=axis),
-        )
+    whole = join_wide(values.reshape((1,) * bits + values.shape), order)
     return whole.reshape((1 << bits,) + values.shape)
-
-
-def scatter_wide(values, order):
-    bits = wide_bits()
-    rest = values.shape[1:]
-    whole = values.reshape((2,) * bits + rest)
-    for level in order:
-        axis = bits - 1 - level
-        bit = bit_value(level)
-        mine = lax.dynamic_index_in_dim(whole, bit, axis, keepdims=True)
-        theirs = lax.dynamic_index_in_dim(whole, 1 - bit, axis, keepdims=True)
-        got = swap(low(theirs), 1 << level)
-        whole = low(mine.astype(jnp.float32) + got.astype(jnp.float32))
-    return whole.reshape(rest)
 
 
 def split_orders():
@@ -393,13 +389,187 @@
     )
 
 
-def scatter_wide_fast(values):
-    first, second = split_orders()
-    half = values.shape[-1] // 2
-    return jnp.concatenate(
-        [scatter_wide(values[..., :half], [0] + first), scatter_wide(values[..., half:], [0] + second)],
-        axis=-1,
-    )
+def tie(*values):
+    return lax.optimization_barrier(values)
+
+
+def from_narrow(rows):
+    count = lax.axis_size("narrow")
+    ahead = [rows] + [shift(rows, -step) for step in range(1, count)]
+    start = (count - lax.axis_index("narrow")) % count
+    return lax.dynamic_slice_in_dim(jnp.stack(ahead + ahead), start, count, axis=0)
+
+
+def join(whole, other, level):
+    axis = wide_bits() - 1 - level
+    return jnp.where(
+        bit_value(level) == 1,
+        jnp.concatenate([other, whole], axis=axis),
+        jnp.concatenate([whole, other], axis=axis),
+    )
+
+
+def join_wide(whole, order):
+    for level in order:
+        whole = join(whole, swap(whole, 1 << level), level)
+    return whole
+
+
+class Flow:
+    def __init__(self, stages):
+        self.stages, self.result, self.values = stages, None, None
+        self.pull(None)
+
+    def pull(self, values):
+        try:
+            self.values = self.stages.send(values)
+        except StopIteration as end:
+            self.result, self.values = end.value, None
+
+    def drain(self):
+        while self.values is not None:
+            self.pull(self.values)
+        return self.result
+
+
+def step(main, *flows):
+    for _ in range(2):
+        live = [flow for flow in flows if flow.values is not None]
+        main, values = lax.optimization_barrier((main, [flow.values for flow in live]))
+        for flow, tied in zip(live, values):
+            flow.pull(tied)
+    return main
+
+
+def scatter_flow(factors, extra=None):
+    bits = wide_bits()
+    count = lax.axis_size("narrow")
+    here = lax.axis_index("narrow")
+    pairs = 1 << (bits - 1)
+    low_bit = bit_value(0)
+
+    def products(side, got):
+        results, offset = [], 0
+        for left, right in factors:
+            split = left.reshape(left.shape[0], pairs, 2, -1)
+            chosen = lax.dynamic_index_in_dim(split, side, 2, keepdims=False)
+            result = dot_tn(chosen.reshape(left.shape[0], -1), right)
+            if got is not None:
+                result = result + got[:, offset : offset + right.shape[1]].astype(jnp.float32)
+            if extra is not None and extra[0] == offset:
+                split = extra[1].reshape(pairs, 2, -1, right.shape[1])
+                chosen = lax.dynamic_index_in_dim(split, side, 1, keepdims=False)
+                result = result + chosen.reshape(result.shape)
+            offset += right.shape[1]
+            results.append(low(result))
+        return jnp.concatenate(results, axis=1)
+
+    yield []
+    (sent,) = yield [products(1 - low_bit, None)]
+    (got,) = yield [swap(sent, 1)]
+    mine = products(low_bit, got)
+    middle = mine.shape[1] // 256 * 128
+    orders = split_orders()
+    wholes = [
+        part.reshape((2,) * (bits - 1) + (-1, part.shape[1]))
+        for part in (mine[:, :middle], mine[:, middle:])
+    ]
+    for number in range(bits - 1):
+        levels = [order[number] for order in orders]
+        theirs = [
+            lax.dynamic_index_in_dim(whole, 1 - bit_value(level), bits - 1 - level, keepdims=True)
+            for whole, level in zip(wholes, levels)
+        ]
+        tied = yield wholes + theirs
+        wholes, theirs = tied[:2], tied[2:]
+        got = yield [swap(part, 1 << level) for part, level in zip(theirs, levels)]
+        wholes = [
+            low(
+                lax.dynamic_index_in_dim(
+                    whole, bit_value(level), bits - 1 - level, keepdims=True
+                ).astype(jnp.float32)
+                + part.astype(jnp.float32)
+            )
+            for whole, part, level in zip(wholes, got, levels)
+        ]
+    rows = jnp.concatenate([whole.reshape(count, -1, whole.shape[-1]) for whole in wholes], axis=-1)
+    pieces = [
+        lax.dynamic_index_in_dim(rows, (here + k) % count, 0, keepdims=False) for k in range(count)
+    ]
+    pieces = yield pieces
+    got = yield [shift(pieces[k], k) for k in range(1, count)]
+    total = pieces[0].astype(jnp.float32)
+    for piece in got:
+        total = total + piece.astype(jnp.float32)
+    return low(total)
+
+
+def ring_flow(parts):
+    moving = parts[-1]
+    yield []
+    for part in parts[-2::-1]:
+        (moving,) = yield [low(moving)]
+        (moving,) = yield [shift(moving, 1)]
+        moving = part.astype(jnp.float32) + moving.astype(jnp.float32)
+    return moving
+
+
+def table_flow(own):
+    parts = [own]
+    yield []
+    for _ in range(lax.axis_size("narrow") - 1):
+        (moving,) = yield [parts[-1]]
+        (moving,) = yield [shift(moving, -1)]
+        parts.append(moving)
+    return parts
+
+
+def keys_flow(rows):
+    bit = lax.axis_size("narrow") // 2
+    yield []
+    while bit:
+        (rows,) = yield [rows]
+        rows, other = yield [rows, swap(rows, bit)]
+        rows = jnp.concatenate([rows, other], axis=0)
+        bit //= 2
+    return rows
+
+
+def return_flow(parts):
+    bit = 1
+    yield []
+    while bit < lax.axis_size("narrow"):
+        half = parts[0].shape[0] // 2
+        sent = yield [part[half:] for part in parts]
+        got = yield [swap(other, bit) for other in sent]
+        parts = [
+            low(part[:half].astype(jnp.float32) + other.astype(jnp.float32))
+            for part, other in zip(parts, got)
+        ]
+        bit *= 2
+    return jnp.concatenate(parts, axis=1)
+
+
+def gather_flow(rows):
+    bits = wide_bits()
+    count = lax.axis_size("narrow")
+    columns = rows.shape[1]
+    middle = columns // 2
+    yield []
+    (rows,) = yield [rows]
+    ahead = yield [rows] + [shift(rows, -k) for k in range(1, count)]
+    start = (count - lax.axis_index("narrow")) % count
+    stacked = lax.dynamic_slice_in_dim(jnp.stack(ahead + ahead), start, count, axis=0)
+    stacked = stacked.reshape((1,) * bits + stacked.shape)
+    parts = [stacked[..., :middle], stacked[..., middle:]]
+    orders = split_orders()
+    for number in range(bits - 1):
+        parts = yield parts
+        tied = yield parts + [swap(part, 1 << o[number]) for part, o in zip(parts, orders)]
+        parts = [join(tied[k], tied[k + 2], orders[k][number]) for k in range(2)]
+    (whole,) = yield [jnp.concatenate(parts, axis=-1)]
+    whole, other = yield [whole, swap(whole, 1)]
+    return join(whole, other, 0).reshape(-1, columns)
 
 
 def group_offsets():
@@ -410,55 +580,11 @@
     return offsets
 
 
-def gather_group(rows):
-    bit = lax.axis_size("narrow") // 2
-    while bit:
-        rows = jnp.concatenate([rows, swap(rows, bit)], axis=0)
-        bit //= 2
-    return rows
-
-
-def return_group(grads):
-    bit = 1
-    while bit < lax.axis_size("narrow"):
-        half = grads.shape[0] // 2
-        got = swap(low(grads[half:]), bit)
-        grads = grads[:half].astype(jnp.float32) + got.astype(jnp.float32)
-        bit *= 2
-    return low(grads)
-
-
 def feed_forward(stream, gain_vec, w_in, w_back):
     normed = low(rms_norm(stream, gain_vec))
     gate_up = dot_nn(normed, w_in)
     hidden = low(gated_unit(gate_up))
     return (dot_nt(hidden, w_back), (normed, gate_up, hidden))
-
-
-def feed_back(stream, gain_vec, w_in, w_back, kept_state, grad_out):
-    normed, gate_up, hidden = kept_state
-    grad_low = low(grad_out)
-    grad_w_back = low(dot_tn(grad_low, hidden))
-    _, pullback = jax.vjp(gated_unit, gate_up)
-    grad_gate_up = low(pullback(dot_nn(grad_low, w_back))[0])
-    grad_w_in = low(dot_tn(normed, grad_gate_up))
-    grad_stream, grad_gain = norm_back(stream, gain_vec, dot_nt(grad_gate_up, w_in))
-    return (grad_stream, grad_gain, grad_w_in, grad_w_back)
-
-
-def attention_back(queries, keys_values, positions, mixed_rows, log_total, w_out, grad_out):
-    grad_low = low(grad_out)
-    grad_w_out = low(dot_tn(mixed_rows, grad_low))
-    grad_mixed = low(dot_nt(grad_low, w_out))
-    grad_query, grad_key, grad_value = attend_back(
-        queries, keys_values, positions, mixed_rows, log_total, grad_mixed
-    )
-    grad_pair = return_group(jnp.concatenate([grad_key, grad_value], axis=1))
-    return (grad_w_out, grad_query, grad_pair)
-
-
-def own_shards(columns):
-    return lax.psum_scatter(columns, BOTH, scatter_dimension=0, tiled=True)
 
 
 def adamw(param, moment, second, grad, step_count):
@@ -512,24 +638,13 @@
 
     block_of_slot = (slot_ids[:, None] == jnp.arange(slot_total)[None, :]).astype(jnp.bfloat16)
     pieces = low(master_slabs).reshape(own_count, devices, piece, BW).transpose(1, 0, 2, 3)
-    pieces = lax.all_to_all(pieces, BOTH, 0, 0).reshape(slot_total, piece * BW)
-    ordered = low(dot_nn(block_of_slot, pieces)).reshape(BLOCKS, piece, BW)
-    row_shard = ordered.transpose(1, 0, 2).reshape(piece, BLOCKS * BW)
-    weights = [None] * len(EXTENTS)
-    for numbers in GATHERS:
-        begin = sum(EXTENTS[: numbers[0]])
-        size = sum(EXTENTS[n] for n in numbers)
-        group = lax.all_gather(row_shard[:, begin : begin + size], BOTH, axis=0, tiled=True)
-        for n in numbers:
-            offset = sum(EXTENTS[:n]) - begin
-            weights[n] = group[:, offset : offset + EXTENTS[n]]
+    pieces = lax.all_to_all(pieces, BOTH, 0, 0)
 
     exchange = []
     for w in range(wide_count):
         for n in range(narrow_count):
             base = w // narrow_count * narrow_count
             exchange.append((w * narrow_count + n, (base + n) * narrow_count + w % narrow_count))
-    patches = lax.ppermute(patches, BOTH, exchange)
     whole_ids = lax.ppermute(
         jnp.concatenate([patch_rows, patch_cols, input_ids, target_ids]), BOTH, exchange
     )
@@ -541,6 +656,8 @@
     screens_info = lax.all_gather(
         jnp.concatenate([target_lengths[:, None], loss_mask], axis=1), "wide", axis=0, tiled=True
     )
+    pieces, patches, every_input, screens_info = tie(pieces, patches, every_input, screens_info)
+    patches = lax.ppermute(patches, BOTH, exchange)
     counted = (
         (jnp.arange(TGT)[None, :] < screens_info[:, :1]) & (screens_info[:, 1:] == 1)
     ).astype(jnp.float32)
@@ -550,6 +667,24 @@
     ).reshape(-1)
     own_counted = lax.dynamic_slice_in_dim(row_counted, wide_pos * dec_rows, dec_rows)
 
+    ordered = low(dot_nn(block_of_slot, pieces.reshape(slot_total, piece * BW)))
+    row_shard = ordered.reshape(BLOCKS, piece, BW).transpose(1, 0, 2).reshape(piece, BLOCKS * BW)
+    weights = [None] * len(EXTENTS)
+
+    def shard_of(numbers):
+        begin = sum(EXTENTS[: numbers[0]])
+        return row_shard[:, begin : begin + sum(EXTENTS[n] for n in numbers)]
+
+    def take(numbers, group):
+        offset = 0
+        for n in numbers:
+            weights[n] = group[:, offset : offset + EXTENTS[n]]
+            offset += EXTENTS[n]
+
+    for numbers in GATHERS:
+        take(numbers, lax.all_gather(shard_of(numbers), BOTH, axis=0, tiled=True))
+    flow_weights = Flow(gather_flow(shard_of(PERMUTED)))
+
     padded = -(-vocab_rows // 256) * 256
     table_low = low(vocab_table)
     columns = jnp.arange(vocab_rows)
@@ -559,17 +694,19 @@
 
     def looked_up(ids):
         onehot = (ids[:, None] == columns[None, :]).astype(jnp.bfloat16)
-        found = low(dot_nn(onehot, table_low)).reshape(wide_count, narrow_count * dec_rows, features)
-        found = scatter_wide(found, list(range(wide_bits())))
+        found = low(dot_nn(onehot, table_low))
+        return found.reshape(wide_count, narrow_count * dec_rows, features)
+
+    def delivered(found):
+        found = low(jnp.sum(found.astype(jnp.float32), axis=0))
         found = lax.all_to_all(found.reshape(narrow_count, dec_rows, features), "narrow", 0, 0)
-        return found.transpose(1, 0, 2).reshape(dec_rows, D)
-
-    stream_dec = looked_up(flat_inputs).astype(jnp.float32)
-    target_rows = looked_up(flat_targets).astype(jnp.float32)
-    table_parts = [jnp.pad(table_low.T, ((0, 0), (0, padded - vocab_rows)))]
-    for _ in range(narrow_count - 1):
-        table_parts.append(shift(table_parts[-1], -1))
-    table = jnp.concatenate(table_parts, axis=0)
+        return found.transpose(1, 0, 2).reshape(dec_rows, D).astype(jnp.float32)
+
+    flat_inputs = step(flat_inputs, flow_weights)
+    found_inputs = looked_up(flat_inputs)
+    found_inputs = step(found_inputs, flow_weights)
+    found_inputs = lax.all_to_all(found_inputs, "wide", 0, 0)
+    flow_table = Flow(table_flow(jnp.pad(table_low.T, ((0, 0), (0, padded - vocab_rows)))))
 
     gain_rows = small_params[2 * POS :]
     picked = jnp.concatenate(
@@ -588,34 +725,57 @@
         + dot_nn(picked, tables_high)
         + dot_nn(picked, tables_rest)
     )
+    enc_zero = step(enc_zero, flow_weights)
     enc_normed = low(rms_norm(enc_zero, gain_rows[0]))
     enc_mix = low(dot_nn(enc_normed, weights[1]))
-    enc_keys = gather_group(enc_mix[:, D:])
-    enc_mixed, enc_total = attend(enc_mix[:, :D], enc_keys, None)
+    enc_query = enc_mix[:, :D]
+    flow_keys = Flow(keys_flow(enc_mix[:, D:]))
+    enc_query, flat_targets = step((enc_query, flat_targets), flow_keys, flow_table)
+    found_targets = looked_up(flat_targets)
+    enc_query, found_targets = step((enc_query, found_targets), flow_keys, flow_weights)
+    found_targets = lax.all_to_all(found_targets, "wide", 0, 0)
+    enc_query = step(enc_query, flow_keys)
+    enc_keys = flow_keys.drain()
+    enc_mixed, enc_total = attend(enc_query, enc_keys, None)
+    enc_mixed, found_inputs = step((enc_mixed, found_inputs), flow_weights)
+    take(PERMUTED, flow_weights.drain())
+    dec_zero = delivered(found_inputs)
     enc_one = enc_zero + dot_nn(enc_mixed, weights[2])
-    branch, enc_ffn = feed_forward(enc_one, gain_rows[1], weights[3], weights[4])
-    enc_two = enc_one + branch
-    encoded = low(rms_norm(enc_two, gain_rows[2]))
+    enc_fnormed = low(rms_norm(enc_one, gain_rows[1]))
+    enc_gate = dot_nn(enc_fnormed, weights[3])
+    enc_hidden = low(gated_unit(enc_gate))
+    enc_ffn = (enc_fnormed, enc_gate, enc_hidden)
 
     query_pos = (member * dec_rows + jnp.arange(dec_rows)).astype(jnp.int32)
     key_pos = jnp.concatenate(
         [(member ^ offset) * dec_rows + jnp.arange(dec_rows) for offset in group_offsets()]
     ).astype(jnp.int32)
     causal = (query_pos, key_pos)
-    dec_zero = stream_dec
     dec_normed = low(rms_norm(dec_zero, gain_rows[3]))
     dec_mix = low(dot_nn(dec_normed, weights[5]))
-    self_keys = gather_group(dec_mix[:, D:])
-    self_mixed, self_total = attend(dec_mix[:, :D], self_keys, causal)
+    flow_keys = Flow(keys_flow(dec_mix[:, D:]))
+    enc_hidden, found_targets = step((enc_hidden, found_targets), flow_keys, flow_table)
+    enc_two = enc_one + dot_nt(enc_hidden, weights[4])
+    encoded = low(rms_norm(enc_two, gain_rows[2]))
+    flow_cross = Flow(keys_flow(low(dot_nn(encoded, weights[8]))))
+    dec_query = dec_mix[:, :D]
+    dec_query, found_targets = step((dec_query, found_targets), flow_keys, flow_cross)
+    target_rows = delivered(found_targets)
+    dec_query = step(dec_query, flow_keys)
+    self_keys = flow_keys.drain()
+    self_mixed, self_total = attend(dec_query, self_keys, causal)
     dec_one = dec_zero + dot_nn(self_mixed, weights[6])
     cross_normed = low(rms_norm(dec_one, gain_rows[4]))
     cross_query = low(dot_nn(cross_normed, weights[7]))
-    cross_keys = gather_group(low(dot_nn(encoded, weights[8])))
+    cross_query, target_rows = step((cross_query, target_rows), flow_cross)
+    cross_query = step(cross_query, flow_cross, flow_table)
+    cross_keys = flow_cross.drain()
     cross_mixed, cross_total = attend(cross_query, cross_keys, None)
     dec_two = dec_one + dot_nn(cross_mixed, weights[9])
     branch, dec_ffn = feed_forward(dec_two, gain_rows[5], weights[10], weights[11])
     dec_three = dec_two + branch
     final = low(rms_norm(dec_three, gain_rows[6]) * D ** (-0.5))
+    table_parts = flow_table.drain()
 
     rotated = lax.dynamic_slice_in_dim(
         jnp.concatenate([final, final], axis=1), narrow_pos * features, D, axis=1
@@ -625,7 +785,9 @@
     block_rows = 256
     used = jnp.any(row_counted.reshape(-1, block_rows) != 0, axis=1).astype(jnp.int32)
     tile = padded // 5 if padded % 640 == 0 else 256
-    mixed, exps, stats = head_forward(rows_all, table, used, vocab_rows, block_rows, tile)
+    mixed, exps, stats = head_forward(
+        rows_all, table_parts, used, vocab_rows, block_rows, tile
+    )
     top_part, summed_part = stats[:, 0], stats[:, 1]
     stats_all = lax.all_gather(jnp.stack([top_part, summed_part]), "wide", axis=0)
     top_logit = jnp.max(stats_all[:, 0], axis=0)
@@ -633,13 +795,9 @@
     log_total = top_logit + jnp.log(summed)
     row_weight = row_counted / tokens_counted
     scale = row_weight * jnp.exp(top_part - log_total)
-    grad_rows = (mixed * scale[:, None]).reshape(wide_count, dec_rows, D)
-    grad_back = scatter_wide_fast(grad_rows).astype(jnp.float32)
-    grad_back = lax.dynamic_slice_in_dim(
-        jnp.concatenate([grad_back, grad_back], axis=1), (D - narrow_pos * features) % D, D, axis=1
-    )
+    grad_rows = low(mixed * scale[:, None]).reshape(wide_count, dec_rows, D)
+    grad_rows = lax.all_to_all(grad_rows, "wide", 0, 0)
     own_weight = own_counted / tokens_counted
-    grad_final = grad_back - own_weight[:, None] * target_rows
     target_logit = jnp.sum(final.astype(jnp.float32) * target_rows, axis=1)
     own_total = lax.dynamic_slice_in_dim(log_total, wide_pos * dec_rows, dec_rows)
     loss_local = jnp.sum(own_counted * (own_total - target_logit))
@@ -653,74 +811,121 @@
     )
     grad_table = table_grad(rows_all, exps, info, used, block_rows, tile)
     grad_parts = grad_table.reshape(narrow_count, features, padded)
-    moving = grad_parts[narrow_count - 1]
-    for k in range(narrow_count - 2, -1, -1):
-        moving = grad_parts[k].astype(jnp.float32) + shift(low(moving), 1).astype(jnp.float32)
-    head_grad = moving[:, :vocab_rows].T
+    ring = Flow(ring_flow([grad_parts[k] for k in range(narrow_count)]))
+    grad_rows = step(grad_rows, ring)
+    grad_back = jnp.sum(grad_rows.astype(jnp.float32), axis=0)
+    grad_back = lax.dynamic_slice_in_dim(
+        jnp.concatenate([grad_back, grad_back], axis=1), (D - narrow_pos * features) % D, D, axis=1
+    )
+    grad_final = grad_back - own_weight[:, None] * target_rows
 
     grad_three, gain_final = norm_back(dec_three, gain_rows[6], grad_final * D ** (-0.5))
-    grad_two, gain_dffn, grad_in, grad_out = feed_back(
-        dec_two, gain_rows[5], weights[10], weights[11], dec_ffn, grad_three
-    )
-    shard_dffn = own_shards(jnp.concatenate([grad_in, grad_out], axis=1))
+    low_three = low(grad_three)
+    _, pullback = jax.vjp(gated_unit, dec_ffn[1])
+    grad_gate = low(pullback(dot_nn(low_three, weights[11]))[0])
+    flow_dffn = Flow(scatter_flow([(dec_ffn[0], grad_gate), (low_three, dec_ffn[2])]))
+    grad_gate = step(grad_gate, flow_dffn)
+    grad_two, gain_dffn = norm_back(dec_two, gain_rows[5], dot_nt(grad_gate, weights[10]))
     grad_two = grad_two + grad_three
-    grad_cout, grad_query, grad_pair = attention_back(
-        cross_query, cross_keys, None, cross_mixed, cross_total, weights[9], grad_two
-    )
-    grad_cq = low(dot_tn(cross_normed, grad_query))
-    grad_one, gain_cross = norm_back(dec_one, gain_rows[4], dot_nt(grad_query, weights[7]))
+    low_two = low(grad_two)
+    grad_mixed = low(dot_nt(low_two, weights[9]))
+    grad_mixed = step(grad_mixed, flow_dffn)
+    grad_cq, grad_key, grad_value = attend_back(
+        cross_query, cross_keys, None, cross_mixed, cross_total, grad_mixed
+    )
+    flow_cross = Flow(return_flow([grad_key, grad_value]))
+    grad_cq = step(grad_cq, flow_cross)
+    grad_one, gain_cross = norm_back(dec_one, gain_rows[4], dot_nt(grad_cq, weights[7]))
     grad_one = grad_one + grad_two
-    grad_ckv = low(dot_tn(encoded, grad_pair))
-    grad_encoded = dot_nt(grad_pair, weights[8])
-    grad_so, grad_query, grad_pair = attention_back(
-        dec_mix[:, :D], self_keys, causal, self_mixed, self_total, weights[6], grad_one
-    )
-    grad_mix = jnp.concatenate([grad_query, grad_pair], axis=1)
-    grad_sqkv = low(dot_tn(dec_normed, grad_mix))
-    shard_dattn = own_shards(
-        jnp.concatenate([grad_sqkv, grad_so, grad_cq, grad_ckv, grad_cout], axis=1)
-    )
-    grad_zero, gain_self = norm_back(dec_zero, gain_rows[3], dot_nt(grad_mix, weights[5]))
+    low_one = low(grad_one)
+    grad_mixed = low(dot_nt(low_one, weights[6]))
+    grad_mixed = step(grad_mixed, flow_cross)
+    grad_sq, grad_key, grad_value = attend_back(
+        dec_mix[:, :D], self_keys, causal, self_mixed, self_total, grad_mixed
+    )
+    flow_self = Flow(return_flow([grad_key, grad_value]))
+    grad_sq = step(grad_sq, flow_self, flow_dffn)
+    grad_sq = step(grad_sq, flow_self, ring)
+    grad_sq = step(grad_sq, flow_cross)
+    grad_ckv = flow_cross.drain()
+
+    grad_two, gain_efinal = norm_back(enc_two, gain_rows[2], dot_nt(grad_ckv, weights[8]))
+    low_etwo = low(grad_two)
+    _, pullback = jax.vjp(gated_unit, enc_ffn[1])
+    grad_gate = low(pullback(dot_nn(low_etwo, weights[4]))[0])
+    grad_gate = step(grad_gate, flow_self, flow_dffn)
+    grad_smix = jnp.concatenate([grad_sq, flow_self.drain()], axis=1)
+    grad_zero, gain_self = norm_back(dec_zero, gain_rows[3], dot_nt(grad_smix, weights[5]))
     grad_tokens = low(grad_zero + grad_one)
-
     sent = grad_tokens.reshape(dec_rows, narrow_count, features).transpose(1, 0, 2)
     sent = lax.all_to_all(sent, "narrow", 0, 0).reshape(narrow_count * dec_rows, features)
-    sent = gather_wide(sent, list(range(wide_bits()))[::-1]).reshape(-1, features)
+    sent = lax.all_gather(sent, "wide", axis=0, tiled=True)
+    flow_dattn = Flow(
+        scatter_flow(
+            [
+                (dec_normed, grad_smix),
+                (self_mixed, low_one),
+                (cross_normed, grad_cq),
+                (encoded, grad_ckv),
+                (cross_mixed, low_two),
+            ]
+        )
+    )
+    flow_effn = Flow(scatter_flow([(enc_ffn[0], grad_gate), (low_etwo, enc_ffn[2])]))
+    grad_gate = step(grad_gate, flow_dattn, flow_effn)
+    grad_one, gain_effn = norm_back(enc_one, gain_rows[1], dot_nt(grad_gate, weights[3]))
+    grad_one = grad_one + grad_two
+    low_eone = low(grad_one)
+    grad_mixed = low(dot_nt(low_eone, weights[2]))
+    grad_mixed = step(grad_mixed, flow_dattn, flow_effn)
+    grad_mixed = step(grad_mixed, flow_dffn, ring)
+    grad_eq, grad_key, grad_value = attend_back(
+        enc_mix[:, :D], enc_keys, None, enc_mixed, enc_total, grad_mixed
+    )
+    flow_enc = Flow(return_flow([grad_key, grad_value]))
+    grad_eq = step(grad_eq, flow_enc)
+    grad_eq = step(grad_eq, flow_enc)
+    grad_eq, sent = step((grad_eq, sent), flow_dattn, flow_effn)
     onehot = (flat_inputs[:, None] == columns[None, :]).astype(jnp.bfloat16)
-    vocab_grad = head_grad + dot_tn(onehot, sent)
-
-    grad_two, gain_efinal = norm_back(enc_two, gain_rows[2], grad_encoded)
-    grad_one, gain_effn, grad_in, grad_out = feed_back(
-        enc_one, gain_rows[1], weights[3], weights[4], enc_ffn, grad_two
-    )
-    shard_effn = own_shards(jnp.concatenate([grad_in, grad_out], axis=1))
-    grad_one = grad_one + grad_two
-    grad_eo, grad_query, grad_pair = attention_back(
-        enc_mix[:, :D], enc_keys, None, enc_mixed, enc_total, weights[2], grad_one
-    )
-    grad_mix = jnp.concatenate([grad_query, grad_pair], axis=1)
-    grad_eqkv = low(dot_tn(enc_normed, grad_mix))
-    grad_zero, gain_eattn = norm_back(enc_zero, gain_rows[0], dot_nt(grad_mix, weights[1]))
+    looked_grad = dot_tn(onehot, sent)
+    grad_eq, looked_grad = step((grad_eq, looked_grad), flow_enc)
+    grad_eq = step(grad_eq, flow_dattn, flow_effn)
+    grad_emix = jnp.concatenate([grad_eq, flow_enc.drain()], axis=1)
+    grad_zero, gain_eattn = norm_back(enc_zero, gain_rows[0], dot_nt(grad_emix, weights[1]))
     grad_zero = grad_zero + grad_one
-    grad_patch = low(dot_tn(patches, low(grad_zero)))
-    grad_tables = dot_tn(low(grad_zero), picked)
+    low_zero = low(grad_zero)
     gains = [gain_eattn, gain_effn, gain_efinal, gain_self, gain_cross, gain_dffn, gain_final]
-    grad_small = low(
-        jnp.concatenate(
-            [grad_tables, jnp.stack(gains + [jnp.sum(grad_zero, axis=0)], axis=1)], axis=1
+    width = -(-SMALL_ROWS // BW) * BW
+    gains = jnp.pad(jnp.stack(gains, axis=1), ((0, 0), (2 * POS, width - 2 * POS - 7)))
+    marks = (jnp.arange(width) == SMALL_ROWS - 1).astype(jnp.bfloat16)
+    small_factor = marks[None, :] + jnp.pad(picked, ((0, 0), (0, width - 2 * POS)))
+    flow_eattn = Flow(
+        scatter_flow(
+            [
+                (patches, low_zero),
+                (enc_normed, grad_emix),
+                (enc_mixed, low_eone),
+                (low_zero, small_factor),
+            ],
+            (5 * D, gains),
         )
     )
-    filler = jnp.zeros((D, -SMALL_ROWS % BW), jnp.bfloat16)
-    shard_eattn = own_shards(
-        jnp.concatenate([grad_patch, grad_eqkv, grad_eo, grad_small, filler], axis=1)
-    )
+    looked_grad = step(looked_grad, flow_eattn)
+    head_grad = ring.drain()[:, :vocab_rows].T
+    vocab_grad = head_grad + looked_grad
+    vocab_square = jnp.sum(vocab_grad * vocab_grad)
+    vocab_square = step(vocab_square, flow_eattn)
+    vocab_square = step(vocab_square, flow_dattn, flow_effn)
+    vocab_square = step(vocab_square, flow_eattn)
+    shard_dffn, shard_dattn = flow_dffn.drain(), flow_dattn.drain()
+    shard_effn, shard_eattn = flow_effn.drain(), flow_eattn.drain()
 
     projection = shard_eattn[:, : 5 * D]
     small_shard = shard_eattn[:, 5 * D : 5 * D + SMALL_ROWS].astype(jnp.float32)
     grads = jnp.concatenate([projection, shard_effn, shard_dattn, shard_dffn], axis=1)
     partial_square = (
         jnp.sum(jnp.square(grads.astype(jnp.float32)))
-        + jnp.sum(vocab_grad * vocab_grad)
+        + vocab_square
         + jnp.sum(small_shard * small_shard)
     )
     scalars = jnp.where(
@@ -728,15 +933,16 @@
         partial_square,
         jnp.where(jnp.arange(SMALL_ROWS)[None, :] == 1, loss_local, 0.0),
     )
-    shared = lax.all_gather(
-        jnp.concatenate([small_shard, scalars], axis=0), BOTH, axis=0
-    )
+    slotted = grads.reshape(piece, BLOCKS, BW).transpose(1, 0, 2).reshape(BLOCKS, piece * BW)
+    slotted = low(dot_tn(block_of_slot, slotted)).reshape(devices, own_count, piece, BW)
+    small_shard, scalars, slotted = tie(small_shard, scalars, slotted)
+    slab = lax.all_to_all(slotted, BOTH, 0, 0).transpose(1, 0, 2, 3).reshape(own_count, D, BW)
+    shared = from_narrow(jnp.concatenate([small_shard, scalars], axis=0))
+    shared = join_wide(shared.reshape((1,) * wide_bits() + shared.shape), split_orders()[0] + [0])
+    shared = shared.reshape(devices, piece + 1, SMALL_ROWS)
     small_grad = shared[:, :piece].reshape(D, SMALL_ROWS).T
     total_square = jnp.sum(shared[:, piece, 0])
     loss_sum = jnp.sum(shared[:, piece, 1])
-    slotted = grads.reshape(piece, BLOCKS, BW).transpose(1, 0, 2).reshape(BLOCKS, piece * BW)
-    slotted = low(dot_tn(block_of_slot, slotted)).reshape(devices, own_count, piece, BW)
-    slab = lax.all_to_all(slotted, BOTH, 0, 0).transpose(1, 0, 2, 3).reshape(own_count, D, BW)
 
     grad_norm = jnp.sqrt(total_square)
     factor = jnp.minimum(1.0, clip_limit / (grad_norm + 1e-06))

time: 1820 us -> 1530 us (0.84)
  waiting for transfers between devices: 783 us -> 438 us
  blocking collectives: 152 us -> 57.7 us
  starting transfers between devices: 94.2 us -> 165 us
  other arithmetic: 124 us -> 157 us
  local copies, waits for them, and re-layouts: 139 us -> 170 us
    reduce_scatter x3 -> x0, waiting for transfers between devices: 369 us -> none  [own_shards(): return lax.psum_scatter(columns, BOTH, scatter_dimension=0, tiled=True)]
    ppermute x33 -> x52, waiting for transfers between devices: 238 us -> 131 us  [swap(): return lax.ppermute(values, 'wide', [(w, w ^ bit) for w in range(count)])]
    all_to_all x2 -> x0, blocking collectives: 105 us -> none  [the longest x1 67.6 us: shards(): lax.all_to_all(sent, 'narrow', 0, 0)]
    all_to_all x2 -> x7, waiting for transfers between devices: 3.1 us -> 95.8 us  [the longest x1 50 us: shards(): lax.all_to_all(sent, 'narrow', 0, 0)]
    ppermute x6 -> x24, waiting for transfers between devices: 112 us -> 195 us  [shift(): lax.ppermute(values, 'narrow', [(i, (i + step) % count) for i in range(co...]
    all_to_all x2 -> x7, starting transfers between devices: 7.6 us -> 48.8 us  [the longest x2 15.2 us: delivered(): lax.all_to_all(found.reshape(narrow_count, dec_rows, features), 'narrow',...]
    all_to_all x1, waiting for transfers between devices: 32.3 us -> 0.01 us  [shards(): lax.all_to_all(slotted, BOTH, 0, 0).transpose(1, 0, 2, 3)]
    convert_element_type x18 -> x50, other arithmetic: 28.9 us -> 58.4 us  [low(): return values.astype(jnp.bfloat16)]
  transfers between devices with their start and end apart: 53 -> 90, of which waited for: 29 -> 38; matrix products, arithmetic and copies ran while one was open for 22% -> 31% of each run, Pallas kernels for 5% -> 9%
where the time goes in v2:
time: 1530 us
  waiting for transfers between devices  438 us (29%)
  matrix products  292 us (19%)
  Pallas kernels  221 us (14%)
  local copies, waits for them, and re-layouts  170 us (11%)
  starting transfers between devices  165 us (11%)
  other arithmetic  157 us (10%)
  blocking collectives  57.7 us (4%)
  between operations  25.2 us (2%)
    ppermute x24, waiting for transfers between devices, shift(): lax.ppermute(values, 'narrow', [(i, (i + step) % count) for i in range(co...  195 us
    dot_general x17, matrix products, dot_nn(): lax.dot_general(left, right, (((1,), (0,)), ((), ())), preferred_element_...  132 us
    ppermute x52, waiting for transfers between devices, swap(): return lax.ppermute(values, 'wide', [(w, w ^ bit) for w in range(count)])  131 us
    dot_general x28, matrix products, dot_tn(): lax.dot_general(left, right, (((0,), (0,)), ((), ())), preferred_element_...  96.6 us
    pallas_call x3, Pallas kernels, attend_back(): pl.pallas_call(lambda *refs: attend_back_kernel(positions is not None, ke...  76.4 us
    pallas_call x1, Pallas kernels, head_forward(): pl.pallas_call(lambda *refs: head_kernel(vocab, tile, parts, *refs), grid...  68 us
    unnamed x526, local copies, waits for them, and re-layouts  61.5 us
    convert_element_type x50, other arithmetic, low(): return values.astype(jnp.bfloat16)  58.4 us
  transfers between devices with their start and end apart: 90, of which 38 were waited for; matrix products, arithmetic and copies ran while one was open for 31% of the time, Pallas kernels for 9%

profile of v2, /device:TPU:0, one launch (start us, length us, event | category | flops | bytes accessed | tf_op | source)
XLA Modules:
  0.0 1526.3 jit_solution(17191037381214047000)
XLA Ops:
  19.2 14.0 all-gather.2
  33.8 22.1 %all_gather.30 = s32[8,2,256]{2,1,0:T(2,128)S(1)} all-gather(s32[1,2,256]{2,1,0:T(2,128)S(1)} %slice.353), channel_id=1, replica_groups=mesh['wide'=8,'narrow'=4] {'wide'}, dimensions={0}, use_global_device_ids=true | all-gather | bytes 18432 | tf_op jit(solution)/shard_map/all_gather | solution.py:653
  83.4 41.5 %fusion.7 = bf16[8192,192]{0,1:T(8,128)(2,1)S(1)} fusion(s32[8192]{0:T(1024)S(1)} %bitcast.449, f32[6288,192]{0,1:T(8,128)} %param.33), kind=kOutput, calls=%fused_computation.11 | convolution fusion | flops 19834630144 | bytes 8007680 | tf_op jit(solution)/shard_map/dot_general | solution.py:21
  147.0 15.7 %all-gather.9.cloned.1.call-done = bf16[768,3072]{1,0:T(8,128)(2,1)} async-done(((bf16[24,3072]{1,0:T(8,128)(2,1)}), bf16[768,3072]{1,0:T(8,128)(2,1)}) %all-gather.9.cloned.1.call-update) | async-done | bytes 4718608 | tf_op jit(solution)/shard_map/all_gather | solution.py:685
  188.9 39.3 %fusion.6 = bf16[8192,192]{0,1:T(8,128)(2,1)S(1)} fusion(s32[8192]{0:T(1024)S(1)} %bitcast.451, f32[6288,192]{0,1:T(8,128)S(1)} %bitcast.326), kind=kOutput, calls=%fused_computation.10 | convolution fusion | flops 19834630144 | bytes 8007680 | tf_op jit(solution)/shard_map/dot_general | solution.py:21
  232.0 30.9 %collective-permute-done.9 = bf16[2,1,1,4,24,3456]{5,4,3,2,1,0:T(8,128)(2,1)S(1)} collective-permute-done((bf16[2,1,1,4,24,3456]{5,4,3,2,1,0:T(8,128)(2,1)S(1)}, bf16[2,1,1,4,24,3456]{5,4,3,2,1,0:T(8,128)(2,1)S(1)}, u32[]{:S(2)}, u32[]{:S(2)}) %collective-permute-start.9) | collective-permute-done | bytes 1327136 | tf_op jit(solution)/shard_map/ppermute | solution.py:356
  292.1 21.7 %shard_map.307 = (bf16[512,768]{1,0:T(8,128)(2,1)}, f32[512,768]{1,0:T(8,128)}) custom-call(bf16[512,768]{1,0:T(8,128)(2,1)} %slice.466.refs_0_, bf16[2048,1536]{1,0:T(8,128)(2,1)} %constant_dynamic-update-slice_fusion.refs_1_.refs_2_, bf16[2048,1536]{1,0:T(8,128)(2,1)} %constant_dynamic-update-slice_fusion.refs_1_.refs_2_), custom_call_target="tpu_custom_call" | custom-call | flops 12884901888 | bytes 9437184 | tf_op jit(solution)/shard_map/pallas_call | solution.py:75
  349.1 18.8 %all-to-all-done.3 = bf16[8,1024,192]{1,2,0:T(8,128)(2,1)} async-done(((bf16[8,1024,192]{1,2,0:T(8,128)(2,1)}), bf16[8,1024,192]{1,2,0:T(8,128)(2,1)}, u32[]{:S(2)}, u32[]{:S(2)}) %all-to-all-start.3) | async-done | bytes 3145760 | tf_op jit(solution)/shard_map/all_to_all | solution.py:736
  384.0 15.5 %all-to-all-done.2 = bf16[4,256,192]{1,2,0:T(8,128)(2,1)S(1)} async-done(((bf16[4,256,192]{1,2,0:T(8,128)(2,1)}), bf16[4,256,192]{1,2,0:T(8,128)(2,1)S(1)}, u32[]{:S(2)}, u32[]{:S(2)}) %all-to-all-start.2) | async-done | bytes 393248 | tf_op jit(solution)/shard_map/all_to_all | solution.py:702
  472.6 51.3 %collective-permute-done.17.refs_4_ = bf16[192,6400]{1,0:T(8,128)(2,1)} collective-permute-done((bf16[192,6400]{1,0:T(8,128)(2,1)}, bf16[192,6400]{1,0:T(8,128)(2,1)}, u32[]{:S(2)}, u32[]{:S(2)}) %collective-permute-start.17) | collective-permute-done | bytes 2457632 | tf_op jit(solution)/shard_map/ppermute | solution.py:361
  587.0 30.2 %collective-permute-done.24.refs_5_ = bf16[192,6400]{1,0:T(8,128)(2,1)} collective-permute-done((bf16[192,6400]{1,0:T(8,128)(2,1)}, bf16[192,6400]{1,0:T(8,128)(2,1)}, u32[]{:S(2)}, u32[]{:S(2)}) %collective-permute-start.24) | collective-permute-done | bytes 2457632 | tf_op jit(solution)/shard_map/ppermute | solution.py:361
  617.2 68.0 %shard_map.310 = (f32[2048,768]{1,0:T(8,128)}, bf16[2048,6400]{1,0:T(8,128)(2,1)}, f32[2048,128]{1,0:T(8,128)}) custom-call(s32[8]{0:T(128)} %convert_element_type.664.refs_0_, bf16[2048,768]{1,0:T(8,128)(2,1)} %pad_maximum_fusion.6.refs_1_, bf16[192,6400]{1,0:T(8,128)(2,1)} %pad.27.refs_2_, bf16[192,6400]{1,0:T(8,128)(2,1)} %collective-permute-done.12.refs_3_, ...), custom_call_target="tpu_custom_call" | custom-call | flops 40265318400 | bytes 36044800 | tf_op jit(solution)/shard_map/pallas_call | solution.py:231
  710.0 32.4 %shard_map.311 = bf16[768,6400]{1,0:T(8,128)(2,1)} custom-call(s32[8]{0:T(128)} %convert_element_type.664.refs_0_, bf16[2048,768]{1,0:T(8,128)(2,1)} %pad_maximum_fusion.6.refs_1_, bf16[2048,6400]{1,0:T(8,128)(2,1)} %get-tuple-element.340.refs_2_, f32[2048,128]{1,0:T(8,128)} %maximum_maximum_fusion.refs_3_), custom_call_target="tpu_custom_call" | custom-call | flops 20132659200 | bytes 36044800 | tf_op jit(solution)/shard_map/pallas_call | solution.py:290
  781.0 23.4 %shard_map.312 = (bf16[256,768]{1,0:T(8,128)(2,1)}, bf16[2048,768]{1,0:T(8,128)(2,1)}, bf16[2048,768]{1,0:T(8,128)(2,1)}) custom-call(bf16[256,768]{1,0:T(8,128)(2,1)} %convolution_convert_fusion.20.refs_0_, bf16[2048,1536]{1,0:T(8,128)(2,1)} %constant_dynamic-update-slice_fusion.4.refs_1_.refs_2_, ...), custom_call_target="tpu_custom_call" | custom-call | flops 16106127360 | bytes 14942208 | tf_op jit(solution)/shard_map/pallas_call | solution.py:159
  830.1 14.1 shard_map.313
  861.8 19.0 %collective-permute-done.32 = bf16[192,6400]{1,0:T(8,128)(2,1)} collective-permute-done((bf16[192,6400]{1,0:T(8,128)(2,1)}, bf16[192,6400]{1,0:T(8,128)(2,1)}, u32[]{:S(2)}, u32[]{:S(2)}) %collective-permute-start.32) | collective-permute-done | bytes 2457632 | tf_op jit(solution)/shard_map/ppermute | solution.py:361
  983.4 50.0 %all-to-all-done.6 = bf16[4,256,192]{1,2,0:T(8,128)(2,1)} async-done(((bf16[4,256,192]{1,2,0:T(8,128)(2,1)}), bf16[4,256,192]{1,2,0:T(8,128)(2,1)}, u32[]{:S(2)}, u32[]{:S(2)}) %all-to-all-start.6) | async-done | bytes 393248 | tf_op jit(solution)/shard_map/all_to_all | solution.py:861
  1063.8 38.9 %shard_map.314 = (bf16[512,768]{1,0:T(8,128)(2,1)}, bf16[2048,768]{1,0:T(8,128)(2,1)}, bf16[2048,768]{1,0:T(8,128)(2,1)}) custom-call(bf16[512,768]{1,0:T(8,128)(2,1)} %slice.466.refs_0_, bf16[2048,1536]{1,0:T(8,128)(2,1)} %constant_dynamic-update-slice_fusion.refs_1_.refs_2_, bf16[2048,1536]{1,0:T(8,128)(2,1)} %constant_dynamic-update-slice_fusion.refs_1_.refs_2_, ...), custom_call_target="tpu_custom_call" | custom-call | flops 32212254720 | bytes 17301504 | tf_op jit(solution)/shard_map/pallas_call | solution.py:159
  1140.3 23.9 %collective-permute-done.50 = bf16[2,1,96,3072]{3,2,1,0:T(8,128)(2,1)} collective-permute-done((bf16[2,1,96,3072]{3,2,1,0:T(8,128)(2,1)}, bf16[2,1,96,3072]{3,2,1,0:T(8,128)(2,1)}, u32[]{:S(2)}, u32[]{:S(2)}) %collective-permute-start.50) | collective-permute-done | bytes 1179680 | tf_op jit(solution)/shard_map/ppermute | solution.py:356
  1188.8 52.0 %fusion = f32[6288,192]{0,1:T(8,128)} fusion(bf16[8192,192]{0,1:T(8,128)(2,1)S(1)} %copy-done.230, s32[8192]{0:T(1024)S(1)} %bitcast.450), kind=kOutput, calls=%fused_computation.2 | convolution fusion | flops 19831848960 | bytes 8007680 | tf_op jit(solution)/shard_map/dot_general | solution.py:27
  1267.9 52.4 %collective-permute-done.45 = bf16[192,6400]{1,0:T(8,128)(2,1)S(1)} collective-permute-done((bf16[192,6400]{1,0:T(8,128)(2,1)S(1)}, bf16[192,6400]{1,0:T(8,128)(2,1)S(1)}, u32[]{:S(2)}, u32[]{:S(2)}) %collective-permute-start.45) | collective-permute-done | bytes 2457632 | tf_op jit(solution)/shard_map/ppermute | solution.py:361
  1345.6 17.0 %collective-permute-done.63 = bf16[24,6144]{1,0:T(8,128)(2,1)S(1)} collective-permute-done((bf16[24,6144]{1,0:T(8,128)(2,1)S(1)}, bf16[24,6144]{1,0:T(8,128)(2,1)S(1)}, u32[]{:S(2)}, u32[]{:S(2)}) %collective-permute-start.63) | collective-permute-done | bytes 294944 | tf_op jit(solution)/shard_map/ppermute | solution.py:361
  1376.9 13.8 collective-permute-start.69
  1474.8 15.3 %fusion.191 = (bf16[6288,192]{0,1:T(8,128)(2,1)}, f32[6288,192]{0,1:T(8,128)}, f32[6288,192]{0,1:T(8,128)}, f32[6288,192]{0,1:T(8,128)}) fusion(f32[6288,192]{0,1:T(8,128)} %param.33, f32[]{:T(128)S(6)} %sub.129, f32[]{:T(128)S(6)} %sub.128, f32[]{:T(128)S(6)} %min.3, f32[6288,192]{0,1:T(8,128)} %fusion, bf16[192,6400]{1,0:T(8,128)(2,1)} %copy-done.20, ...), kind=kLoop, calls=%fused_computation.525 | loop fusion | flops 25353216 | bytes 41048076 | tf_op jit(solution)/shard_map/convert_element_type | solution.py:978
  (1036 shorter events, 779.9 us)
Async XLA Ops:
  10.4 59.3 %all-to-all-start = ((bf16[32,6,24,128]{3,2,1,0:T(8,128)(2,1)}), bf16[32,6,24,128]{3,2,1,0:T(8,128)(2,1)S(1)}, u32[]{:S(2)}, u32[]{:S(2)}) async-start(bf16[32,6,24,128]{3,2,1,0:T(8,128)(2,1)} %bitcast.315), calls=%async_computation | async-start | bytes 2359296 | tf_op jit(solution)/shard_map/all_to_all | solution.py:641
  17.7 145.1 %all-gather.9.cloned.1.call-start = ((), (), s32[]{:S(2)}) async-start(), calls=%async_computation.8 | async-start | bytes 4866048 | tf_op jit(solution)/shard_map/all_gather | solution.py:685
  71.7 330.9 %all-gather.11.cloned.1.call-start = ((), (), s32[]{:S(2)}) async-start(), calls=%async_computation.9 | async-start | bytes 8515584 | tf_op jit(solution)/shard_map/all_gather | solution.py:685
  83.4 458.9 %all-gather.13.cloned.1.call-start = ((), (), s32[]{:S(2)}) async-start(), calls=%async_computation.10 | async-start | bytes 10948608 | tf_op jit(solution)/shard_map/all_gather | solution.py:685
  175.3 87.6 %collective-permute-start.7 = (bf16[512,1536]{1,0:T(8,128)(2,1)S(1)}, bf16[512,1536]{1,0:T(8,128)(2,1)S(1)}, u32[]{:S(2)}, u32[]{:S(2)}) collective-permute-start(bf16[512,1536]{1,0:T(8,128)(2,1)S(1)} %slice.468), channel_id=1, source_target_pairs={{0,8},{4,12},{8,0},{12,4},{16,24},{20,28},{24,16},{28,20},{1,9},{5... | collective-permute-start | bytes 4718600 | tf_op jit(solution)/shard_map/ppermute | solution.py:356
  188.9 74.0 %collective-permute-start.9 = (bf16[2,1,1,4,24,3456]{5,4,3,2,1,0:T(8,128)(2,1)S(1)}, bf16[2,1,1,4,24,3456]{5,4,3,2,1,0:T(8,128)(2,1)S(1)}, u32[]{:S(2)}, u32[]{:S(2)}) collective-permute-start(bf16[2,1,1,4,24,3456]{5,4,3,2,1,0:T(8,128)(2,1)S(1)} %maximum_select_fusion.7), channel_id=1, source_target_pairs={{0,8},{4,12},{8,0},{12,4},{16,24},{20,28},{24,16},{28,20},{1,9},{5... | collective-permute-start | bytes 3981320 | tf_op jit(solution)/shard_map/ppermute | solution.py:356
  277.0 107.0 %collective-permute-start.12 = (bf16[192,6400]{1,0:T(8,128)(2,1)}, bf16[192,6400]{1,0:T(8,128)(2,1)}, u32[]{:S(2)}, u32[]{:S(2)}) collective-permute-start(bf16[192,6400]{1,0:T(8,128)(2,1)} %pad.27.refs_2_), channel_id=1, source_target_pairs={{0,3},{1,0},{2,1},{3,2},{4,7},{5,4},{6,5},{7,6},{8,11},{9,8},{10,9... | collective-permute-start | bytes 7372808 | tf_op jit(solution)/shard_map/ppermute | solution.py:361
  815.1 65.7 %collective-permute-start.32 = (bf16[192,6400]{1,0:T(8,128)(2,1)}, bf16[192,6400]{1,0:T(8,128)(2,1)}, u32[]{:S(2)}, u32[]{:S(2)}) collective-permute-start(bf16[192,6400]{1,0:T(8,128)(2,1)} %get-tuple-element.375), channel_id=1, source_target_pairs={{0,1},{1,2},{2,3},{3,0},{4,5},{5,6},{6,7},{7,4},{8,9},{9,10},{10,1... | collective-permute-start | bytes 7372808 | tf_op jit(solution)/shard_map/ppermute | solution.py:361
  946.2 88.9 %collective-permute-start.39 = (bf16[384,6144]{1,0:T(8,128)(2,1)}, bf16[384,6144]{1,0:T(8,128)(2,1)}, u32[]{:S(2)}, u32[]{:S(2)}) collective-permute-start(bf16[384,6144]{1,0:T(8,128)(2,1)} %fusion.61), channel_id=1, source_target_pairs={{0,4},{4,0},{8,12},{12,8},{16,20},{20,16},{24,28},{28,24},{1,5},{5... | collective-permute-start | bytes 14155784 | tf_op jit(solution)/shard_map/ppermute | solution.py:356
  946.2 89.2 %collective-permute-start.40 = (bf16[384,6144]{1,0:T(8,128)(2,1)}, bf16[384,6144]{1,0:T(8,128)(2,1)}, u32[]{:S(2)}, u32[]{:S(2)}) collective-permute-start(bf16[384,6144]{1,0:T(8,128)(2,1)} %pad_maximum_fusion.2), channel_id=1, source_target_pairs={{0,4},{4,0},{8,12},{12,8},{16,20},{20,16},{24,28},{28,24},{1,5},{5... | collective-permute-start | bytes 14155784 | tf_op jit(solution)/shard_map/ppermute | solution.py:356
  946.7 112.4 %collective-permute-start.44 = (bf16[192,6400]{1,0:T(8,128)(2,1)}, bf16[192,6400]{1,0:T(8,128)(2,1)}, u32[]{:S(2)}, u32[]{:S(2)}) collective-permute-start(bf16[192,6400]{1,0:T(8,128)(2,1)} %add_convert_fusion.4), channel_id=1, source_target_pairs={{0,1},{1,2},{2,3},{3,0},{4,5},{5,6},{6,7},{7,4},{8,9},{9,10},{10,1... | collective-permute-start | bytes 7372808 | tf_op jit(solution)/shard_map/ppermute | solution.py:361
  953.5 79.9 %all-to-all-start.6 = ((bf16[4,256,192]{1,2,0:T(8,128)(2,1)}), bf16[4,256,192]{1,2,0:T(8,128)(2,1)}, u32[]{:S(2)}, u32[]{:S(2)}) async-start(bf16[4,256,192]{1,2,0:T(8,128)(2,1)} %bitcast.397), calls=%async_computation.6 | async-start | bytes 786432 | tf_op jit(solution)/shard_map/all_to_all | solution.py:861
  967.2 197.1 %all-gather.15.cloned.1.call-start = ((), (), s32[]{:S(2)}) async-start(), calls=%async_computation.11 | async-start | bytes 3538944 | tf_op jit(solution)/shard_map/all_gather | solution.py:862
  967.3 91.8 %collective-permute-start.41 = (bf16[24,6144]{1,0:T(8,128)(2,1)}, bf16[24,6144]{1,0:T(8,128)(2,1)}, u32[]{:S(2)}, u32[]{:S(2)}) collective-permute-start(bf16[24,6144]{1,0:T(8,128)(2,1)} %get-tuple-element.405), channel_id=1, source_target_pairs={{0,1},{1,2},{2,3},{3,0},{4,5},{5,6},{6,7},{7,4},{8,9},{9,10},{10,1... | collective-permute-start | bytes 884744 | tf_op jit(solution)/shard_map/ppermute | solution.py:361
  970.2 88.9 %collective-permute-start.42 = (bf16[24,6144]{1,0:T(8,128)(2,1)}, bf16[24,6144]{1,0:T(8,128)(2,1)}, u32[]{:S(2)}, u32[]{:S(2)}) collective-permute-start(bf16[24,6144]{1,0:T(8,128)(2,1)} %get-tuple-element.406), channel_id=1, source_target_pairs={{0,2},{1,3},{2,0},{3,1},{4,6},{5,7},{6,4},{7,5},{8,10},{9,11},{10,... | collective-permute-start | bytes 884744 | tf_op jit(solution)/shard_map/ppermute | solution.py:361
  1174.0 66.7 %collective-permute-start.53 = (bf16[512,768]{1,0:T(8,128)(2,1)S(1)}, bf16[512,768]{1,0:T(8,128)(2,1)S(1)}, u32[]{:S(2)}, u32[]{:S(2)}) collective-permute-start(bf16[512,768]{1,0:T(8,128)(2,1)S(1)} %slice.509), channel_id=1, source_target_pairs={{0,8},{4,12},{8,0},{12,4},{16,24},{20,28},{24,16},{28,20},{1,9},{5... | collective-permute-start | bytes 2359304 | tf_op jit(solution)/shard_map/ppermute | solution.py:356
  1174.7 66.1 %collective-permute-start.54 = (bf16[1,1,96,3072]{3,2,1,0:T(8,128)(2,1)S(1)}, bf16[1,1,96,3072]{3,2,1,0:T(8,128)(2,1)S(1)}, u32[]{:S(2)}, u32[]{:S(2)}) collective-permute-start(bf16[1,1,96,3072]{3,2,1,0:T(8,128)(2,1)S(1)} %constant_dynamic-slice_fusion.17), channel_id=1, source_target_pairs={{0,16},{4,20},{8,24},{12,28},{16,0},{20,4},{24,8},{28,12},{1,17},{... | collective-permute-start | bytes 1769480 | tf_op jit(solution)/shard_map/ppermute | solution.py:356
  1176.2 64.6 %collective-permute-start.55 = (bf16[1,1,96,3072]{3,2,1,0:T(8,128)(2,1)S(1)}, bf16[1,1,96,3072]{3,2,1,0:T(8,128)(2,1)S(1)}, u32[]{:S(2)}, u32[]{:S(2)}) collective-permute-start(bf16[1,1,96,3072]{3,2,1,0:T(8,128)(2,1)S(1)} %constant_dynamic-slice_fusion.16), channel_id=1, source_target_pairs={{0,8},{4,12},{8,0},{12,4},{16,24},{20,28},{24,16},{28,20},{1,9},{5... | collective-permute-start | bytes 1769480 | tf_op jit(solution)/shard_map/ppermute | solution.py:356
  1177.6 63.2 %collective-permute-start.56 = (bf16[1,1,96,3072]{3,2,1,0:T(8,128)(2,1)S(1)}, bf16[1,1,96,3072]{3,2,1,0:T(8,128)(2,1)S(1)}, u32[]{:S(2)}, u32[]{:S(2)}) collective-permute-start(bf16[1,1,96,3072]{3,2,1,0:T(8,128)(2,1)S(1)} %constant_dynamic-slice_fusion.15), channel_id=1, source_target_pairs={{0,16},{4,20},{8,24},{12,28},{16,0},{20,4},{24,8},{28,12},{1,17},{... | collective-permute-start | bytes 1769480 | tf_op jit(solution)/shard_map/ppermute | solution.py:356
  1260.6 61.9 %collective-permute-start.58 = (bf16[384,4480]{1,0:T(8,128)(2,1)S(1)}, bf16[384,4480]{1,0:T(8,128)(2,1)S(1)}, u32[]{:S(2)}, u32[]{:S(2)}) collective-permute-start(bf16[384,4480]{1,0:T(8,128)(2,1)S(1)} %pad_maximum_fusion.3), channel_id=1, source_target_pairs={{0,4},{4,0},{8,12},{12,8},{16,20},{20,16},{24,28},{28,24},{1,5},{5... | collective-permute-start | bytes 10321928 | tf_op jit(solution)/shard_map/ppermute | solution.py:356
  1262.0 58.3 %collective-permute-start.45 = (bf16[192,6400]{1,0:T(8,128)(2,1)S(1)}, bf16[192,6400]{1,0:T(8,128)(2,1)S(1)}, u32[]{:S(2)}, u32[]{:S(2)}) collective-permute-start(bf16[192,6400]{1,0:T(8,128)(2,1)S(1)} %copy-done.91), channel_id=1, source_target_pairs={{0,1},{1,2},{2,3},{3,0},{4,5},{5,6},{6,7},{7,4},{8,9},{9,10},{10,1... | collective-permute-start | bytes 7372808 | tf_op jit(solution)/shard_map/ppermute | solution.py:361
  1264.0 63.6 %collective-permute-start.59 = (bf16[24,6144]{1,0:T(8,128)(2,1)S(1)}, bf16[24,6144]{1,0:T(8,128)(2,1)S(1)}, u32[]{:S(2)}, u32[]{:S(2)}) collective-permute-start(bf16[24,6144]{1,0:T(8,128)(2,1)S(1)} %copy-done.160), channel_id=1, source_target_pairs={{0,1},{1,2},{2,3},{3,0},{4,5},{5,6},{6,7},{7,4},{8,9},{9,10},{10,1... | collective-permute-start | bytes 884744 | tf_op jit(solution)/shard_map/ppermute | solution.py:361
  1264.0 75.3 %collective-permute-start.60 = (bf16[24,6144]{1,0:T(8,128)(2,1)S(1)}, bf16[24,6144]{1,0:T(8,128)(2,1)S(1)}, u32[]{:S(2)}, u32[]{:S(2)}) collective-permute-start(bf16[24,6144]{1,0:T(8,128)(2,1)S(1)} %copy-done.159), channel_id=1, source_target_pairs={{0,2},{1,3},{2,0},{3,1},{4,6},{5,7},{6,4},{7,5},{8,10},{9,11},{10,... | collective-permute-start | bytes 884744 | tf_op jit(solution)/shard_map/ppermute | solution.py:361
  1266.4 74.4 %collective-permute-start.61 = (bf16[24,6144]{1,0:T(8,128)(2,1)S(1)}, bf16[24,6144]{1,0:T(8,128)(2,1)S(1)}, u32[]{:S(2)}, u32[]{:S(2)}) collective-permute-start(bf16[24,6144]{1,0:T(8,128)(2,1)S(1)} %copy-done.158), channel_id=1, source_target_pairs={{0,3},{1,0},{2,1},{3,2},{4,7},{5,4},{6,5},{7,6},{8,11},{9,8},{10,9... | collective-permute-start | bytes 884744 | tf_op jit(solution)/shard_map/ppermute | solution.py:361
  (315 other events, 5781.5 us)
Sparse Core Ops, SparseCore 0:
  71.8 90.9 all-gather.8
  166.1 99.5 all-gather.10
  269.1 149.1 all-gather.12
  1035.3 29.5 all-gather.14

commit v3 on v2

--- a/solution.py
+++ b/solution.py
@@ -9,6 +9,7 @@
 D = 768
 attn_scale = 0.125
 KERNEL_VMEM = 56 * 1024 * 1024
+SMALL_COST = pl.CostEstimate(flops=1 << 20, bytes_accessed=1 << 20, transcendentals=0)
 
 
 def dot_nt(left, right):
@@ -90,11 +91,7 @@
             jax.ShapeDtypeStruct((rows, D), jnp.float32),
         ],
         compiler_params=pltpu.CompilerParams(vmem_limit_bytes=KERNEL_VMEM),
-        cost_estimate=pl.CostEstimate(
-            flops=16 * rows * keys * D,
-            bytes_accessed=4 * keys * D + 8 * rows * D,
-            transcendentals=rows * keys * 12,
-        ),
+        cost_estimate=SMALL_COST,
     )(*extra, queries, keys_values, keys_values)
 
 
@@ -167,35 +164,15 @@
             jax.ShapeDtypeStruct((keys, D), jnp.bfloat16),
         ],
         compiler_params=pltpu.CompilerParams(vmem_limit_bytes=KERNEL_VMEM),
-        cost_estimate=pl.CostEstimate(
-            flops=40 * rows * keys * D,
-            bytes_accessed=8 * keys * D + 12 * rows * D,
-            transcendentals=rows * keys * 12,
-        ),
+        cost_estimate=SMALL_COST,
     )(*extra, queries, keys_values, keys_values, mixed_rows, log_total, grad_mixed)
 
 
-def head_kernel(vocab, tile, parts, used_ref, rows_ref, *refs):
-    part_refs, refs = refs[:parts], refs[parts:]
-    mixed_ref, exp_ref, stats_ref, logits_ref, table_ref, arrived = refs
+def head_kernel(vocab, tile, used_ref, rows_ref, table_ref, mixed_ref, exp_ref, stats_ref, logits_ref):
     step = pl.program_id(0)
     padded = table_ref.shape[1]
     shape = (rows_ref.shape[0], 128)
     lane = lax.broadcasted_iota(jnp.int32, shape, 1)
-
-    @pl.when(step == 0)
-    def _():
-        height = D // parts
-        copies = [
-            pltpu.make_async_copy(
-                part, table_ref.at[pl.ds(k * height, height), :], arrived.at[k]
-            )
-            for k, part in enumerate(part_refs)
-        ]
-        for copy in copies:
-            copy.start()
-        for copy in copies:
-            copy.wait()
 
     @pl.when(used_ref[step] == 0)
     def _():
@@ -219,32 +196,30 @@
         for start in range(0, padded, tile):
             exponent = jnp.exp(logits_ref[:, start : start + tile] - top)
             summed += jnp.sum(exponent, axis=1, keepdims=True)
-            lowered = exponent.astype(jnp.bfloat16)
-            exp_ref[:, start : start + tile] = lowered
-            mixed += dot_nt(lowered, table_ref[:, start : start + tile])
+            low = exponent.astype(jnp.bfloat16)
+            exp_ref[:, start : start + tile] = low
+            mixed += dot_nt(low, table_ref[:, start : start + tile])
         mixed_ref[...] = mixed
         stats_ref[...] = jnp.where(lane == 0, top, summed)
 
 
-def head_forward(rows_all, table_parts, used, vocab, block_rows, tile):
-    rows, padded, parts = rows_all.shape[0], table_parts[0].shape[1], len(table_parts)
+def head_forward(rows_all, table, used, vocab, block_rows, tile):
+    rows, padded = rows_all.shape[0], table.shape[1]
     return pl.pallas_call(
-        lambda *refs: head_kernel(vocab, tile, parts, *refs),
+        lambda *refs: head_kernel(vocab, tile, *refs),
         grid_spec=pltpu.PrefetchScalarGridSpec(
             num_scalar_prefetch=1,
             grid=(rows // block_rows,),
-            in_specs=[pl.BlockSpec((block_rows, D), lambda i, used: (i, 0))]
-            + [pl.BlockSpec(memory_space=pl.ANY)] * parts,
+            in_specs=[
+                pl.BlockSpec((block_rows, D), lambda i, used: (i, 0)),
+                pl.BlockSpec((D, padded), lambda i, used: (0, 0), pipeline_mode=pl.Buffered(1)),
+            ],
             out_specs=[
                 pl.BlockSpec((block_rows, D), lambda i, used: (i, 0)),
                 pl.BlockSpec((block_rows, padded), lambda i, used: (i, 0)),
                 pl.BlockSpec((block_rows, 128), lambda i, used: (i, 0)),
             ],
-            scratch_shapes=[
-                pltpu.VMEM((block_rows, padded), jnp.float32),
-                pltpu.VMEM((D, padded), jnp.bfloat16),
-                pltpu.SemaphoreType.DMA((parts,)),
-            ],
+            scratch_shapes=[pltpu.VMEM((block_rows, padded), jnp.float32)],
         ),
         out_shape=[
             jax.ShapeDtypeStruct((rows, D), jnp.float32),
@@ -252,12 +227,8 @@
             jax.ShapeDtypeStruct((rows, 128), jnp.float32),
         ],
         compiler_params=pltpu.CompilerParams(vmem_limit_bytes=KERNEL_VMEM),
-        cost_estimate=pl.CostEstimate(
-            flops=4 * rows * padded * D,
-            bytes_accessed=2 * rows * padded + 2 * padded * D,
-            transcendentals=rows * padded,
-        ),
-    )(used, rows_all, *table_parts)
+        cost_estimate=SMALL_COST,
+    )(used, rows_all, table)
 
 
 def table_grad_kernel(tile, used_ref, rows_ref, exp_ref, info_ref, grad_ref, total_ref):
@@ -302,11 +273,7 @@
         ),
         out_shape=jax.ShapeDtypeStruct((D, padded), jnp.bfloat16),
         compiler_params=pltpu.CompilerParams(vmem_limit_bytes=KERNEL_VMEM),
-        cost_estimate=pl.CostEstimate(
-            flops=2 * rows * padded * D,
-            bytes_accessed=2 * rows * padded + 2 * padded * D,
-            transcendentals=0,
-        ),
+        cost_estimate=SMALL_COST,
     )(used, rows_all, exps, info)
 
 
@@ -650,23 +617,14 @@
     )
     rows_ids, cols_ids = whole_ids[:enc_rows], whole_ids[enc_rows : 2 * enc_rows]
     token_ids = whole_ids[2 * enc_rows :].reshape(2, dec_rows)
-    layer_tokens = lax.all_gather(token_ids, "wide", axis=0)
+    every_token = from_narrow(token_ids)
+    every_token = every_token.reshape((1,) * wide_bits() + every_token.shape)
+    every_token = join_wide(every_token, split_orders()[0] + [0])
+    every_token = every_token.reshape(wide_count, narrow_count, 2, dec_rows)
+    pieces, patches, every_token = tie(pieces, patches, every_token)
+    layer_tokens = lax.dynamic_index_in_dim(every_token, narrow_pos, 1, keepdims=False)
     layer_targets = layer_tokens[:, 1].reshape(-1)
-    every_input = lax.all_gather(layer_tokens, "narrow", axis=1)
-    screens_info = lax.all_gather(
-        jnp.concatenate([target_lengths[:, None], loss_mask], axis=1), "wide", axis=0, tiled=True
-    )
-    pieces, patches, every_input, screens_info = tie(pieces, patches, every_input, screens_info)
     patches = lax.ppermute(patches, BOTH, exchange)
-    counted = (
-        (jnp.arange(TGT)[None, :] < screens_info[:, :1]) & (screens_info[:, 1:] == 1)
-    ).astype(jnp.float32)
-    tokens_counted = jnp.maximum(jnp.sum(counted), 1.0)
-    row_counted = lax.dynamic_index_in_dim(
-        counted.reshape(screen_sets, narrow_count, TGT), narrow_pos, 1, keepdims=False
-    ).reshape(-1)
-    own_counted = lax.dynamic_slice_in_dim(row_counted, wide_pos * dec_rows, dec_rows)
-
     ordered = low(dot_nn(block_of_slot, pieces.reshape(slot_total, piece * BW)))
     row_shard = ordered.reshape(BLOCKS, piece, BW).transpose(1, 0, 2).reshape(piece, BLOCKS * BW)
     weights = [None] * len(EXTENTS)
@@ -689,8 +647,8 @@
     table_low = low(vocab_table)
     columns = jnp.arange(vocab_rows)
     vocab_start = wide_pos * vocab_rows
-    flat_inputs = every_input[:, :, 0].reshape(-1) - vocab_start
-    flat_targets = every_input[:, :, 1].reshape(-1) - vocab_start
+    flat_inputs = every_token[:, :, 0].reshape(-1) - vocab_start
+    flat_targets = every_token[:, :, 1].reshape(-1) - vocab_start
 
     def looked_up(ids):
         onehot = (ids[:, None] == columns[None, :]).astype(jnp.bfloat16)
@@ -730,16 +688,33 @@
     enc_mix = low(dot_nn(enc_normed, weights[1]))
     enc_query = enc_mix[:, :D]
     flow_keys = Flow(keys_flow(enc_mix[:, D:]))
-    enc_query, flat_targets = step((enc_query, flat_targets), flow_keys, flow_table)
+    enc_query, flat_targets, found_inputs = step(
+        (enc_query, flat_targets, found_inputs), flow_keys, flow_table
+    )
     found_targets = looked_up(flat_targets)
-    enc_query, found_targets = step((enc_query, found_targets), flow_keys, flow_weights)
+    dec_zero = delivered(found_inputs)
+    enc_query, found_targets, dec_zero = step(
+        (enc_query, found_targets, dec_zero), flow_keys, flow_weights, flow_table
+    )
     found_targets = lax.all_to_all(found_targets, "wide", 0, 0)
     enc_query = step(enc_query, flow_keys)
     enc_keys = flow_keys.drain()
     enc_mixed, enc_total = attend(enc_query, enc_keys, None)
-    enc_mixed, found_inputs = step((enc_mixed, found_inputs), flow_weights)
+    enc_mixed = step(enc_mixed, flow_weights)
     take(PERMUTED, flow_weights.drain())
-    dec_zero = delivered(found_inputs)
+    enc_mixed, target_lengths, loss_mask = tie(enc_mixed, target_lengths, loss_mask)
+    screens_info = lax.all_gather(
+        jnp.concatenate([target_lengths[:, None], loss_mask], axis=1), "wide", axis=0, tiled=True
+    )
+    counted = (
+        (jnp.arange(TGT)[None, :] < screens_info[:, :1]) & (screens_info[:, 1:] == 1)
+    ).astype(jnp.float32)
+    tokens_counted = jnp.maximum(jnp.sum(counted), 1.0)
+    row_counted = lax.dynamic_index_in_dim(
+        counted.reshape(screen_sets, narrow_count, TGT), narrow_pos, 1, keepdims=False
+    ).reshape(-1)
+    own_counted = lax.dynamic_slice_in_dim(row_counted, wide_pos * dec_rows, dec_rows)
+
     enc_one = enc_zero + dot_nn(enc_mixed, weights[2])
     enc_fnormed = low(rms_norm(enc_one, gain_rows[1]))
     enc_gate = dot_nn(enc_fnormed, weights[3])
@@ -768,14 +743,14 @@
     cross_normed = low(rms_norm(dec_one, gain_rows[4]))
     cross_query = low(dot_nn(cross_normed, weights[7]))
     cross_query, target_rows = step((cross_query, target_rows), flow_cross)
-    cross_query = step(cross_query, flow_cross, flow_table)
+    cross_query = step(cross_query, flow_cross)
     cross_keys = flow_cross.drain()
     cross_mixed, cross_total = attend(cross_query, cross_keys, None)
     dec_two = dec_one + dot_nn(cross_mixed, weights[9])
     branch, dec_ffn = feed_forward(dec_two, gain_rows[5], weights[10], weights[11])
     dec_three = dec_two + branch
     final = low(rms_norm(dec_three, gain_rows[6]) * D ** (-0.5))
-    table_parts = flow_table.drain()
+    table = jnp.concatenate(flow_table.drain(), axis=0)
 
     rotated = lax.dynamic_slice_in_dim(
         jnp.concatenate([final, final], axis=1), narrow_pos * features, D, axis=1
@@ -785,9 +760,7 @@
     block_rows = 256
     used = jnp.any(row_counted.reshape(-1, block_rows) != 0, axis=1).astype(jnp.int32)
     tile = padded // 5 if padded % 640 == 0 else 256
-    mixed, exps, stats = head_forward(
-        rows_all, table_parts, used, vocab_rows, block_rows, tile
-    )
+    mixed, exps, stats = head_forward(rows_all, table, used, vocab_rows, block_rows, tile)
     top_part, summed_part = stats[:, 0], stats[:, 1]
     stats_all = lax.all_gather(jnp.stack([top_part, summed_part]), "wide", axis=0)
     top_logit = jnp.max(stats_all[:, 0], axis=0)
@@ -834,7 +807,7 @@
         cross_query, cross_keys, None, cross_mixed, cross_total, grad_mixed
     )
     flow_cross = Flow(return_flow([grad_key, grad_value]))
-    grad_cq = step(grad_cq, flow_cross)
+    grad_cq = step(grad_cq, flow_cross, ring)
     grad_one, gain_cross = norm_back(dec_one, gain_rows[4], dot_nt(grad_cq, weights[7]))
     grad_one = grad_one + grad_two
     low_one = low(grad_one)
@@ -845,8 +818,8 @@
     )
     flow_self = Flow(return_flow([grad_key, grad_value]))
     grad_sq = step(grad_sq, flow_self, flow_dffn)
-    grad_sq = step(grad_sq, flow_self, ring)
-    grad_sq = step(grad_sq, flow_cross)
+    grad_sq = step(grad_sq, flow_self)
+    grad_sq = step(grad_sq, flow_cross, ring)
     grad_ckv = flow_cross.drain()
 
     grad_two, gain_efinal = norm_back(enc_two, gain_rows[2], dot_nt(grad_ckv, weights[8]))
@@ -859,7 +832,6 @@
     grad_tokens = low(grad_zero + grad_one)
     sent = grad_tokens.reshape(dec_rows, narrow_count, features).transpose(1, 0, 2)
     sent = lax.all_to_all(sent, "narrow", 0, 0).reshape(narrow_count * dec_rows, features)
-    sent = lax.all_gather(sent, "wide", axis=0, tiled=True)
     flow_dattn = Flow(
         scatter_flow(
             [
@@ -872,13 +844,14 @@
         )
     )
     flow_effn = Flow(scatter_flow([(enc_ffn[0], grad_gate), (low_etwo, enc_ffn[2])]))
-    grad_gate = step(grad_gate, flow_dattn, flow_effn)
+    grad_gate = step(grad_gate, flow_dattn, flow_effn, ring)
     grad_one, gain_effn = norm_back(enc_one, gain_rows[1], dot_nt(grad_gate, weights[3]))
     grad_one = grad_one + grad_two
     low_eone = low(grad_one)
     grad_mixed = low(dot_nt(low_eone, weights[2]))
     grad_mixed = step(grad_mixed, flow_dattn, flow_effn)
-    grad_mixed = step(grad_mixed, flow_dffn, ring)
+    grad_mixed, sent = step((grad_mixed, sent), flow_dffn)
+    sent = lax.all_gather(sent, "wide", axis=0, tiled=True)
     grad_eq, grad_key, grad_value = attend_back(
         enc_mix[:, :D], enc_keys, None, enc_mixed, enc_total, grad_mixed
     )

time: 1530 us -> 1430 us (0.935)
  waiting for transfers between devices: 438 us -> 335 us
  blocking collectives: 57.7 us -> 17.6 us
  starting transfers between devices: 165 us -> 199 us
  Pallas kernels: 221 us -> 203 us
  local copies, waits for them, and re-layouts: 170 us -> 187 us
    ppermute x24 -> x27, waiting for transfers between devices: 195 us -> 95.5 us  [shift(): lax.ppermute(values, 'narrow', [(i, (i + step) % count) for i in range(co...]
    ppermute x24 -> x27, starting transfers between devices: 52.7 us -> 108 us  [shift(): lax.ppermute(values, 'narrow', [(i, (i + step) % count) for i in range(co...]
    all_gather x2 -> x0, blocking collectives: 35.3 us -> none  [the longest x1 22.1 us: shards(): layer_tokens = lax.all_gather(token_ids, 'wide', axis=0)]
    all_to_all x1, waiting for transfers between devices: 50 us -> 19.8 us  [shards(): lax.all_to_all(sent, 'narrow', 0, 0)]
    all_to_all x1, waiting for transfers between devices: 2.2 us -> 32.2 us  [shards(): found_inputs = lax.all_to_all(found_inputs, 'wide', 0, 0)]
    ppermute x52 -> x55, waiting for transfers between devices: 131 us -> 157 us  [swap(): return lax.ppermute(values, 'wide', [(w, w ^ bit) for w in range(count)])]
    all_to_all x1, waiting for transfers between devices: 18.8 us -> 0.01 us  [shards(): found_targets = lax.all_to_all(found_targets, 'wide', 0, 0)]
    ppermute x52 -> x55, starting transfers between devices: 57.3 us -> 49.1 us  [swap(): return lax.ppermute(values, 'wide', [(w, w ^ bit) for w in range(count)])]
  transfers between devices with their start and end apart: 90 -> 96, of which waited for: 38 -> 37; matrix products, arithmetic and copies ran while one was open for 31% -> 37% of each run, Pallas kernels for 9% -> 11%
where the time goes in v3:
time: 1430 us
  waiting for transfers between devices  335 us (23%)
  matrix products  288 us (20%)
  Pallas kernels  203 us (14%)
  starting transfers between devices  199 us (14%)
  local copies, waits for them, and re-layouts  187 us (13%)
  other arithmetic  170 us (12%)
  between operations  25.1 us (2%)
  blocking collectives  17.6 us (1%)
    ppermute x55, waiting for transfers between devices, swap(): return lax.ppermute(values, 'wide', [(w, w ^ bit) for w in range(count)])  157 us
    dot_general x17, matrix products, dot_nn(): lax.dot_general(left, right, (((1,), (0,)), ((), ())), preferred_element_...  128 us
    ppermute x27, starting transfers between devices, shift(): lax.ppermute(values, 'narrow', [(i, (i + step) % count) for i in range(co...  108 us
    ppermute x27, waiting for transfers between devices, shift(): lax.ppermute(values, 'narrow', [(i, (i + step) % count) for i in range(co...  95.5 us
    dot_general x28, matrix products, dot_tn(): lax.dot_general(left, right, (((0,), (0,)), ((), ())), preferred_element_...  95.1 us
    pallas_call x3, Pallas kernels, attend_back(): pl.pallas_call(lambda *refs: attend_back_kernel(positions is not None, ke...  76.5 us
    unnamed x501, local copies, waits for them, and re-layouts  64.9 us
    convert_element_type x50, other arithmetic, low(): return values.astype(jnp.bfloat16)  57.4 us
  transfers between devices with their start and end apart: 96, of which 37 were waited for; matrix products, arithmetic and copies ran while one was open for 37% of the time, Pallas kernels for 11%

profile of v3, /device:TPU:0, one launch (start us, length us, event | category | flops | bytes accessed | tf_op | source)
XLA Modules:
  0.0 1425.5 jit_solution(16944711737738329238)
XLA Ops:
  18.5 24.0 %collective-permute-start.1 = (s32[2,256]{1,0:T(2,128)S(1)}, s32[2,256]{1,0:T(2,128)S(1)}, u32[]{:S(2)}, u32[]{:S(2)}) collective-permute-start(s32[2,256]{1,0:T(2,128)S(1)} %slice.364), channel_id=1, source_target_pairs={{0,3},{1,0},{2,1},{3,2},{4,7},{5,4},{6,5},{7,6},{8,11},{9,8},{10,9... | collective-permute-start | bytes 6152 | tf_op jit(solution)/shard_map/ppermute | solution.py:328
  77.3 41.5 %fusion.7 = bf16[8192,192]{0,1:T(8,128)(2,1)S(1)} fusion(s32[8192]{0:T(1024)S(1)} %bitcast.473, f32[6288,192]{0,1:T(8,128)} %param.33), kind=kOutput, calls=%fused_computation.11 | convolution fusion | flops 19834630144 | bytes 8007680 | tf_op jit(solution)/shard_map/dot_general | solution.py:22
  175.6 32.2 %all-to-all-done.1 = bf16[8,1024,192]{1,2,0:T(8,128)(2,1)} async-done(((bf16[8,1024,192]{1,2,0:T(8,128)(2,1)}), bf16[8,1024,192]{1,2,0:T(8,128)(2,1)}, u32[]{:S(2)}, u32[]{:S(2)}) %all-to-all-start.1) | async-done | bytes 3145760 | tf_op jit(solution)/shard_map/all_to_all | solution.py:666
  221.5 41.5 %fusion.6 = bf16[8192,192]{0,1:T(8,128)(2,1)S(1)} fusion(s32[8192]{0:T(1024)S(1)} %bitcast.475, f32[6288,192]{0,1:T(8,128)} %param.33), kind=kOutput, calls=%fused_computation.10 | convolution fusion | flops 19834630144 | bytes 8007680 | tf_op jit(solution)/shard_map/dot_general | solution.py:22
  271.2 16.9 %collective-permute-done.15 = bf16[2,1,1,4,24,3456]{5,4,3,2,1,0:T(8,128)(2,1)} collective-permute-done((bf16[2,1,1,4,24,3456]{5,4,3,2,1,0:T(8,128)(2,1)}, bf16[2,1,1,4,24,3456]{5,4,3,2,1,0:T(8,128)(2,1)}, u32[]{:S(2)}, u32[]{:S(2)}) %collective-permute-start.15) | collective-permute-done | bytes 1327136 | tf_op jit(solution)/shard_map/ppermute | solution.py:323
  324.3 21.8 %shard_map.307 = (bf16[512,768]{1,0:T(8,128)(2,1)}, f32[512,768]{1,0:T(8,128)}) custom-call(bf16[512,768]{1,0:T(8,128)(2,1)} %slice.476.refs_0_, bf16[2048,1536]{1,0:T(8,128)(2,1)} %constant_dynamic-update-slice_fusion.refs_1_.refs_2_, bf16[2048,1536]{1,0:T(8,128)(2,1)} %constant_dynamic-update-slice_fusion.refs_1_.refs_2_), custom_call_target="tpu_custom_call" | custom-call | flops 1048576 | bytes 1048576 | tf_op jit(solution)/shard_map/pallas_call | solution.py:76
  387.9 16.7 %collective-permute-done.20 = bf16[256,1536]{1,0:T(8,128)(2,1)S(1)} collective-permute-done((bf16[256,1536]{1,0:T(8,128)(2,1)S(1)}, bf16[256,1536]{1,0:T(8,128)(2,1)S(1)}, u32[]{:S(2)}, u32[]{:S(2)}) %collective-permute-start.20) | collective-permute-done | bytes 786464 | tf_op jit(solution)/shard_map/ppermute | solution.py:323
  418.4 19.3 %all-to-all-done.4 = bf16[4,256,192]{1,2,0:T(8,128)(2,1)} async-done(((bf16[4,256,192]{1,2,0:T(8,128)(2,1)}), bf16[4,256,192]{1,2,0:T(8,128)(2,1)}, u32[]{:S(2)}, u32[]{:S(2)}) %all-to-all-start.4) | async-done | bytes 393248 | tf_op jit(solution)/shard_map/all_to_all | solution.py:660
  456.9 15.4 %collective-permute-done.22 = bf16[512,1536]{1,0:T(8,128)(2,1)} collective-permute-done((bf16[512,1536]{1,0:T(8,128)(2,1)}, bf16[512,1536]{1,0:T(8,128)(2,1)}, u32[]{:S(2)}, u32[]{:S(2)}) %collective-permute-start.22) | collective-permute-done | bytes 1572896 | tf_op jit(solution)/shard_map/ppermute | solution.py:323
  497.9 12.9 shard_map.309
  556.6 53.4 %shard_map.310 = (f32[2048,768]{1,0:T(8,128)}, bf16[2048,6400]{1,0:T(8,128)(2,1)}, f32[2048,128]{1,0:T(8,128)}) custom-call(s32[8]{0:T(128)} %convert_element_type.662.refs_0_, bf16[2048,768]{1,0:T(8,128)(2,1)} %pad_maximum_fusion.7.refs_1_, bf16[768,6400]{1,0:T(8,128)(2,1)} %pad_maximum_fusion.refs_2_), custom_call_target="tpu_custom_call" | custom-call | flops 1048576 | bytes 1048576 | tf_op jit(solution)/shard_map/pallas_call | solution.py:208
  642.0 28.6 %shard_map.311 = bf16[768,6400]{1,0:T(8,128)(2,1)} custom-call(s32[8]{0:T(128)} %convert_element_type.662.refs_0_, bf16[2048,768]{1,0:T(8,128)(2,1)} %pad_maximum_fusion.7.refs_1_, bf16[2048,6400]{1,0:T(8,128)(2,1)} %get-tuple-element.350.refs_2_, f32[2048,128]{1,0:T(8,128)} %maximum_maximum_fusion.refs_3_), custom_call_target="tpu_custom_call" | custom-call | flops 1048576 | bytes 1048576 | tf_op jit(solution)/shard_map/pallas_call | solution.py:261
  692.6 24.2 %collective-permute-start.32 = (bf16[192,6400]{1,0:T(8,128)(2,1)}, bf16[192,6400]{1,0:T(8,128)(2,1)S(1)}, u32[]{:S(2)}, u32[]{:S(2)}) collective-permute-start(bf16[192,6400]{1,0:T(8,128)(2,1)} %get-tuple-element.363), channel_id=1, source_target_pairs={{0,1},{1,2},{2,3},{3,0},{4,5},{5,6},{6,7},{7,4},{8,9},{9,10},{10,1... | collective-permute-start | bytes 7372808 | tf_op jit(solution)/shard_map/ppermute | solution.py:328
  733.3 23.4 %shard_map.312 = (bf16[256,768]{1,0:T(8,128)(2,1)}, bf16[2048,768]{1,0:T(8,128)(2,1)}, bf16[2048,768]{1,0:T(8,128)(2,1)}) custom-call(bf16[256,768]{1,0:T(8,128)(2,1)} %convolution_convert_fusion.20.refs_0_, bf16[2048,1536]{1,0:T(8,128)(2,1)} %constant_dynamic-update-slice_fusion.4.refs_1_.refs_2_, ...), custom_call_target="tpu_custom_call" | custom-call | flops 1048576 | bytes 1048576 | tf_op jit(solution)/shard_map/pallas_call | solution.py:156
  756.7 13.3 collective-permute-done.32
  797.3 14.0 shard_map.313
  858.1 16.3 %collective-permute-done.40 = bf16[512,768]{1,0:T(8,128)(2,1)} collective-permute-done((bf16[512,768]{1,0:T(8,128)(2,1)}, bf16[512,768]{1,0:T(8,128)(2,1)}, u32[]{:S(2)}, u32[]{:S(2)}) %collective-permute-start.40) | collective-permute-done | bytes 786464 | tf_op jit(solution)/shard_map/ppermute | solution.py:323
  920.5 29.1 %collective-permute-done.46 = bf16[192,6400]{1,0:T(8,128)(2,1)} collective-permute-done((bf16[192,6400]{1,0:T(8,128)(2,1)}, bf16[192,6400]{1,0:T(8,128)(2,1)}, u32[]{:S(2)}, u32[]{:S(2)}) %collective-permute-start.46) | collective-permute-done | bytes 2457632 | tf_op jit(solution)/shard_map/ppermute | solution.py:328
  967.1 19.8 %all-to-all-done.6 = bf16[4,256,192]{1,2,0:T(8,128)(2,1)} async-done(((bf16[4,256,192]{1,2,0:T(8,128)(2,1)}), bf16[4,256,192]{1,2,0:T(8,128)(2,1)}, u32[]{:S(2)}, u32[]{:S(2)}) %all-to-all-start.6) | async-done | bytes 393248 | tf_op jit(solution)/shard_map/all_to_all | solution.py:834
  1024.7 39.1 %shard_map.314 = (bf16[512,768]{1,0:T(8,128)(2,1)}, bf16[2048,768]{1,0:T(8,128)(2,1)}, bf16[2048,768]{1,0:T(8,128)(2,1)}) custom-call(bf16[512,768]{1,0:T(8,128)(2,1)} %slice.476.refs_0_, bf16[2048,1536]{1,0:T(8,128)(2,1)} %constant_dynamic-update-slice_fusion.refs_1_.refs_2_, bf16[2048,1536]{1,0:T(8,128)(2,1)} %constant_dynamic-update-slice_fusion.refs_1_.refs_2_, ...), custom_call_target="tpu_custom_call" | custom-call | flops 1048576 | bytes 1048576 | tf_op jit(solution)/shard_map/pallas_call | solution.py:156
  1102.6 23.7 %collective-permute-done.56 = bf16[2,1,96,3072]{3,2,1,0:T(8,128)(2,1)} collective-permute-done((bf16[2,1,96,3072]{3,2,1,0:T(8,128)(2,1)}, bf16[2,1,96,3072]{3,2,1,0:T(8,128)(2,1)}, u32[]{:S(2)}, u32[]{:S(2)}) %collective-permute-start.56) | collective-permute-done | bytes 1179680 | tf_op jit(solution)/shard_map/ppermute | solution.py:323
  1144.7 52.0 %fusion = f32[6288,192]{0,1:T(8,128)} fusion(bf16[8192,192]{0,1:T(8,128)(2,1)S(1)} %copy-done.218, s32[8192]{0:T(1024)S(1)} %bitcast.474), kind=kOutput, calls=%fused_computation.2 | convolution fusion | flops 19831848960 | bytes 8007680 | tf_op jit(solution)/shard_map/dot_general | solution.py:28
  1236.1 17.5 %collective-permute-done.66 = bf16[24,6144]{1,0:T(8,128)(2,1)S(1)} collective-permute-done((bf16[24,6144]{1,0:T(8,128)(2,1)S(1)}, bf16[24,6144]{1,0:T(8,128)(2,1)S(1)}, u32[]{:S(2)}, u32[]{:S(2)}) %collective-permute-start.66) | collective-permute-done | bytes 294944 | tf_op jit(solution)/shard_map/ppermute | solution.py:328
  1374.0 15.2 %fusion.191 = (bf16[6288,192]{0,1:T(8,128)(2,1)}, f32[6288,192]{0,1:T(8,128)}, f32[6288,192]{0,1:T(8,128)}, f32[6288,192]{0,1:T(8,128)}) fusion(f32[6288,192]{0,1:T(8,128)} %param.33, f32[]{:T(128)S(6)} %sub.130, f32[]{:T(128)S(6)} %sub.129, f32[]{:T(128)S(6)} %min.3, f32[6288,192]{0,1:T(8,128)} %fusion, bf16[192,6400]{1,0:T(8,128)(2,1)} %collective-permute-done.46, ...), kind=kLoop, calls=%fused_computation.532 | loop fusion | flops 25353216 | bytes 41048076 | tf_op jit(solution)/shard_map/convert_element_type | solution.py:951
  (1029 shorter events, 788.4 us)
Async XLA Ops:
  17.7 139.2 %all-gather.8.cloned.1.call-start = ((), (), s32[]{:S(2)}) async-start(), calls=%async_computation.8 | async-start | bytes 4866048 | tf_op jit(solution)/shard_map/all_gather | solution.py:643
  64.4 281.7 %all-gather.10.cloned.1.call-start = ((), (), s32[]{:S(2)}) async-start(), calls=%async_computation.9 | async-start | bytes 8515584 | tf_op jit(solution)/shard_map/all_gather | solution.py:643
  142.3 65.4 %all-to-all-start.1 = ((bf16[8,1024,192]{1,2,0:T(8,128)(2,1)}), bf16[8,1024,192]{1,2,0:T(8,128)(2,1)}, u32[]{:S(2)}, u32[]{:S(2)}) async-start(bf16[8,1024,192]{1,2,0:T(8,128)(2,1)} %copy.420), calls=%async_computation.1 | async-start | bytes 6291456 | tf_op jit(solution)/shard_map/all_to_all | solution.py:666
  146.8 363.9 %all-gather.12.cloned.1.call-start = ((), (), s32[]{:S(2)}) async-start(), calls=%async_computation.10 | async-start | bytes 10948608 | tf_op jit(solution)/shard_map/all_gather | solution.py:643
  207.7 80.4 %collective-permute-start.16 = (bf16[192,6400]{1,0:T(8,128)(2,1)}, bf16[192,6400]{1,0:T(8,128)(2,1)}, u32[]{:S(2)}, u32[]{:S(2)}) collective-permute-start(bf16[192,6400]{1,0:T(8,128)(2,1)} %pad.27), channel_id=1, source_target_pairs={{0,3},{1,0},{2,1},{3,2},{4,7},{5,4},{6,5},{7,6},{8,11},{9,8},{10,9... | collective-permute-start | bytes 7372808 | tf_op jit(solution)/shard_map/ppermute | solution.py:328
  212.9 58.3 %all-to-all-start.2 = ((bf16[4,256,192]{1,2,0:T(8,128)(2,1)}), bf16[4,256,192]{1,2,0:T(8,128)(2,1)S(1)}, u32[]{:S(2)}, u32[]{:S(2)}) async-start(bf16[4,256,192]{1,2,0:T(8,128)(2,1)} %bitcast.334), calls=%async_computation.2 | async-start | bytes 786432 | tf_op jit(solution)/shard_map/all_to_all | solution.py:660
  218.9 69.3 %collective-permute-start.13 = (bf16[512,1536]{1,0:T(8,128)(2,1)}, bf16[512,1536]{1,0:T(8,128)(2,1)}, u32[]{:S(2)}, u32[]{:S(2)}) collective-permute-start(bf16[512,1536]{1,0:T(8,128)(2,1)} %slice.477), channel_id=1, source_target_pairs={{0,8},{4,12},{8,0},{12,4},{16,24},{20,28},{24,16},{28,20},{1,9},{5... | collective-permute-start | bytes 4718600 | tf_op jit(solution)/shard_map/ppermute | solution.py:323
  219.6 68.6 %collective-permute-start.15 = (bf16[2,1,1,4,24,3456]{5,4,3,2,1,0:T(8,128)(2,1)}, bf16[2,1,1,4,24,3456]{5,4,3,2,1,0:T(8,128)(2,1)}, u32[]{:S(2)}, u32[]{:S(2)}) collective-permute-start(bf16[2,1,1,4,24,3456]{5,4,3,2,1,0:T(8,128)(2,1)} %maximum_select_fusion.7), channel_id=1, source_target_pairs={{0,8},{4,12},{8,0},{12,4},{16,24},{20,28},{24,16},{28,20},{1,9},{5... | collective-permute-start | bytes 3981320 | tf_op jit(solution)/shard_map/ppermute | solution.py:323
  307.1 69.1 %all-to-all-start.3 = ((bf16[8,1024,192]{1,2,0:T(8,128)(2,1)}), bf16[8,1024,192]{1,2,0:T(8,128)(2,1)}, u32[]{:S(2)}, u32[]{:S(2)}) async-start(bf16[8,1024,192]{1,2,0:T(8,128)(2,1)} %copy.423), calls=%async_computation.3 | async-start | bytes 6291456 | tf_op jit(solution)/shard_map/all_to_all | solution.py:699
  311.6 64.6 %collective-permute-start.19 = (bf16[192,6400]{1,0:T(8,128)(2,1)}, bf16[192,6400]{1,0:T(8,128)(2,1)}, u32[]{:S(2)}, u32[]{:S(2)}) collective-permute-start(bf16[192,6400]{1,0:T(8,128)(2,1)} %collective-permute-done.16), channel_id=1, source_target_pairs={{0,3},{1,0},{2,1},{3,2},{4,7},{5,4},{6,5},{7,6},{8,11},{9,8},{10,9... | collective-permute-start | bytes 7372808 | tf_op jit(solution)/shard_map/ppermute | solution.py:328
  476.8 68.8 %collective-permute-start.30 = (bf16[192,6400]{1,0:T(8,128)(2,1)}, bf16[192,6400]{1,0:T(8,128)(2,1)}, u32[]{:S(2)}, u32[]{:S(2)}) collective-permute-start(bf16[192,6400]{1,0:T(8,128)(2,1)} %collective-permute-done.19), channel_id=1, source_target_pairs={{0,3},{1,0},{2,1},{3,2},{4,7},{5,4},{6,5},{7,6},{8,11},{9,8},{10,9... | collective-permute-start | bytes 7372808 | tf_op jit(solution)/shard_map/ppermute | solution.py:328
  692.6 77.4 %collective-permute-start.32 = (bf16[192,6400]{1,0:T(8,128)(2,1)}, bf16[192,6400]{1,0:T(8,128)(2,1)S(1)}, u32[]{:S(2)}, u32[]{:S(2)}) collective-permute-start(bf16[192,6400]{1,0:T(8,128)(2,1)} %get-tuple-element.363), channel_id=1, source_target_pairs={{0,1},{1,2},{2,3},{3,0},{4,5},{5,6},{6,7},{7,4},{8,9},{9,10},{10,1... | collective-permute-start | bytes 7372808 | tf_op jit(solution)/shard_map/ppermute | solution.py:328
  783.2 91.7 %collective-permute-start.41 = (bf16[192,6400]{1,0:T(8,128)(2,1)}, bf16[192,6400]{1,0:T(8,128)(2,1)}, u32[]{:S(2)}, u32[]{:S(2)}) collective-permute-start(bf16[192,6400]{1,0:T(8,128)(2,1)} %add_convert_fusion.4), channel_id=1, source_target_pairs={{0,1},{1,2},{2,3},{3,0},{4,5},{5,6},{6,7},{7,4},{8,9},{9,10},{10,1... | collective-permute-start | bytes 7372808 | tf_op jit(solution)/shard_map/ppermute | solution.py:328
  844.5 56.7 %collective-permute-start.44 = (bf16[1,1,96,3072]{3,2,1,0:T(8,128)(2,1)}, bf16[1,1,96,3072]{3,2,1,0:T(8,128)(2,1)}, u32[]{:S(2)}, u32[]{:S(2)}) collective-permute-start(bf16[1,1,96,3072]{3,2,1,0:T(8,128)(2,1)} %constant_dynamic-slice_fusion.37), channel_id=1, source_target_pairs={{0,16},{4,20},{8,24},{12,28},{16,0},{20,4},{24,8},{28,12},{1,17},{... | collective-permute-start | bytes 1769480 | tf_op jit(solution)/shard_map/ppermute | solution.py:323
  845.0 56.1 %collective-permute-start.45 = (bf16[1,1,96,3072]{3,2,1,0:T(8,128)(2,1)}, bf16[1,1,96,3072]{3,2,1,0:T(8,128)(2,1)}, u32[]{:S(2)}, u32[]{:S(2)}) collective-permute-start(bf16[1,1,96,3072]{3,2,1,0:T(8,128)(2,1)} %constant_dynamic-slice_fusion.36), channel_id=1, source_target_pairs={{0,8},{4,12},{8,0},{12,4},{16,24},{20,28},{24,16},{28,20},{1,9},{5... | collective-permute-start | bytes 1769480 | tf_op jit(solution)/shard_map/ppermute | solution.py:323
  961.1 165.5 %all-gather.14.cloned.1.call-start = ((), (), s32[]{:S(2)}) async-start(), calls=%async_computation.11 | async-start | bytes 3538944 | tf_op jit(solution)/shard_map/all_gather | solution.py:854
  961.1 63.6 %collective-permute-start.49 = (bf16[24,6144]{1,0:T(8,128)(2,1)}, bf16[24,6144]{1,0:T(8,128)(2,1)}, u32[]{:S(2)}, u32[]{:S(2)}) collective-permute-start(bf16[24,6144]{1,0:T(8,128)(2,1)} %get-tuple-element.423), channel_id=1, source_target_pairs={{0,1},{1,2},{2,3},{3,0},{4,5},{5,6},{6,7},{7,4},{8,9},{9,10},{10,1... | collective-permute-start | bytes 884744 | tf_op jit(solution)/shard_map/ppermute | solution.py:328
  963.1 61.6 %collective-permute-start.50 = (bf16[24,6144]{1,0:T(8,128)(2,1)}, bf16[24,6144]{1,0:T(8,128)(2,1)}, u32[]{:S(2)}, u32[]{:S(2)}) collective-permute-start(bf16[24,6144]{1,0:T(8,128)(2,1)} %get-tuple-element.424), channel_id=1, source_target_pairs={{0,2},{1,3},{2,0},{3,1},{4,6},{5,7},{6,4},{7,5},{8,10},{9,11},{10,... | collective-permute-start | bytes 884744 | tf_op jit(solution)/shard_map/ppermute | solution.py:328
  965.4 59.3 %collective-permute-start.51 = (bf16[24,6144]{1,0:T(8,128)(2,1)}, bf16[24,6144]{1,0:T(8,128)(2,1)}, u32[]{:S(2)}, u32[]{:S(2)}) collective-permute-start(bf16[24,6144]{1,0:T(8,128)(2,1)} %get-tuple-element.425), channel_id=1, source_target_pairs={{0,3},{1,0},{2,1},{3,2},{4,7},{5,4},{6,5},{7,6},{8,11},{9,8},{10,9... | collective-permute-start | bytes 884744 | tf_op jit(solution)/shard_map/ppermute | solution.py:328
  1101.1 95.7 %collective-permute-start.59 = (bf16[512,768]{1,0:T(8,128)(2,1)}, bf16[512,768]{1,0:T(8,128)(2,1)}, u32[]{:S(2)}, u32[]{:S(2)}) collective-permute-start(bf16[512,768]{1,0:T(8,128)(2,1)} %slice.520), channel_id=1, source_target_pairs={{0,8},{4,12},{8,0},{12,4},{16,24},{20,28},{24,16},{28,20},{1,9},{5... | collective-permute-start | bytes 2359304 | tf_op jit(solution)/shard_map/ppermute | solution.py:323
  1134.9 64.8 %collective-permute-start.60 = (bf16[1,1,96,3072]{3,2,1,0:T(8,128)(2,1)S(1)}, bf16[1,1,96,3072]{3,2,1,0:T(8,128)(2,1)S(1)}, u32[]{:S(2)}, u32[]{:S(2)}) collective-permute-start(bf16[1,1,96,3072]{3,2,1,0:T(8,128)(2,1)S(1)} %constant_dynamic-slice_fusion.17), channel_id=1, source_target_pairs={{0,16},{4,20},{8,24},{12,28},{16,0},{20,4},{24,8},{28,12},{1,17},{... | collective-permute-start | bytes 1769480 | tf_op jit(solution)/shard_map/ppermute | solution.py:323
  1135.5 64.2 %collective-permute-start.61 = (bf16[1,1,96,3072]{3,2,1,0:T(8,128)(2,1)S(1)}, bf16[1,1,96,3072]{3,2,1,0:T(8,128)(2,1)S(1)}, u32[]{:S(2)}, u32[]{:S(2)}) collective-permute-start(bf16[1,1,96,3072]{3,2,1,0:T(8,128)(2,1)S(1)} %constant_dynamic-slice_fusion.16), channel_id=1, source_target_pairs={{0,8},{4,12},{8,0},{12,4},{16,24},{20,28},{24,16},{28,20},{1,9},{5... | collective-permute-start | bytes 1769480 | tf_op jit(solution)/shard_map/ppermute | solution.py:323
  1136.8 63.0 %collective-permute-start.62 = (bf16[1,1,96,3072]{3,2,1,0:T(8,128)(2,1)S(1)}, bf16[1,1,96,3072]{3,2,1,0:T(8,128)(2,1)S(1)}, u32[]{:S(2)}, u32[]{:S(2)}) collective-permute-start(bf16[1,1,96,3072]{3,2,1,0:T(8,128)(2,1)S(1)} %constant_dynamic-slice_fusion.15), channel_id=1, source_target_pairs={{0,16},{4,20},{8,24},{12,28},{16,0},{20,4},{24,8},{28,12},{1,17},{... | collective-permute-start | bytes 1769480 | tf_op jit(solution)/shard_map/ppermute | solution.py:323
  1143.2 56.5 %collective-permute-start.63 = (bf16[1,1,96,3072]{3,2,1,0:T(8,128)(2,1)S(1)}, bf16[1,1,96,3072]{3,2,1,0:T(8,128)(2,1)S(1)}, u32[]{:S(2)}, u32[]{:S(2)}) collective-permute-start(bf16[1,1,96,3072]{3,2,1,0:T(8,128)(2,1)S(1)} %constant_dynamic-slice_fusion.14), channel_id=1, source_target_pairs={{0,8},{4,12},{8,0},{12,4},{16,24},{20,28},{24,16},{28,20},{1,9},{5... | collective-permute-start | bytes 1769480 | tf_op jit(solution)/shard_map/ppermute | solution.py:323
  (307 other events, 6192.5 us)
Sparse Core Ops, SparseCore 0:
  64.6 92.2 all-gather.7
  160.3 152.6 all-gather.9
  315.7 155.9 all-gather.11
  1024.9 29.5 all-gather.13

commit v4 on v3

--- a/solution.py
+++ b/solution.py
@@ -30,29 +30,41 @@
     )
 
 
-def attend_kernel(masked, row_step, *refs):
+def attend_kernel(masked, parts, row_step, *refs):
     if masked:
-        query_pos, key_pos, q_ref, k_ref, v_ref, out_ref, lse_ref = refs
-    else:
-        q_ref, k_ref, v_ref, out_ref, lse_ref = refs
-    keys = k_ref[...]
-    values = v_ref[...]
-    key_lane = lax.broadcasted_iota(jnp.int32, values.shape, 1) // HEAD_DIM
+        query_pos, key_pos, refs = refs[0], refs[1], refs[2:]
+    q_ref, pair_refs, out_ref, lse_ref = refs[0], refs[1 : 1 + parts], refs[-2], refs[-1]
     lane = lax.broadcasted_iota(jnp.int32, (row_step, 128), 1) // HEAD_DIM
-    one = jnp.ones((), values.dtype)
-    sides = [jnp.where(key_lane == side, values, one) for side in range(2)]
+    one = jnp.ones((), jnp.bfloat16)
+    keys, sides, begins = [], [], [0]
+    for pair_ref in pair_refs:
+        keys.append(pair_ref[:, :128])
+        values = pair_ref[:, 128:]
+        key_lane = lax.broadcasted_iota(jnp.int32, values.shape, 1) // HEAD_DIM
+        sides.append([jnp.where(key_lane == side, values, one) for side in range(2)])
+        begins.append(begins[-1] + values.shape[0])
     for start in range(0, q_ref.shape[0], row_step):
         rows = pl.ds(start, row_step)
         queries = q_ref[rows, :]
         mixed, totals = [], []
         for side in range(2):
             half = jnp.where(lane == side, queries, jnp.zeros((), queries.dtype)) * attn_scale
-            scores = dot_nt(half.astype(jnp.bfloat16), keys)
+            scores = [dot_nt(half.astype(jnp.bfloat16), part) for part in keys]
             if masked:
-                scores = jnp.where(key_pos[...] <= query_pos[rows, :], scores, -1000000000.0)
-            top = jnp.max(scores, axis=1, keepdims=True)
-            exponent = jnp.exp(scores - top).astype(jnp.bfloat16)
-            both = dot_nn(exponent, sides[side])
+                scores = [
+                    jnp.where(
+                        key_pos[:, begins[k] : begins[k + 1]] <= query_pos[rows, :],
+                        part,
+                        -1000000000.0,
+                    )
+                    for k, part in enumerate(scores)
+                ]
+            top = jnp.max(scores[0], axis=1, keepdims=True)
+            for part in scores[1:]:
+                top = jnp.maximum(top, jnp.max(part, axis=1, keepdims=True))
+            both = jnp.zeros((row_step, 128), jnp.float32)
+            for part, values in zip(scores, sides):
+                both += dot_nn(jnp.exp(part - top).astype(jnp.bfloat16), values[side])
             other = (1 - side) * HEAD_DIM
             summed = both[:, other : other + 1]
             mixed.append(both / summed)
@@ -61,9 +73,8 @@
         lse_ref[rows, :] = jnp.where(lane == 0, totals[0], totals[1])
 
 
-def attend(queries, keys_values, positions):
-    rows, keys = queries.shape[0], keys_values.shape[0]
-    pairs = D // 128
+def attend(queries, pairs, positions):
+    rows, keys = queries.shape[0], sum(part.shape[0] for part in pairs)
     row_step = min(rows, 256)
     extra, extra_specs = (), []
     if positions is not None:
@@ -73,33 +84,28 @@
             pl.BlockSpec((rows, 1), lambda j: (0, 0)),
             pl.BlockSpec((1, keys), lambda j: (0, 0)),
         ]
+    row_spec = pl.BlockSpec((rows, 128), lambda j: (0, j))
     return pl.pallas_call(
-        lambda *refs: attend_kernel(positions is not None, row_step, *refs),
-        grid=(pairs,),
+        lambda *refs: attend_kernel(positions is not None, len(pairs), row_step, *refs),
+        grid=(D // 128,),
         in_specs=extra_specs
-        + [
-            pl.BlockSpec((rows, 128), lambda j: (0, j)),
-            pl.BlockSpec((keys, 128), lambda j: (0, j)),
-            pl.BlockSpec((keys, 128), lambda j: (0, j + pairs)),
-        ],
-        out_specs=[
-            pl.BlockSpec((rows, 128), lambda j: (0, j)),
-            pl.BlockSpec((rows, 128), lambda j: (0, j)),
-        ],
+        + [row_spec]
+        + [pl.BlockSpec((part.shape[0], 256), lambda j: (0, j)) for part in pairs],
+        out_specs=[row_spec, row_spec],
         out_shape=[
             jax.ShapeDtypeStruct((rows, D), jnp.bfloat16),
             jax.ShapeDtypeStruct((rows, D), jnp.float32),
         ],
         compiler_params=pltpu.CompilerParams(vmem_limit_bytes=KERNEL_VMEM),
         cost_estimate=SMALL_COST,
-    )(*extra, queries, keys_values, keys_values)
-
-
-def attend_back_kernel(masked, key_step, *refs):
+    )(*extra, queries, *pairs)
+
+
+def attend_back_kernel(masked, parts, *refs):
     if masked:
-        query_pos, key_pos, q_ref, k_ref, v_ref, out_ref, lse_ref, grad_ref, dq_ref, dk_ref, dv_ref = refs
-    else:
-        q_ref, k_ref, v_ref, out_ref, lse_ref, grad_ref, dq_ref, dk_ref, dv_ref = refs
+        query_pos, key_pos, refs = refs[0], refs[1], refs[2:]
+    q_ref, pair_refs, refs = refs[0], refs[1 : 1 + parts], refs[1 + parts :]
+    out_ref, lse_ref, grad_ref, dq_ref, pair_grad_ref = refs
     queries = q_ref[...]
     grads = grad_ref[...]
     lane = lax.broadcasted_iota(jnp.int32, queries.shape, 1) // HEAD_DIM
@@ -115,33 +121,36 @@
             jnp.sum(weighted[side * HEAD_DIM : (side + 1) * HEAD_DIM, :], axis=0, keepdims=True)
         )
         grad_queries.append(jnp.zeros(queries.shape, jnp.float32))
-    for start in range(0, k_ref.shape[0], key_step):
-        rows = pl.ds(start, key_step)
-        keys = k_ref[rows, :]
-        values = v_ref[rows, :]
-        grad_keys = jnp.zeros(keys.shape, jnp.float32)
-        grad_values = jnp.zeros(keys.shape, jnp.float32)
-        for side in range(2):
-            scores = dot_nt(keys, halves[side])
-            probs = jnp.exp(scores - total_rows[side])
-            if masked:
-                probs = jnp.where(key_pos[rows, :] <= query_pos[...], probs, 0.0)
-            grad_probs = dot_nt(values, grad_halves[side])
-            grad_scores = (probs * (grad_probs - delta_rows[side])).astype(jnp.bfloat16)
-            grad_values += dot_nn(probs.astype(jnp.bfloat16), grad_halves[side])
-            grad_keys += dot_nn(grad_scores, halves[side])
-            grad_queries[side] += dot_tn(grad_scores, keys)
-        dk_ref[rows, :] = grad_keys.astype(dk_ref.dtype)
-        dv_ref[rows, :] = grad_values.astype(dv_ref.dtype)
+    base = 0
+    for pair_ref in pair_refs:
+        key_step = min(pair_ref.shape[0], 512)
+        for start in range(0, pair_ref.shape[0], key_step):
+            here = pl.ds(start, key_step)
+            rows = pl.ds(base + start, key_step)
+            keys = pair_ref[here, :128]
+            values = pair_ref[here, 128:]
+            grad_keys = jnp.zeros(keys.shape, jnp.float32)
+            grad_values = jnp.zeros(keys.shape, jnp.float32)
+            for side in range(2):
+                scores = dot_nt(keys, halves[side])
+                probs = jnp.exp(scores - total_rows[side])
+                if masked:
+                    probs = jnp.where(key_pos[rows, :] <= query_pos[...], probs, 0.0)
+                grad_probs = dot_nt(values, grad_halves[side])
+                grad_scores = (probs * (grad_probs - delta_rows[side])).astype(jnp.bfloat16)
+                grad_values += dot_nn(probs.astype(jnp.bfloat16), grad_halves[side])
+                grad_keys += dot_nn(grad_scores, halves[side])
+                grad_queries[side] += dot_tn(grad_scores, keys)
+            pair_grad_ref[rows, :128] = grad_keys.astype(pair_grad_ref.dtype)
+            pair_grad_ref[rows, 128:] = grad_values.astype(pair_grad_ref.dtype)
+        base += pair_ref.shape[0]
     dq_ref[...] = (jnp.where(lane == 0, grad_queries[0], grad_queries[1]) * attn_scale).astype(
         dq_ref.dtype
     )
 
 
-def attend_back(queries, keys_values, positions, mixed_rows, log_total, grad_mixed):
-    rows, keys = queries.shape[0], keys_values.shape[0]
-    pairs = D // 128
-    key_step = min(keys, 512)
+def attend_back(queries, pairs, positions, mixed_rows, log_total, grad_mixed):
+    rows, keys = queries.shape[0], sum(part.shape[0] for part in pairs)
     extra, extra_specs = (), []
     if positions is not None:
         query_pos, key_pos = positions
@@ -151,21 +160,21 @@
             pl.BlockSpec((keys, 1), lambda j: (0, 0)),
         ]
     row_spec = pl.BlockSpec((rows, 128), lambda j: (0, j))
-    key_spec = pl.BlockSpec((keys, 128), lambda j: (0, j))
-    value_spec = pl.BlockSpec((keys, 128), lambda j: (0, j + pairs))
     return pl.pallas_call(
-        lambda *refs: attend_back_kernel(positions is not None, key_step, *refs),
-        grid=(pairs,),
-        in_specs=extra_specs + [row_spec, key_spec, value_spec, row_spec, row_spec, row_spec],
-        out_specs=[row_spec, key_spec, key_spec],
+        lambda *refs: attend_back_kernel(positions is not None, len(pairs), *refs),
+        grid=(D // 128,),
+        in_specs=extra_specs
+        + [row_spec]
+        + [pl.BlockSpec((part.shape[0], 256), lambda j: (0, j)) for part in pairs]
+        + [row_spec] * 3,
+        out_specs=[row_spec, pl.BlockSpec((keys, 256), lambda j: (0, j))],
         out_shape=[
             jax.ShapeDtypeStruct((rows, D), jnp.bfloat16),
-            jax.ShapeDtypeStruct((keys, D), jnp.bfloat16),
-            jax.ShapeDtypeStruct((keys, D), jnp.bfloat16),
+            jax.ShapeDtypeStruct((keys, 2 * D), jnp.bfloat16),
         ],
         compiler_params=pltpu.CompilerParams(vmem_limit_bytes=KERNEL_VMEM),
         cost_estimate=SMALL_COST,
-    )(*extra, queries, keys_values, keys_values, mixed_rows, log_total, grad_mixed)
+    )(*extra, queries, *pairs, mixed_rows, log_total, grad_mixed)
 
 
 def head_kernel(vocab, tile, used_ref, rows_ref, table_ref, mixed_ref, exp_ref, stats_ref, logits_ref):
@@ -277,6 +286,35 @@
     )(used, rows_all, exps, info)
 
 
+def row_sums_kernel(step_rows, ids_ref, rows_ref, sums_ref):
+    width, height = sums_ref.shape
+    total = jnp.zeros((height, width), jnp.float32)
+    for start in range(0, rows_ref.shape[1], step_rows):
+        place = pl.program_id(0) * height + lax.broadcasted_iota(
+            jnp.int32, (height, step_rows), 0
+        )
+        hits = jnp.where(place == ids_ref[:, start : start + step_rows], 1.0, 0.0)
+        total += dot_nt(hits.astype(jnp.bfloat16), rows_ref[:, start : start + step_rows])
+    sums_ref[...] = total.T
+
+
+def row_sums(ids, rows, places):
+    width, count = rows.shape
+    height = 640 if places % 640 == 0 else 256
+    return pl.pallas_call(
+        lambda *refs: row_sums_kernel(1024, *refs),
+        grid=(places // height,),
+        in_specs=[
+            pl.BlockSpec((1, count), lambda i: (0, 0)),
+            pl.BlockSpec((width, count), lambda i: (0, 0), pipeline_mode=pl.Buffered(1)),
+        ],
+        out_specs=pl.BlockSpec((width, height), lambda i: (0, i)),
+        out_shape=jax.ShapeDtypeStruct((width, places), jnp.float32),
+        compiler_params=pltpu.CompilerParams(vmem_limit_bytes=KERNEL_VMEM),
+        cost_estimate=SMALL_COST,
+    )(ids.reshape(1, count), rows)
+
+
 FF = 2048
 POS = 256
 TGT = 1024
@@ -299,6 +337,19 @@
 BOTH = ("wide", "narrow")
 
 
+def block_order():
+    order, offset = [], 0
+    for number, extent in enumerate(EXTENTS):
+        blocks = list(range(offset, offset + extent // BW))
+        pairs = D // BW
+        if number in (1, 5, 8):
+            keys, values = blocks[-2 * pairs : -pairs], blocks[-pairs:]
+            blocks = blocks[: -2 * pairs] + [b for both in zip(keys, values) for b in both]
+        order += blocks
+        offset += extent // BW
+    return order
+
+
 def rms_norm(values, gain_vec):
     return (
         values * lax.rsqrt(jnp.mean(values * values, axis=-1, keepdims=True) + norm_eps) * gain_vec
@@ -354,6 +405,15 @@
         [gather_wide(values[..., :half], first + [0]), gather_wide(values[..., half:], second + [0])],
         axis=-1,
     )
+
+
+def in_three(value):
+    parts = []
+    for _ in range(3):
+        part = lax.reduce_precision(value, 8, 7)
+        parts.append(low(part))
+        value = value - part
+    return parts
 
 
 def tie(*values):
@@ -497,9 +557,10 @@
     while bit:
         (rows,) = yield [rows]
         rows, other = yield [rows, swap(rows, bit)]
-        rows = jnp.concatenate([rows, other], axis=0)
         bit //= 2
-    return rows
+        if bit:
+            rows = jnp.concatenate([rows, other], axis=0)
+    return [rows, other]
 
 
 def return_flow(parts):
@@ -514,7 +575,7 @@
             for part, other in zip(parts, got)
         ]
         bit *= 2
-    return jnp.concatenate(parts, axis=1)
+    return parts[0]
 
 
 def gather_flow(rows):
@@ -599,7 +660,7 @@
     slot_total = block_slot.shape[0]
     own_count = master_slabs.shape[0]
     piece = D // devices
-    slot_ids = block_slot[:BLOCKS]
+    slot_ids = block_slot[jnp.array(block_order())]
     enc_rows, dec_rows = patches.shape[0], input_ids.shape[0]
     vocab_rows, features = vocab_table.shape
 
@@ -803,20 +864,20 @@
     low_two = low(grad_two)
     grad_mixed = low(dot_nt(low_two, weights[9]))
     grad_mixed = step(grad_mixed, flow_dffn)
-    grad_cq, grad_key, grad_value = attend_back(
+    grad_cq, grad_pair = attend_back(
         cross_query, cross_keys, None, cross_mixed, cross_total, grad_mixed
     )
-    flow_cross = Flow(return_flow([grad_key, grad_value]))
+    flow_cross = Flow(return_flow([grad_pair]))
     grad_cq = step(grad_cq, flow_cross, ring)
     grad_one, gain_cross = norm_back(dec_one, gain_rows[4], dot_nt(grad_cq, weights[7]))
     grad_one = grad_one + grad_two
     low_one = low(grad_one)
     grad_mixed = low(dot_nt(low_one, weights[6]))
     grad_mixed = step(grad_mixed, flow_cross)
-    grad_sq, grad_key, grad_value = attend_back(
+    grad_sq, grad_pair = attend_back(
         dec_mix[:, :D], self_keys, causal, self_mixed, self_total, grad_mixed
     )
-    flow_self = Flow(return_flow([grad_key, grad_value]))
+    flow_self = Flow(return_flow([grad_pair]))
     grad_sq = step(grad_sq, flow_self, flow_dffn)
     grad_sq = step(grad_sq, flow_self)
     grad_sq = step(grad_sq, flow_cross, ring)
@@ -852,17 +913,16 @@
     grad_mixed = step(grad_mixed, flow_dattn, flow_effn)
     grad_mixed, sent = step((grad_mixed, sent), flow_dffn)
     sent = lax.all_gather(sent, "wide", axis=0, tiled=True)
-    grad_eq, grad_key, grad_value = attend_back(
+    grad_eq, grad_pair = attend_back(
         enc_mix[:, :D], enc_keys, None, enc_mixed, enc_total, grad_mixed
     )
-    flow_enc = Flow(return_flow([grad_key, grad_value]))
+    grad_eq = step(grad_eq, flow_dattn, flow_effn)
+    flow_enc = Flow(return_flow([grad_pair]))
     grad_eq = step(grad_eq, flow_enc)
-    grad_eq = step(grad_eq, flow_enc)
-    grad_eq, sent = step((grad_eq, sent), flow_dattn, flow_effn)
-    onehot = (flat_inputs[:, None] == columns[None, :]).astype(jnp.bfloat16)
-    looked_grad = dot_tn(onehot, sent)
+    grad_eq, sent = step((grad_eq, sent), flow_enc)
+    looked_grad = row_sums(flat_inputs, sent.T, padded)
     grad_eq, looked_grad = step((grad_eq, looked_grad), flow_enc)
-    grad_eq = step(grad_eq, flow_dattn, flow_effn)
+    grad_eq, looked_grad = step((grad_eq, looked_grad), flow_dattn, flow_effn)
     grad_emix = jnp.concatenate([grad_eq, flow_enc.drain()], axis=1)
     grad_zero, gain_eattn = norm_back(enc_zero, gain_rows[0], dot_nt(grad_emix, weights[1]))
     grad_zero = grad_zero + grad_one
@@ -884,11 +944,11 @@
         )
     )
     looked_grad = step(looked_grad, flow_eattn)
-    head_grad = ring.drain()[:, :vocab_rows].T
-    vocab_grad = head_grad + looked_grad
+    vocab_grad = (ring.drain() + looked_grad)[:, :vocab_rows].T
     vocab_square = jnp.sum(vocab_grad * vocab_grad)
     vocab_square = step(vocab_square, flow_eattn)
     vocab_square = step(vocab_square, flow_dattn, flow_effn)
+    vocab_square = step(vocab_square, flow_eattn)
     vocab_square = step(vocab_square, flow_eattn)
     shard_dffn, shard_dattn = flow_dffn.drain(), flow_dattn.drain()
     shard_effn, shard_eattn = flow_effn.drain(), flow_eattn.drain()
@@ -901,21 +961,18 @@
         + vocab_square
         + jnp.sum(small_shard * small_shard)
     )
-    scalars = jnp.where(
-        jnp.arange(SMALL_ROWS)[None, :] == 0,
-        partial_square,
-        jnp.where(jnp.arange(SMALL_ROWS)[None, :] == 1, loss_local, 0.0),
-    )
+    scalars = jnp.stack(in_three(partial_square) + in_three(loss_local))
+    scalars = jnp.pad(scalars[None, :], ((0, 0), (0, SMALL_ROWS - 6)))
     slotted = grads.reshape(piece, BLOCKS, BW).transpose(1, 0, 2).reshape(BLOCKS, piece * BW)
     slotted = low(dot_tn(block_of_slot, slotted)).reshape(devices, own_count, piece, BW)
     small_shard, scalars, slotted = tie(small_shard, scalars, slotted)
     slab = lax.all_to_all(slotted, BOTH, 0, 0).transpose(1, 0, 2, 3).reshape(own_count, D, BW)
-    shared = from_narrow(jnp.concatenate([small_shard, scalars], axis=0))
+    shared = from_narrow(jnp.concatenate([low(small_shard), scalars], axis=0))
     shared = join_wide(shared.reshape((1,) * wide_bits() + shared.shape), split_orders()[0] + [0])
-    shared = shared.reshape(devices, piece + 1, SMALL_ROWS)
+    shared = shared.reshape(devices, piece + 1, SMALL_ROWS).astype(jnp.float32)
     small_grad = shared[:, :piece].reshape(D, SMALL_ROWS).T
-    total_square = jnp.sum(shared[:, piece, 0])
-    loss_sum = jnp.sum(shared[:, piece, 1])
+    total_square = jnp.sum(shared[:, piece, :3])
+    loss_sum = jnp.sum(shared[:, piece, 3:6])
 
     grad_norm = jnp.sqrt(total_square)
     factor = jnp.minimum(1.0, clip_limit / (grad_norm + 1e-06))

time: 1430 us -> 1400 us (0.979)
  matrix products: 288 us -> 243 us
  Pallas kernels: 203 us -> 245 us
  starting transfers between devices: 199 us -> 171 us
  local copies, waits for them, and re-layouts: 187 us -> 164 us
    dot_general x28 -> x27, matrix products: 95.1 us -> 47.9 us  [dot_tn(): lax.dot_general(left, right, (((0,), (0,)), ((), ())), preferred_element_...]
    pallas_call x6 -> x7, Pallas kernels: 121 us -> 154 us  [the longest x3 76.3 us: attend_back(): pl.pallas_call(lambda *refs: attend_back_kernel(positions is not None, le...]
    ppermute x27, waiting for transfers between devices: 95.5 us -> 128 us  [shift(): lax.ppermute(values, 'narrow', [(i, (i + step) % count) for i in range(co...]
    ppermute x27, starting transfers between devices: 108 us -> 82.1 us  [shift(): lax.ppermute(values, 'narrow', [(i, (i + step) % count) for i in range(co...]
    ppermute x55 -> x49, waiting for transfers between devices: 157 us -> 133 us  [swap(): return lax.ppermute(values, 'wide', [(w, w ^ bit) for w in range(count)])]
    all_to_all x1, waiting for transfers between devices: 19.8 us -> 0.01 us  [shards(): lax.all_to_all(sent, 'narrow', 0, 0)]
    unnamed x501 -> x498, local copies, waits for them, and re-layouts: 64.9 us -> 60.3 us
    convert_element_type x50 -> x43, other arithmetic: 57.4 us -> 54.1 us  [low(): return values.astype(jnp.bfloat16)]
  transfers between devices with their start and end apart: 96 -> 90, of which waited for: 37 -> 40; matrix products, arithmetic and copies ran while one was open for 37% -> 33% of each run, Pallas kernels for 11% -> 13%
where the time goes in v4:
time: 1400 us; the launch traced here: 1380 us
  waiting for transfers between devices  337 us (24%)
  Pallas kernels  245 us (18%)
  matrix products  243 us (17%)
  starting transfers between devices  171 us (12%)
  other arithmetic  170 us (12%)
  local copies, waits for them, and re-layouts  164 us (12%)
  between operations  34.5 us (2%)
  blocking collectives  18 us (1%)
    ppermute x49, waiting for transfers between devices, swap(): return lax.ppermute(values, 'wide', [(w, w ^ bit) for w in range(count)])  133 us
    dot_general x17, matrix products, dot_nn(): lax.dot_general(left, right, (((1,), (0,)), ((), ())), preferred_element_...  131 us
    ppermute x27, waiting for transfers between devices, shift(): lax.ppermute(values, 'narrow', [(i, (i + step) % count) for i in range(co...  128 us
    ppermute x27, starting transfers between devices, shift(): lax.ppermute(values, 'narrow', [(i, (i + step) % count) for i in range(co...  82.1 us
    pallas_call x3, Pallas kernels, attend_back(): pl.pallas_call(lambda *refs: attend_back_kernel(positions is not None, le...  76.3 us
    pallas_call x1, Pallas kernels, head_forward(): pl.pallas_call(lambda *refs: head_kernel(vocab, tile, *refs), grid_spec=p...  60.5 us
    unnamed x498, local copies, waits for them, and re-layouts  60.3 us
    convert_element_type x43, other arithmetic, low(): return values.astype(jnp.bfloat16)  54.1 us
  transfers between devices with their start and end apart: 90, of which 40 were waited for; matrix products, arithmetic and copies ran while one was open for 33% of the time, Pallas kernels for 13%

profile of v4, /device:TPU:0, one launch (start us, length us, event | category | flops | bytes accessed | tf_op | source)
XLA Modules:
  0.0 1382.3 jit_solution(17782395913362716964)
XLA Ops:
  18.5 24.0 %collective-permute-start.1 = (s32[2,256]{1,0:T(2,128)S(1)}, s32[2,256]{1,0:T(2,128)S(1)}, u32[]{:S(2)}, u32[]{:S(2)}) collective-permute-start(s32[2,256]{1,0:T(2,128)S(1)} %slice.325), channel_id=1, source_target_pairs={{0,3},{1,0},{2,1},{3,2},{4,7},{5,4},{6,5},{7,6},{8,11},{9,8},{10,9... | collective-permute-start | bytes 6152 | tf_op jit(solution)/shard_map/ppermute | solution.py:379
  77.8 41.5 %fusion.5 = bf16[8192,192]{0,1:T(8,128)(2,1)S(1)} fusion(s32[8192]{0:T(1024)S(1)} %bitcast.469, f32[6288,192]{0,1:T(8,128)} %param.34), kind=kOutput, calls=%fused_computation.10 | convolution fusion | flops 19834630144 | bytes 8007680 | tf_op jit(solution)/shard_map/dot_general | solution.py:22
  176.3 32.2 %all-to-all-done.1 = bf16[8,1024,192]{1,2,0:T(8,128)(2,1)} async-done(((bf16[8,1024,192]{1,2,0:T(8,128)(2,1)}), bf16[8,1024,192]{1,2,0:T(8,128)(2,1)}, u32[]{:S(2)}, u32[]{:S(2)}) %all-to-all-start.1) | async-done | bytes 3145760 | tf_op jit(solution)/shard_map/all_to_all | solution.py:727
  222.1 41.5 %fusion.4 = bf16[8192,192]{0,1:T(8,128)(2,1)S(1)} fusion(s32[8192]{0:T(1024)S(1)} %bitcast.482, f32[6288,192]{0,1:T(8,128)} %param.34), kind=kOutput, calls=%fused_computation.9 | convolution fusion | flops 19834630144 | bytes 8007680 | tf_op jit(solution)/shard_map/dot_general | solution.py:22
  271.9 16.4 %collective-permute-done.15 = bf16[2,1,1,4,24,3456]{5,4,3,2,1,0:T(8,128)(2,1)} collective-permute-done((bf16[2,1,1,4,24,3456]{5,4,3,2,1,0:T(8,128)(2,1)}, bf16[2,1,1,4,24,3456]{5,4,3,2,1,0:T(8,128)(2,1)}, u32[]{:S(2)}, u32[]{:S(2)}) %collective-permute-start.15) | collective-permute-done | bytes 1327136 | tf_op jit(solution)/shard_map/ppermute | solution.py:374
  316.1 22.0 %shard_map.316 = (bf16[512,768]{1,0:T(8,128)(2,1)}, f32[512,768]{1,0:T(8,128)}) custom-call(bf16[512,768]{1,0:T(8,128)(2,1)} %slice.426.refs_0_, bf16[1024,1536]{1,0:T(8,128)(2,1)} %pad_maximum_fusion.5.refs_1_, bf16[1024,1536]{1,0:T(8,128)(2,1)} %collective-permute-done.17.refs_2_), custom_call_target="tpu_custom_call" | custom-call | flops 1048576 | bytes 1048576 | tf_op jit(solution)/shard_map/pallas_call | solution.py:88
  361.4 14.5 %collective-permute-done.19 = bf16[192,6400]{1,0:T(8,128)(2,1)} collective-permute-done((bf16[192,6400]{1,0:T(8,128)(2,1)}, bf16[192,6400]{1,0:T(8,128)(2,1)}, u32[]{:S(2)}, u32[]{:S(2)}) %collective-permute-start.19) | collective-permute-done | bytes 2457632 | tf_op jit(solution)/shard_map/ppermute | solution.py:379
  387.8 16.7 %collective-permute-done.20 = bf16[256,1536]{1,0:T(8,128)(2,1)S(1)} collective-permute-done((bf16[256,1536]{1,0:T(8,128)(2,1)S(1)}, bf16[256,1536]{1,0:T(8,128)(2,1)S(1)}, u32[]{:S(2)}, u32[]{:S(2)}) %collective-permute-start.20) | collective-permute-done | bytes 786464 | tf_op jit(solution)/shard_map/ppermute | solution.py:374
  416.9 18.8 %all-to-all-done.4 = bf16[4,256,192]{1,2,0:T(8,128)(2,1)S(1)} async-done(((bf16[4,256,192]{1,2,0:T(8,128)(2,1)}), bf16[4,256,192]{1,2,0:T(8,128)(2,1)S(1)}, u32[]{:S(2)}, u32[]{:S(2)}) %all-to-all-start.4) | async-done | bytes 393248 | tf_op jit(solution)/shard_map/all_to_all | solution.py:721
  451.7 17.6 %collective-permute-done.22 = bf16[512,1536]{1,0:T(8,128)(2,1)} collective-permute-done((bf16[512,1536]{1,0:T(8,128)(2,1)}, bf16[512,1536]{1,0:T(8,128)(2,1)}, u32[]{:S(2)}, u32[]{:S(2)}) %collective-permute-start.22) | collective-permute-done | bytes 1572896 | tf_op jit(solution)/shard_map/ppermute | solution.py:374
  489.9 13.0 shard_map.318
  549.2 60.5 %shard_map.319 = (f32[2048,768]{1,0:T(8,128)}, bf16[2048,6400]{1,0:T(8,128)(2,1)}, f32[2048,128]{1,0:T(8,128)}) custom-call(s32[8]{0:T(128)} %convert_element_type.633.refs_0_, bf16[2048,768]{1,0:T(8,128)(2,1)} %pad_maximum_fusion.7.refs_1_, bf16[768,6400]{1,0:T(8,128)(2,1)} %pad_maximum_fusion.refs_2_), custom_call_target="tpu_custom_call" | custom-call | flops 1048576 | bytes 1048576 | tf_op jit(solution)/shard_map/pallas_call | solution.py:217
  642.0 30.3 %shard_map.320 = bf16[768,6400]{1,0:T(8,128)(2,1)} custom-call(s32[8]{0:T(128)} %convert_element_type.633.refs_0_, bf16[2048,768]{1,0:T(8,128)(2,1)} %pad_maximum_fusion.7.refs_1_, bf16[2048,6400]{1,0:T(8,128)(2,1)} %get-tuple-element.345.refs_2_, f32[2048,128]{1,0:T(8,128)} %maximum_maximum_fusion.refs_3_), custom_call_target="tpu_custom_call" | custom-call | flops 1048576 | bytes 1048576 | tf_op jit(solution)/shard_map/pallas_call | solution.py:270
  711.0 23.4 %shard_map.321 = (bf16[256,768]{1,0:T(8,128)(2,1)}, bf16[2048,1536]{1,0:T(8,128)(2,1)}) custom-call(bf16[256,768]{1,0:T(8,128)(2,1)} %convolution_convert_fusion.20.refs_0_, bf16[1024,1536]{1,0:T(8,128)(2,1)} %copy-done.4, bf16[1024,1536]{1,0:T(8,128)(2,1)} %collective-permute-done.23.refs_2_, bf16[256,768]{1,0:T(8,128)(2,1)} %get-tuple-element.343.refs_3_, ...), custom_call_target="tpu_custom_call" | custom-call | flops 1048576 | bytes 1048576 | tf_op jit(solution)/shard_map/pallas_call | solution.py:163
  734.4 17.2 %collective-permute-done.32 = bf16[192,6400]{1,0:T(8,128)(2,1)S(1)} collective-permute-done((bf16[192,6400]{1,0:T(8,128)(2,1)}, bf16[192,6400]{1,0:T(8,128)(2,1)S(1)}, u32[]{:S(2)}, u32[]{:S(2)}) %collective-permute-start.32) | collective-permute-done | bytes 2457632 | tf_op jit(solution)/shard_map/ppermute | solution.py:379
  773.5 14.0 %shard_map.322 = (bf16[256,768]{1,0:T(8,128)(2,1)}, bf16[1024,1536]{1,0:T(8,128)(2,1)}) custom-call(s32[1,256]{1,0:T(1,128)} %iota_add_fusion.1.refs_0_, s32[1024,1]{1,0:T(8,128)} %copy.463.refs_1_, bf16[256,768]{1,0:T(8,128)(2,1)} %slice.432.refs_2_, bf16[512,1536]{1,0:T(8,128)(2,1)} %copy-done.8, bf16[512,1536]{1,0:T(8,128)(2,1)} %collective-permute-done.21.refs_4_, ...), custom_call_target="tpu_custom_call" | custom-call | flops 1048576 | bytes 1048576 | tf_op jit(solution)/shard_map/pallas_call | solution.py:163
  889.7 25.3 %collective-permute-done.42 = bf16[192,6400]{1,0:T(8,128)(2,1)S(1)} collective-permute-done((bf16[192,6400]{1,0:T(8,128)(2,1)}, bf16[192,6400]{1,0:T(8,128)(2,1)S(1)}, u32[]{:S(2)}, u32[]{:S(2)}) %collective-permute-start.42) | collective-permute-done | bytes 2457632 | tf_op jit(solution)/shard_map/ppermute | solution.py:379
  968.3 20.8 %collective-permute-done.46 = bf16[24,6144]{1,0:T(8,128)(2,1)S(1)} collective-permute-done((bf16[24,6144]{1,0:T(8,128)(2,1)}, bf16[24,6144]{1,0:T(8,128)(2,1)S(1)}, u32[]{:S(2)}, u32[]{:S(2)}) %collective-permute-start.46) | collective-permute-done | bytes 294944 | tf_op jit(solution)/shard_map/ppermute | solution.py:379
  997.5 39.0 %shard_map.323 = (bf16[512,768]{1,0:T(8,128)(2,1)}, bf16[2048,1536]{1,0:T(8,128)(2,1)}) custom-call(bf16[512,768]{1,0:T(8,128)(2,1)} %slice.426.refs_0_, bf16[1024,1536]{1,0:T(8,128)(2,1)} %pad_maximum_fusion.5.refs_1_, bf16[1024,1536]{1,0:T(8,128)(2,1)} %collective-permute-done.17.refs_2_, bf16[512,768]{1,0:T(8,128)(2,1)} %get-tuple-element.311.refs_3_, ...), custom_call_target="tpu_custom_call" | custom-call | flops 1048576 | bytes 1048576 | tf_op jit(solution)/shard_map/pallas_call | solution.py:163
  1059.8 13.1 all-gather.14.cloned.1.call-done
  1096.3 32.8 %shard_map.324 = f32[192,6400]{1,0:T(8,128)} custom-call(s32[1,8192]{1,0:T(1,128)} %bitcast.470, bf16[192,8192]{1,0:T(8,128)(2,1)} %bitcast.410), custom_call_target="tpu_custom_call" | custom-call | flops 1048576 | bytes 1048576 | tf_op jit(solution)/shard_map/pallas_call | solution.py:304
  1203.2 18.5 %collective-permute-done.63 = bf16[24,6144]{1,0:T(8,128)(2,1)S(1)} collective-permute-done((bf16[24,6144]{1,0:T(8,128)(2,1)S(1)}, bf16[24,6144]{1,0:T(8,128)(2,1)S(1)}, u32[]{:S(2)}, u32[]{:S(2)}) %collective-permute-start.63) | collective-permute-done | bytes 294944 | tf_op jit(solution)/shard_map/ppermute | solution.py:379
  1235.4 13.9 %collective-permute-start.69 = (bf16[24,4480]{1,0:T(8,128)(2,1)S(1)}, bf16[24,4480]{1,0:T(8,128)(2,1)S(1)}, u32[]{:S(2)}, u32[]{:S(2)}) collective-permute-start(bf16[24,4480]{1,0:T(8,128)(2,1)S(1)} %get-tuple-element.488), channel_id=1, source_target_pairs={{0,1},{1,2},{2,3},{3,0},{4,5},{5,6},{6,7},{7,4},{8,9},{9,10},{10,1... | collective-permute-start | bytes 645128 | tf_op jit(solution)/shard_map/ppermute | solution.py:379
  1330.9 15.3 %fusion.191 = (bf16[6288,192]{0,1:T(8,128)(2,1)}, f32[6288,192]{0,1:T(8,128)}, f32[6288,192]{0,1:T(8,128)}, f32[6288,192]{0,1:T(8,128)}) fusion(f32[6288,192]{0,1:T(8,128)} %param.34, f32[]{:T(128)S(6)} %sub.146, f32[]{:T(128)S(6)} %sub.145, f32[]{:T(128)S(6)} %min.3, f32[192,6400]{1,0:T(8,128)} %shard_map.324, bf16[192,6400]{1,0:T(8,128)(2,1)} %copy-done.27, ...), kind=kLoop, calls=%fused_computation.528 | loop fusion | flops 25353216 | bytes 41048076 | tf_op jit(solution)/shard_map/convert_element_type | solution.py:1008
  (999 shorter events, 765.4 us)
Async XLA Ops:
  10.4 52.5 %all-to-all-start = ((bf16[32,6,24,128]{3,2,1,0:T(8,128)(2,1)}), bf16[32,6,24,128]{3,2,1,0:T(8,128)(2,1)S(1)}, u32[]{:S(2)}, u32[]{:S(2)}) async-start(bf16[32,6,24,128]{3,2,1,0:T(8,128)(2,1)} %bitcast.342), calls=%async_computation | async-start | bytes 2359296 | tf_op jit(solution)/shard_map/all_to_all | solution.py:669
  17.7 140.0 %all-gather.8.cloned.1.call-start = ((), (), s32[]{:S(2)}) async-start(), calls=%async_computation.8 | async-start | bytes 4866048 | tf_op jit(solution)/shard_map/all_gather | solution.py:704
  64.9 273.3 %all-gather.10.cloned.1.call-start = ((), (), s32[]{:S(2)}) async-start(), calls=%async_computation.9 | async-start | bytes 8515584 | tf_op jit(solution)/shard_map/all_gather | solution.py:704
  73.2 53.1 %collective-permute-start.10 = (bf16[24,6912]{1,0:T(8,128)(2,1)S(1)}, bf16[24,6912]{1,0:T(8,128)(2,1)}, u32[]{:S(2)}, u32[]{:S(2)}) collective-permute-start(bf16[24,6912]{1,0:T(8,128)(2,1)S(1)} %get-tuple-element.267), channel_id=1, source_target_pairs={{0,1},{1,2},{2,3},{3,0},{4,5},{5,6},{6,7},{7,4},{8,9},{9,10},{10,1... | collective-permute-start | bytes 995336 | tf_op jit(solution)/shard_map/ppermute | solution.py:379
  73.2 53.1 %collective-permute-start.8 = (bf16[24,6912]{1,0:T(8,128)(2,1)S(1)}, bf16[24,6912]{1,0:T(8,128)(2,1)}, u32[]{:S(2)}, u32[]{:S(2)}) collective-permute-start(bf16[24,6912]{1,0:T(8,128)(2,1)S(1)} %get-tuple-element.267), channel_id=1, source_target_pairs={{0,3},{1,0},{2,1},{3,2},{4,7},{5,4},{6,5},{7,6},{8,11},{9,8},{10,9... | collective-permute-start | bytes 995336 | tf_op jit(solution)/shard_map/ppermute | solution.py:379
  142.8 65.7 %all-to-all-start.1 = ((bf16[8,1024,192]{1,2,0:T(8,128)(2,1)}), bf16[8,1024,192]{1,2,0:T(8,128)(2,1)}, u32[]{:S(2)}, u32[]{:S(2)}) async-start(bf16[8,1024,192]{1,2,0:T(8,128)(2,1)} %copy.446), calls=%async_computation.1 | async-start | bytes 6291456 | tf_op jit(solution)/shard_map/all_to_all | solution.py:727
  147.3 355.6 %all-gather.12.cloned.1.call-start = ((), (), s32[]{:S(2)}) async-start(), calls=%async_computation.10 | async-start | bytes 10948608 | tf_op jit(solution)/shard_map/all_gather | solution.py:704
  208.5 79.8 %collective-permute-start.16 = (bf16[192,6400]{1,0:T(8,128)(2,1)}, bf16[192,6400]{1,0:T(8,128)(2,1)}, u32[]{:S(2)}, u32[]{:S(2)}) collective-permute-start(bf16[192,6400]{1,0:T(8,128)(2,1)} %pad.31), channel_id=1, source_target_pairs={{0,3},{1,0},{2,1},{3,2},{4,7},{5,4},{6,5},{7,6},{8,11},{9,8},{10,9... | collective-permute-start | bytes 7372808 | tf_op jit(solution)/shard_map/ppermute | solution.py:379
  213.8 58.0 %all-to-all-start.2 = ((bf16[4,256,192]{1,2,0:T(8,128)(2,1)}), bf16[4,256,192]{1,2,0:T(8,128)(2,1)S(1)}, u32[]{:S(2)}, u32[]{:S(2)}) async-start(bf16[4,256,192]{1,2,0:T(8,128)(2,1)} %bitcast.345), calls=%async_computation.2 | async-start | bytes 786432 | tf_op jit(solution)/shard_map/all_to_all | solution.py:721
  219.4 68.8 %collective-permute-start.13 = (bf16[512,1536]{1,0:T(8,128)(2,1)}, bf16[512,1536]{1,0:T(8,128)(2,1)}, u32[]{:S(2)}, u32[]{:S(2)}) collective-permute-start(bf16[512,1536]{1,0:T(8,128)(2,1)} %slice.427), channel_id=1, source_target_pairs={{0,8},{4,12},{8,0},{12,4},{16,24},{20,28},{24,16},{28,20},{1,9},{5... | collective-permute-start | bytes 4718600 | tf_op jit(solution)/shard_map/ppermute | solution.py:374
  220.1 68.1 %collective-permute-start.15 = (bf16[2,1,1,4,24,3456]{5,4,3,2,1,0:T(8,128)(2,1)}, bf16[2,1,1,4,24,3456]{5,4,3,2,1,0:T(8,128)(2,1)}, u32[]{:S(2)}, u32[]{:S(2)}) collective-permute-start(bf16[2,1,1,4,24,3456]{5,4,3,2,1,0:T(8,128)(2,1)} %maximum_select_fusion.6), channel_id=1, source_target_pairs={{0,8},{4,12},{8,0},{12,4},{16,24},{20,28},{24,16},{28,20},{1,9},{5... | collective-permute-start | bytes 3981320 | tf_op jit(solution)/shard_map/ppermute | solution.py:374
  307.1 68.8 %all-to-all-start.3 = ((bf16[8,1024,192]{1,2,0:T(8,128)(2,1)}), bf16[8,1024,192]{1,2,0:T(8,128)(2,1)}, u32[]{:S(2)}, u32[]{:S(2)}) async-start(bf16[8,1024,192]{1,2,0:T(8,128)(2,1)} %copy.449), calls=%async_computation.3 | async-start | bytes 6291456 | tf_op jit(solution)/shard_map/all_to_all | solution.py:760
  311.6 64.3 %collective-permute-start.19 = (bf16[192,6400]{1,0:T(8,128)(2,1)}, bf16[192,6400]{1,0:T(8,128)(2,1)}, u32[]{:S(2)}, u32[]{:S(2)}) collective-permute-start(bf16[192,6400]{1,0:T(8,128)(2,1)} %collective-permute-done.16), channel_id=1, source_target_pairs={{0,3},{1,0},{2,1},{3,2},{4,7},{5,4},{6,5},{7,6},{8,11},{9,8},{10,9... | collective-permute-start | bytes 7372808 | tf_op jit(solution)/shard_map/ppermute | solution.py:379
  414.0 55.3 %collective-permute-start.22 = (bf16[512,1536]{1,0:T(8,128)(2,1)}, bf16[512,1536]{1,0:T(8,128)(2,1)}, u32[]{:S(2)}, u32[]{:S(2)}) collective-permute-start(bf16[512,1536]{1,0:T(8,128)(2,1)} %convolution_convert_fusion.8), channel_id=1, source_target_pairs={{0,8},{4,12},{8,0},{12,4},{16,24},{20,28},{24,16},{28,20},{1,9},{5... | collective-permute-start | bytes 4718600 | tf_op jit(solution)/shard_map/ppermute | solution.py:374
  474.0 64.2 %collective-permute-start.30 = (bf16[192,6400]{1,0:T(8,128)(2,1)}, bf16[192,6400]{1,0:T(8,128)(2,1)}, u32[]{:S(2)}, u32[]{:S(2)}) collective-permute-start(bf16[192,6400]{1,0:T(8,128)(2,1)} %collective-permute-done.19), channel_id=1, source_target_pairs={{0,3},{1,0},{2,1},{3,2},{4,7},{5,4},{6,5},{7,6},{8,11},{9,8},{10,9... | collective-permute-start | bytes 7372808 | tf_op jit(solution)/shard_map/ppermute | solution.py:379
  694.2 57.4 %collective-permute-start.32 = (bf16[192,6400]{1,0:T(8,128)(2,1)}, bf16[192,6400]{1,0:T(8,128)(2,1)S(1)}, u32[]{:S(2)}, u32[]{:S(2)}) collective-permute-start(bf16[192,6400]{1,0:T(8,128)(2,1)} %get-tuple-element.358), channel_id=1, source_target_pairs={{0,1},{1,2},{2,3},{3,0},{4,5},{5,6},{6,7},{7,4},{8,9},{9,10},{10,1... | collective-permute-start | bytes 7372808 | tf_op jit(solution)/shard_map/ppermute | solution.py:379
  762.4 57.3 %collective-permute-start.38 = (bf16[192,6400]{1,0:T(8,128)(2,1)}, bf16[192,6400]{1,0:T(8,128)(2,1)}, u32[]{:S(2)}, u32[]{:S(2)}) collective-permute-start(bf16[192,6400]{1,0:T(8,128)(2,1)} %add_convert_fusion.6), channel_id=1, source_target_pairs={{0,1},{1,2},{2,3},{3,0},{4,5},{5,6},{6,7},{7,4},{8,9},{9,10},{10,1... | collective-permute-start | bytes 7372808 | tf_op jit(solution)/shard_map/ppermute | solution.py:379
  809.1 52.7 %collective-permute-start.40 = (bf16[1,1,96,3072]{3,2,1,0:T(8,128)(2,1)}, bf16[1,1,96,3072]{3,2,1,0:T(8,128)(2,1)}, u32[]{:S(2)}, u32[]{:S(2)}) collective-permute-start(bf16[1,1,96,3072]{3,2,1,0:T(8,128)(2,1)} %constant_dynamic-slice_fusion.37), channel_id=1, source_target_pairs={{0,16},{4,20},{8,24},{12,28},{16,0},{20,4},{24,8},{28,12},{1,17},{... | collective-permute-start | bytes 1769480 | tf_op jit(solution)/shard_map/ppermute | solution.py:374
  858.6 56.5 %collective-permute-start.42 = (bf16[192,6400]{1,0:T(8,128)(2,1)}, bf16[192,6400]{1,0:T(8,128)(2,1)S(1)}, u32[]{:S(2)}, u32[]{:S(2)}) collective-permute-start(bf16[192,6400]{1,0:T(8,128)(2,1)} %add_convert_fusion.5), channel_id=1, source_target_pairs={{0,1},{1,2},{2,3},{3,0},{4,5},{5,6},{6,7},{7,4},{8,9},{9,10},{10,1... | collective-permute-start | bytes 7372808 | tf_op jit(solution)/shard_map/ppermute | solution.py:379
  952.9 87.4 %collective-permute-start.48 = (bf16[2,1,96,3072]{3,2,1,0:T(8,128)(2,1)}, bf16[2,1,96,3072]{3,2,1,0:T(8,128)(2,1)}, u32[]{:S(2)}, u32[]{:S(2)}) collective-permute-start(bf16[2,1,96,3072]{3,2,1,0:T(8,128)(2,1)} %constant_dynamic-slice_fusion.23), channel_id=1, source_target_pairs={{0,8},{4,12},{8,0},{12,4},{16,24},{20,28},{24,16},{28,20},{1,9},{5... | collective-permute-start | bytes 3538952 | tf_op jit(solution)/shard_map/ppermute | solution.py:374
  953.7 86.6 %collective-permute-start.49 = (bf16[1,2,96,3072]{3,2,1,0:T(8,128)(2,1)}, bf16[1,2,96,3072]{3,2,1,0:T(8,128)(2,1)}, u32[]{:S(2)}, u32[]{:S(2)}) collective-permute-start(bf16[1,2,96,3072]{3,2,1,0:T(8,128)(2,1)} %constant_dynamic-slice_fusion.22), channel_id=1, source_target_pairs={{0,16},{4,20},{8,24},{12,28},{16,0},{20,4},{24,8},{28,12},{1,17},{... | collective-permute-start | bytes 3538952 | tf_op jit(solution)/shard_map/ppermute | solution.py:374
  955.2 85.1 %collective-permute-start.50 = (bf16[2,1,96,3072]{3,2,1,0:T(8,128)(2,1)}, bf16[2,1,96,3072]{3,2,1,0:T(8,128)(2,1)}, u32[]{:S(2)}, u32[]{:S(2)}) collective-permute-start(bf16[2,1,96,3072]{3,2,1,0:T(8,128)(2,1)} %constant_dynamic-slice_fusion.19), channel_id=1, source_target_pairs={{0,8},{4,12},{8,0},{12,4},{16,24},{20,28},{24,16},{28,20},{1,9},{5... | collective-permute-start | bytes 3538952 | tf_op jit(solution)/shard_map/ppermute | solution.py:374
  956.4 83.9 %collective-permute-start.51 = (bf16[1,2,96,3072]{3,2,1,0:T(8,128)(2,1)}, bf16[1,2,96,3072]{3,2,1,0:T(8,128)(2,1)}, u32[]{:S(2)}, u32[]{:S(2)}) collective-permute-start(bf16[1,2,96,3072]{3,2,1,0:T(8,128)(2,1)} %constant_dynamic-slice_fusion.18), channel_id=1, source_target_pairs={{0,16},{4,20},{8,24},{12,28},{16,0},{20,4},{24,8},{28,12},{1,17},{... | collective-permute-start | bytes 3538952 | tf_op jit(solution)/shard_map/ppermute | solution.py:374
  965.4 107.5 %all-gather.14.cloned.1.call-start = ((), (), s32[]{:S(2)}) async-start(), calls=%async_computation.11 | async-start | bytes 3538944 | tf_op jit(solution)/shard_map/all_gather | solution.py:915
  (299 other events, 5604.5 us)
Sparse Core Ops, SparseCore 0:
  65.1 92.5 all-gather.7
  161.0 151.9 all-gather.9
  316.4 156.2 all-gather.11
  1040.4 32.4 all-gather.13

commit v5 on v4

--- a/solution.py
+++ b/solution.py
@@ -673,15 +673,20 @@
         for n in range(narrow_count):
             base = w // narrow_count * narrow_count
             exchange.append((w * narrow_count + n, (base + n) * narrow_count + w % narrow_count))
+    slots = narrow_pos * dec_rows + jnp.arange(dec_rows)
+    slot_mask = lax.dynamic_slice_in_dim(loss_mask[0], narrow_pos * dec_rows, dec_rows)
+    slot_counted = ((slots < target_lengths[0]) & (slot_mask == 1)).astype(jnp.int32)
     whole_ids = lax.ppermute(
-        jnp.concatenate([patch_rows, patch_cols, input_ids, target_ids]), BOTH, exchange
+        jnp.concatenate([patch_rows, patch_cols, input_ids, target_ids, slot_counted]),
+        BOTH,
+        exchange,
     )
     rows_ids, cols_ids = whole_ids[:enc_rows], whole_ids[enc_rows : 2 * enc_rows]
-    token_ids = whole_ids[2 * enc_rows :].reshape(2, dec_rows)
+    token_ids = whole_ids[2 * enc_rows :].reshape(3, dec_rows)
     every_token = from_narrow(token_ids)
     every_token = every_token.reshape((1,) * wide_bits() + every_token.shape)
     every_token = join_wide(every_token, split_orders()[0] + [0])
-    every_token = every_token.reshape(wide_count, narrow_count, 2, dec_rows)
+    every_token = every_token.reshape(wide_count, narrow_count, 3, dec_rows)
     pieces, patches, every_token = tie(pieces, patches, every_token)
     layer_tokens = lax.dynamic_index_in_dim(every_token, narrow_pos, 1, keepdims=False)
     layer_targets = layer_tokens[:, 1].reshape(-1)
@@ -763,17 +768,9 @@
     enc_mixed, enc_total = attend(enc_query, enc_keys, None)
     enc_mixed = step(enc_mixed, flow_weights)
     take(PERMUTED, flow_weights.drain())
-    enc_mixed, target_lengths, loss_mask = tie(enc_mixed, target_lengths, loss_mask)
-    screens_info = lax.all_gather(
-        jnp.concatenate([target_lengths[:, None], loss_mask], axis=1), "wide", axis=0, tiled=True
-    )
-    counted = (
-        (jnp.arange(TGT)[None, :] < screens_info[:, :1]) & (screens_info[:, 1:] == 1)
-    ).astype(jnp.float32)
+    counted = every_token[:, :, 2].astype(jnp.float32)
     tokens_counted = jnp.maximum(jnp.sum(counted), 1.0)
-    row_counted = lax.dynamic_index_in_dim(
-        counted.reshape(screen_sets, narrow_count, TGT), narrow_pos, 1, keepdims=False
-    ).reshape(-1)
+    row_counted = layer_tokens[:, 2].reshape(-1).astype(jnp.float32)
     own_counted = lax.dynamic_slice_in_dim(row_counted, wide_pos * dec_rows, dec_rows)
 
     enc_one = enc_zero + dot_nn(enc_mixed, weights[2])

time: 1400 us -> 1400 us (level)
  starting transfers between devices: 171 us -> 200 us
  Pallas kernels: 245 us -> 226 us
    ppermute x27, starting transfers between devices: 82.1 us -> 110 us  [shift(): lax.ppermute(values, 'narrow', [(i, (i + step) % count) for i in range(co...]
    pallas_call x1, Pallas kernels: 60.5 us -> 46.2 us  [head_forward(): pl.pallas_call(lambda *refs: head_kernel(vocab, tile, *refs), grid_spec=p...]
    unnamed x498 -> x504, local copies, waits for them, and re-layouts: 60.3 us -> 59.9 us
  transfers between devices with their start and end apart: 90 -> 90, of which waited for: 40 -> 39; matrix products, arithmetic and copies ran while one was open for 33% -> 33% of each run, Pallas kernels for 13% -> 13%
where the time goes in v5:
time: 1400 us; the launch traced here: 1390 us
  waiting for transfers between devices  341 us (24%)
  matrix products  243 us (17%)
  Pallas kernels  226 us (16%)
  starting transfers between devices  200 us (14%)
  other arithmetic  172 us (12%)
  local copies, waits for them, and re-layouts  164 us (12%)
  between operations  34.5 us (2%)
    ppermute x27, waiting for transfers between devices, shift(): lax.ppermute(values, 'narrow', [(i, (i + step) % count) for i in range(co...  133 us
    dot_general x17, matrix products, dot_nn(): lax.dot_general(left, right, (((1,), (0,)), ((), ())), preferred_element_...  131 us
    ppermute x49, waiting for transfers between devices, swap(): return lax.ppermute(values, 'wide', [(w, w ^ bit) for w in range(count)])  131 us
    ppermute x27, starting transfers between devices, shift(): lax.ppermute(values, 'narrow', [(i, (i + step) % count) for i in range(co...  110 us
    pallas_call x3, Pallas kernels, attend_back(): pl.pallas_call(lambda *refs: attend_back_kernel(positions is not None, le...  76.4 us
    unnamed x504, local copies, waits for them, and re-layouts  59.9 us
    convert_element_type x43, other arithmetic, low(): return values.astype(jnp.bfloat16)  54.1 us
    ppermute x49, starting transfers between devices, swap(): return lax.ppermute(values, 'wide', [(w, w ^ bit) for w in range(count)])  49.5 us
  transfers between devices with their start and end apart: 90, of which 39 were waited for; matrix products, arithmetic and copies ran while one was open for 33% of the time, Pallas kernels for 13%

profile of v5, /device:TPU:0, one launch (start us, length us, event | category | flops | bytes accessed | tf_op | source)
XLA Modules:
  0.0 1388.5 jit_solution(4201149655412224977)
XLA Ops:
  19.9 22.6 %collective-permute-start.1 = (s32[3,256]{1,0:T(4,128)S(1)}, s32[3,256]{1,0:T(4,128)S(1)}, u32[]{:S(2)}, u32[]{:S(2)}) collective-permute-start(s32[3,256]{1,0:T(4,128)S(1)} %slice.314), channel_id=1, source_target_pairs={{0,3},{1,0},{2,1},{3,2},{4,7},{5,4},{6,5},{7,6},{8,11},{9,8},{10,9... | collective-permute-start | bytes 9224 | tf_op jit(solution)/shard_map/ppermute | solution.py:379
  77.9 41.5 %fusion.5 = bf16[8192,192]{0,1:T(8,128)(2,1)S(1)} fusion(s32[8192]{0:T(1024)S(1)} %bitcast.483, f32[6288,192]{0,1:T(8,128)} %param.34), kind=kOutput, calls=%fused_computation.10 | convolution fusion | flops 19834630144 | bytes 8007680 | tf_op jit(solution)/shard_map/dot_general | solution.py:22
  176.5 32.1 %all-to-all-done.1 = bf16[8,1024,192]{1,2,0:T(8,128)(2,1)} async-done(((bf16[8,1024,192]{1,2,0:T(8,128)(2,1)}), bf16[8,1024,192]{1,2,0:T(8,128)(2,1)}, u32[]{:S(2)}, u32[]{:S(2)}) %all-to-all-start.1) | async-done | bytes 3145760 | tf_op jit(solution)/shard_map/all_to_all | solution.py:732
  222.2 41.5 %fusion.4 = bf16[8192,192]{0,1:T(8,128)(2,1)S(1)} fusion(s32[8192]{0:T(1024)S(1)} %bitcast.496, f32[6288,192]{0,1:T(8,128)} %param.34), kind=kOutput, calls=%fused_computation.9 | convolution fusion | flops 19834630144 | bytes 8007680 | tf_op jit(solution)/shard_map/dot_general | solution.py:22
  272.2 15.8 %collective-permute-done.15 = bf16[2,1,1,4,24,3456]{5,4,3,2,1,0:T(8,128)(2,1)} collective-permute-done((bf16[2,1,1,4,24,3456]{5,4,3,2,1,0:T(8,128)(2,1)}, bf16[2,1,1,4,24,3456]{5,4,3,2,1,0:T(8,128)(2,1)}, u32[]{:S(2)}, u32[]{:S(2)}) %collective-permute-start.15) | collective-permute-done | bytes 1327136 | tf_op jit(solution)/shard_map/ppermute | solution.py:374
  316.1 22.1 %shard_map.316 = (bf16[512,768]{1,0:T(8,128)(2,1)}, f32[512,768]{1,0:T(8,128)}) custom-call(bf16[512,768]{1,0:T(8,128)(2,1)} %slice.417.refs_0_, bf16[1024,1536]{1,0:T(8,128)(2,1)} %pad_maximum_fusion.5.refs_1_, bf16[1024,1536]{1,0:T(8,128)(2,1)} %collective-permute-done.17.refs_2_), custom_call_target="tpu_custom_call" | custom-call | flops 1048576 | bytes 1048576 | tf_op jit(solution)/shard_map/pallas_call | solution.py:88
  361.1 14.9 %collective-permute-done.19 = bf16[192,6400]{1,0:T(8,128)(2,1)} collective-permute-done((bf16[192,6400]{1,0:T(8,128)(2,1)}, bf16[192,6400]{1,0:T(8,128)(2,1)}, u32[]{:S(2)}, u32[]{:S(2)}) %collective-permute-start.19) | collective-permute-done | bytes 2457632 | tf_op jit(solution)/shard_map/ppermute | solution.py:379
  387.5 17.1 %collective-permute-done.20 = bf16[256,1536]{1,0:T(8,128)(2,1)S(1)} collective-permute-done((bf16[256,1536]{1,0:T(8,128)(2,1)S(1)}, bf16[256,1536]{1,0:T(8,128)(2,1)S(1)}, u32[]{:S(2)}, u32[]{:S(2)}) %collective-permute-start.20) | collective-permute-done | bytes 786464 | tf_op jit(solution)/shard_map/ppermute | solution.py:374
  416.7 19.2 %all-to-all-done.4 = bf16[4,256,192]{1,2,0:T(8,128)(2,1)S(1)} async-done(((bf16[4,256,192]{1,2,0:T(8,128)(2,1)}), bf16[4,256,192]{1,2,0:T(8,128)(2,1)S(1)}, u32[]{:S(2)}, u32[]{:S(2)}) %all-to-all-start.4) | async-done | bytes 393248 | tf_op jit(solution)/shard_map/all_to_all | solution.py:726
  451.9 17.5 %collective-permute-done.22 = bf16[512,1536]{1,0:T(8,128)(2,1)} collective-permute-done((bf16[512,1536]{1,0:T(8,128)(2,1)}, bf16[512,1536]{1,0:T(8,128)(2,1)}, u32[]{:S(2)}, u32[]{:S(2)}) %collective-permute-start.22) | collective-permute-done | bytes 1572896 | tf_op jit(solution)/shard_map/ppermute | solution.py:374
  543.4 46.2 %shard_map.319 = (f32[2048,768]{1,0:T(8,128)}, bf16[2048,6400]{1,0:T(8,128)(2,1)}, f32[2048,128]{1,0:T(8,128)}) custom-call(s32[8]{0:T(128)} %convert_element_type.643.refs_0_, bf16[2048,768]{1,0:T(8,128)(2,1)} %pad_maximum_fusion.7.refs_1_, bf16[768,6400]{1,0:T(8,128)(2,1)} %pad_maximum_fusion.refs_2_), custom_call_target="tpu_custom_call" | custom-call | flops 1048576 | bytes 1048576 | tf_op jit(solution)/shard_map/pallas_call | solution.py:217
  624.1 25.5 %shard_map.320 = bf16[768,6400]{1,0:T(8,128)(2,1)} custom-call(s32[8]{0:T(128)} %convert_element_type.643.refs_0_, bf16[2048,768]{1,0:T(8,128)(2,1)} %pad_maximum_fusion.7.refs_1_, bf16[2048,6400]{1,0:T(8,128)(2,1)} %get-tuple-element.339.refs_2_, f32[2048,128]{1,0:T(8,128)} %maximum_maximum_fusion.refs_3_), custom_call_target="tpu_custom_call" | custom-call | flops 1048576 | bytes 1048576 | tf_op jit(solution)/shard_map/pallas_call | solution.py:270
  671.6 28.9 %collective-permute-start.32 = (bf16[192,6400]{1,0:T(8,128)(2,1)}, bf16[192,6400]{1,0:T(8,128)(2,1)S(1)}, u32[]{:S(2)}, u32[]{:S(2)}) collective-permute-start(bf16[192,6400]{1,0:T(8,128)(2,1)} %get-tuple-element.352), channel_id=1, source_target_pairs={{0,1},{1,2},{2,3},{3,0},{4,5},{5,6},{6,7},{7,4},{8,9},{9,10},{10,1... | collective-permute-start | bytes 7372808 | tf_op jit(solution)/shard_map/ppermute | solution.py:379
  717.0 23.4 %shard_map.321 = (bf16[256,768]{1,0:T(8,128)(2,1)}, bf16[2048,1536]{1,0:T(8,128)(2,1)}) custom-call(bf16[256,768]{1,0:T(8,128)(2,1)} %convolution_convert_fusion.20.refs_0_, bf16[1024,1536]{1,0:T(8,128)(2,1)} %copy-done.4, bf16[1024,1536]{1,0:T(8,128)(2,1)} %collective-permute-done.23.refs_2_, bf16[256,768]{1,0:T(8,128)(2,1)} %get-tuple-element.337.refs_3_, ...), custom_call_target="tpu_custom_call" | custom-call | flops 1048576 | bytes 1048576 | tf_op jit(solution)/shard_map/pallas_call | solution.py:163
  740.4 17.3 %collective-permute-done.32 = bf16[192,6400]{1,0:T(8,128)(2,1)S(1)} collective-permute-done((bf16[192,6400]{1,0:T(8,128)(2,1)}, bf16[192,6400]{1,0:T(8,128)(2,1)S(1)}, u32[]{:S(2)}, u32[]{:S(2)}) %collective-permute-start.32) | collective-permute-done | bytes 2457632 | tf_op jit(solution)/shard_map/ppermute | solution.py:379
  779.7 14.0 %shard_map.322 = (bf16[256,768]{1,0:T(8,128)(2,1)}, bf16[1024,1536]{1,0:T(8,128)(2,1)}) custom-call(s32[1,256]{1,0:T(1,128)} %iota_add_fusion.1.refs_0_, s32[1024,1]{1,0:T(8,128)} %copy.416.refs_1_, bf16[256,768]{1,0:T(8,128)(2,1)} %slice.422.refs_2_, bf16[512,1536]{1,0:T(8,128)(2,1)} %copy-done.8, bf16[512,1536]{1,0:T(8,128)(2,1)} %collective-permute-done.21.refs_4_, ...), custom_call_target="tpu_custom_call" | custom-call | flops 1048576 | bytes 1048576 | tf_op jit(solution)/shard_map/pallas_call | solution.py:163
  895.9 25.4 %collective-permute-done.42 = bf16[192,6400]{1,0:T(8,128)(2,1)S(1)} collective-permute-done((bf16[192,6400]{1,0:T(8,128)(2,1)}, bf16[192,6400]{1,0:T(8,128)(2,1)S(1)}, u32[]{:S(2)}, u32[]{:S(2)}) %collective-permute-start.42) | collective-permute-done | bytes 2457632 | tf_op jit(solution)/shard_map/ppermute | solution.py:379
  974.5 20.8 %collective-permute-done.46 = bf16[24,6144]{1,0:T(8,128)(2,1)S(1)} collective-permute-done((bf16[24,6144]{1,0:T(8,128)(2,1)}, bf16[24,6144]{1,0:T(8,128)(2,1)S(1)}, u32[]{:S(2)}, u32[]{:S(2)}) %collective-permute-start.46) | collective-permute-done | bytes 294944 | tf_op jit(solution)/shard_map/ppermute | solution.py:379
  1003.7 39.0 %shard_map.323 = (bf16[512,768]{1,0:T(8,128)(2,1)}, bf16[2048,1536]{1,0:T(8,128)(2,1)}) custom-call(bf16[512,768]{1,0:T(8,128)(2,1)} %slice.417.refs_0_, bf16[1024,1536]{1,0:T(8,128)(2,1)} %pad_maximum_fusion.5.refs_1_, bf16[1024,1536]{1,0:T(8,128)(2,1)} %collective-permute-done.17.refs_2_, bf16[512,768]{1,0:T(8,128)(2,1)} %get-tuple-element.305.refs_3_, ...), custom_call_target="tpu_custom_call" | custom-call | flops 1048576 | bytes 1048576 | tf_op jit(solution)/shard_map/pallas_call | solution.py:163
  1066.0 13.1 all-gather.13.cloned.1.call-done
  1102.5 32.9 %shard_map.324 = f32[192,6400]{1,0:T(8,128)} custom-call(s32[1,8192]{1,0:T(1,128)} %bitcast.484, bf16[192,8192]{1,0:T(8,128)(2,1)} %bitcast.422), custom_call_target="tpu_custom_call" | custom-call | flops 1048576 | bytes 1048576 | tf_op jit(solution)/shard_map/pallas_call | solution.py:304
  1209.4 18.5 %collective-permute-done.63 = bf16[24,6144]{1,0:T(8,128)(2,1)S(1)} collective-permute-done((bf16[24,6144]{1,0:T(8,128)(2,1)S(1)}, bf16[24,6144]{1,0:T(8,128)(2,1)S(1)}, u32[]{:S(2)}, u32[]{:S(2)}) %collective-permute-start.63) | collective-permute-done | bytes 294944 | tf_op jit(solution)/shard_map/ppermute | solution.py:379
  1241.6 13.9 %collective-permute-start.69 = (bf16[24,4480]{1,0:T(8,128)(2,1)S(1)}, bf16[24,4480]{1,0:T(8,128)(2,1)S(1)}, u32[]{:S(2)}, u32[]{:S(2)}) collective-permute-start(bf16[24,4480]{1,0:T(8,128)(2,1)S(1)} %get-tuple-element.482), channel_id=1, source_target_pairs={{0,1},{1,2},{2,3},{3,0},{4,5},{5,6},{6,7},{7,4},{8,9},{9,10},{10,1... | collective-permute-start | bytes 645128 | tf_op jit(solution)/shard_map/ppermute | solution.py:379
  1337.1 15.3 %fusion.190 = (bf16[6288,192]{0,1:T(8,128)(2,1)}, f32[6288,192]{0,1:T(8,128)}, f32[6288,192]{0,1:T(8,128)}, f32[6288,192]{0,1:T(8,128)}) fusion(f32[6288,192]{0,1:T(8,128)} %param.34, f32[]{:T(128)S(6)} %sub.146, f32[]{:T(128)S(6)} %sub.145, f32[]{:T(128)S(6)} %min.3, f32[192,6400]{1,0:T(8,128)} %shard_map.324, bf16[192,6400]{1,0:T(8,128)(2,1)} %copy-done.27, ...), kind=kLoop, calls=%fused_computation.540 | loop fusion | flops 25353216 | bytes 41048076 | tf_op jit(solution)/shard_map/convert_element_type | solution.py:1005
  (1000 shorter events, 775.7 us)
Async XLA Ops:
  10.4 52.6 %all-to-all-start = ((bf16[32,6,24,128]{3,2,1,0:T(8,128)(2,1)}), bf16[32,6,24,128]{3,2,1,0:T(8,128)(2,1)S(1)}, u32[]{:S(2)}, u32[]{:S(2)}) async-start(bf16[32,6,24,128]{3,2,1,0:T(8,128)(2,1)} %bitcast.353), calls=%async_computation | async-start | bytes 2359296 | tf_op jit(solution)/shard_map/all_to_all | solution.py:669
  17.7 140.0 %all-gather.7.cloned.1.call-start = ((), (), s32[]{:S(2)}) async-start(), calls=%async_computation.8 | async-start | bytes 4866048 | tf_op jit(solution)/shard_map/all_gather | solution.py:709
  65.0 273.1 %all-gather.9.cloned.1.call-start = ((), (), s32[]{:S(2)}) async-start(), calls=%async_computation.9 | async-start | bytes 8515584 | tf_op jit(solution)/shard_map/all_gather | solution.py:709
  73.3 53.1 %collective-permute-start.10 = (bf16[24,6912]{1,0:T(8,128)(2,1)S(1)}, bf16[24,6912]{1,0:T(8,128)(2,1)}, u32[]{:S(2)}, u32[]{:S(2)}) collective-permute-start(bf16[24,6912]{1,0:T(8,128)(2,1)S(1)} %get-tuple-element.264), channel_id=1, source_target_pairs={{0,1},{1,2},{2,3},{3,0},{4,5},{5,6},{6,7},{7,4},{8,9},{9,10},{10,1... | collective-permute-start | bytes 995336 | tf_op jit(solution)/shard_map/ppermute | solution.py:379
  73.3 53.1 %collective-permute-start.8 = (bf16[24,6912]{1,0:T(8,128)(2,1)S(1)}, bf16[24,6912]{1,0:T(8,128)(2,1)}, u32[]{:S(2)}, u32[]{:S(2)}) collective-permute-start(bf16[24,6912]{1,0:T(8,128)(2,1)S(1)} %get-tuple-element.264), channel_id=1, source_target_pairs={{0,3},{1,0},{2,1},{3,2},{4,7},{5,4},{6,5},{7,6},{8,11},{9,8},{10,9... | collective-permute-start | bytes 995336 | tf_op jit(solution)/shard_map/ppermute | solution.py:379
  142.9 65.7 %all-to-all-start.1 = ((bf16[8,1024,192]{1,2,0:T(8,128)(2,1)}), bf16[8,1024,192]{1,2,0:T(8,128)(2,1)}, u32[]{:S(2)}, u32[]{:S(2)}) async-start(bf16[8,1024,192]{1,2,0:T(8,128)(2,1)} %copy.399), calls=%async_computation.1 | async-start | bytes 6291456 | tf_op jit(solution)/shard_map/all_to_all | solution.py:732
  147.4 347.2 %all-gather.11.cloned.1.call-start = ((), (), s32[]{:S(2)}) async-start(), calls=%async_computation.10 | async-start | bytes 10948608 | tf_op jit(solution)/shard_map/all_gather | solution.py:709
  208.6 79.4 %collective-permute-start.16 = (bf16[192,6400]{1,0:T(8,128)(2,1)}, bf16[192,6400]{1,0:T(8,128)(2,1)}, u32[]{:S(2)}, u32[]{:S(2)}) collective-permute-start(bf16[192,6400]{1,0:T(8,128)(2,1)} %pad.31), channel_id=1, source_target_pairs={{0,3},{1,0},{2,1},{3,2},{4,7},{5,4},{6,5},{7,6},{8,11},{9,8},{10,9... | collective-permute-start | bytes 7372808 | tf_op jit(solution)/shard_map/ppermute | solution.py:379
  214.3 57.8 %all-to-all-start.2 = ((bf16[4,256,192]{1,2,0:T(8,128)(2,1)}), bf16[4,256,192]{1,2,0:T(8,128)(2,1)S(1)}, u32[]{:S(2)}, u32[]{:S(2)}) async-start(bf16[4,256,192]{1,2,0:T(8,128)(2,1)} %bitcast.356), calls=%async_computation.2 | async-start | bytes 786432 | tf_op jit(solution)/shard_map/all_to_all | solution.py:726
  219.6 68.4 %collective-permute-start.13 = (bf16[512,1536]{1,0:T(8,128)(2,1)}, bf16[512,1536]{1,0:T(8,128)(2,1)}, u32[]{:S(2)}, u32[]{:S(2)}) collective-permute-start(bf16[512,1536]{1,0:T(8,128)(2,1)} %slice.419), channel_id=1, source_target_pairs={{0,8},{4,12},{8,0},{12,4},{16,24},{20,28},{24,16},{28,20},{1,9},{5... | collective-permute-start | bytes 4718600 | tf_op jit(solution)/shard_map/ppermute | solution.py:374
  220.2 67.8 %collective-permute-start.15 = (bf16[2,1,1,4,24,3456]{5,4,3,2,1,0:T(8,128)(2,1)}, bf16[2,1,1,4,24,3456]{5,4,3,2,1,0:T(8,128)(2,1)}, u32[]{:S(2)}, u32[]{:S(2)}) collective-permute-start(bf16[2,1,1,4,24,3456]{5,4,3,2,1,0:T(8,128)(2,1)} %maximum_select_fusion.6), channel_id=1, source_target_pairs={{0,8},{4,12},{8,0},{12,4},{16,24},{20,28},{24,16},{28,20},{1,9},{5... | collective-permute-start | bytes 3981320 | tf_op jit(solution)/shard_map/ppermute | solution.py:374
  307.0 68.9 %all-to-all-start.3 = ((bf16[8,1024,192]{1,2,0:T(8,128)(2,1)}), bf16[8,1024,192]{1,2,0:T(8,128)(2,1)}, u32[]{:S(2)}, u32[]{:S(2)}) async-start(bf16[8,1024,192]{1,2,0:T(8,128)(2,1)} %copy.402), calls=%async_computation.3 | async-start | bytes 6291456 | tf_op jit(solution)/shard_map/all_to_all | solution.py:765
  311.5 64.4 %collective-permute-start.19 = (bf16[192,6400]{1,0:T(8,128)(2,1)}, bf16[192,6400]{1,0:T(8,128)(2,1)}, u32[]{:S(2)}, u32[]{:S(2)}) collective-permute-start(bf16[192,6400]{1,0:T(8,128)(2,1)} %collective-permute-done.16), channel_id=1, source_target_pairs={{0,3},{1,0},{2,1},{3,2},{4,7},{5,4},{6,5},{7,6},{8,11},{9,8},{10,9... | collective-permute-start | bytes 7372808 | tf_op jit(solution)/shard_map/ppermute | solution.py:379
  414.1 55.3 %collective-permute-start.22 = (bf16[512,1536]{1,0:T(8,128)(2,1)}, bf16[512,1536]{1,0:T(8,128)(2,1)}, u32[]{:S(2)}, u32[]{:S(2)}) collective-permute-start(bf16[512,1536]{1,0:T(8,128)(2,1)} %convolution_convert_fusion.8), channel_id=1, source_target_pairs={{0,8},{4,12},{8,0},{12,4},{16,24},{20,28},{24,16},{28,20},{1,9},{5... | collective-permute-start | bytes 4718600 | tf_op jit(solution)/shard_map/ppermute | solution.py:374
  475.6 56.9 %collective-permute-start.30 = (bf16[192,6400]{1,0:T(8,128)(2,1)}, bf16[192,6400]{1,0:T(8,128)(2,1)}, u32[]{:S(2)}, u32[]{:S(2)}) collective-permute-start(bf16[192,6400]{1,0:T(8,128)(2,1)} %collective-permute-done.19), channel_id=1, source_target_pairs={{0,3},{1,0},{2,1},{3,2},{4,7},{5,4},{6,5},{7,6},{8,11},{9,8},{10,9... | collective-permute-start | bytes 7372808 | tf_op jit(solution)/shard_map/ppermute | solution.py:379
  671.6 86.2 %collective-permute-start.32 = (bf16[192,6400]{1,0:T(8,128)(2,1)}, bf16[192,6400]{1,0:T(8,128)(2,1)S(1)}, u32[]{:S(2)}, u32[]{:S(2)}) collective-permute-start(bf16[192,6400]{1,0:T(8,128)(2,1)} %get-tuple-element.352), channel_id=1, source_target_pairs={{0,1},{1,2},{2,3},{3,0},{4,5},{5,6},{6,7},{7,4},{8,9},{9,10},{10,1... | collective-permute-start | bytes 7372808 | tf_op jit(solution)/shard_map/ppermute | solution.py:379
  768.5 57.3 %collective-permute-start.38 = (bf16[192,6400]{1,0:T(8,128)(2,1)}, bf16[192,6400]{1,0:T(8,128)(2,1)}, u32[]{:S(2)}, u32[]{:S(2)}) collective-permute-start(bf16[192,6400]{1,0:T(8,128)(2,1)} %add_convert_fusion.6), channel_id=1, source_target_pairs={{0,1},{1,2},{2,3},{3,0},{4,5},{5,6},{6,7},{7,4},{8,9},{9,10},{10,1... | collective-permute-start | bytes 7372808 | tf_op jit(solution)/shard_map/ppermute | solution.py:379
  815.3 52.7 %collective-permute-start.40 = (bf16[1,1,96,3072]{3,2,1,0:T(8,128)(2,1)}, bf16[1,1,96,3072]{3,2,1,0:T(8,128)(2,1)}, u32[]{:S(2)}, u32[]{:S(2)}) collective-permute-start(bf16[1,1,96,3072]{3,2,1,0:T(8,128)(2,1)} %constant_dynamic-slice_fusion.37), channel_id=1, source_target_pairs={{0,16},{4,20},{8,24},{12,28},{16,0},{20,4},{24,8},{28,12},{1,17},{... | collective-permute-start | bytes 1769480 | tf_op jit(solution)/shard_map/ppermute | solution.py:374
  864.7 56.5 %collective-permute-start.42 = (bf16[192,6400]{1,0:T(8,128)(2,1)}, bf16[192,6400]{1,0:T(8,128)(2,1)S(1)}, u32[]{:S(2)}, u32[]{:S(2)}) collective-permute-start(bf16[192,6400]{1,0:T(8,128)(2,1)} %add_convert_fusion.5), channel_id=1, source_target_pairs={{0,1},{1,2},{2,3},{3,0},{4,5},{5,6},{6,7},{7,4},{8,9},{9,10},{10,1... | collective-permute-start | bytes 7372808 | tf_op jit(solution)/shard_map/ppermute | solution.py:379
  959.1 87.4 %collective-permute-start.48 = (bf16[2,1,96,3072]{3,2,1,0:T(8,128)(2,1)}, bf16[2,1,96,3072]{3,2,1,0:T(8,128)(2,1)}, u32[]{:S(2)}, u32[]{:S(2)}) collective-permute-start(bf16[2,1,96,3072]{3,2,1,0:T(8,128)(2,1)} %constant_dynamic-slice_fusion.23), channel_id=1, source_target_pairs={{0,8},{4,12},{8,0},{12,4},{16,24},{20,28},{24,16},{28,20},{1,9},{5... | collective-permute-start | bytes 3538952 | tf_op jit(solution)/shard_map/ppermute | solution.py:374
  959.9 86.6 %collective-permute-start.49 = (bf16[1,2,96,3072]{3,2,1,0:T(8,128)(2,1)}, bf16[1,2,96,3072]{3,2,1,0:T(8,128)(2,1)}, u32[]{:S(2)}, u32[]{:S(2)}) collective-permute-start(bf16[1,2,96,3072]{3,2,1,0:T(8,128)(2,1)} %constant_dynamic-slice_fusion.22), channel_id=1, source_target_pairs={{0,16},{4,20},{8,24},{12,28},{16,0},{20,4},{24,8},{28,12},{1,17},{... | collective-permute-start | bytes 3538952 | tf_op jit(solution)/shard_map/ppermute | solution.py:374
  961.4 85.2 %collective-permute-start.50 = (bf16[2,1,96,3072]{3,2,1,0:T(8,128)(2,1)}, bf16[2,1,96,3072]{3,2,1,0:T(8,128)(2,1)}, u32[]{:S(2)}, u32[]{:S(2)}) collective-permute-start(bf16[2,1,96,3072]{3,2,1,0:T(8,128)(2,1)} %constant_dynamic-slice_fusion.19), channel_id=1, source_target_pairs={{0,8},{4,12},{8,0},{12,4},{16,24},{20,28},{24,16},{28,20},{1,9},{5... | collective-permute-start | bytes 3538952 | tf_op jit(solution)/shard_map/ppermute | solution.py:374
  962.6 84.0 %collective-permute-start.51 = (bf16[1,2,96,3072]{3,2,1,0:T(8,128)(2,1)}, bf16[1,2,96,3072]{3,2,1,0:T(8,128)(2,1)}, u32[]{:S(2)}, u32[]{:S(2)}) collective-permute-start(bf16[1,2,96,3072]{3,2,1,0:T(8,128)(2,1)} %constant_dynamic-slice_fusion.18), channel_id=1, source_target_pairs={{0,16},{4,20},{8,24},{12,28},{16,0},{20,4},{24,8},{28,12},{1,17},{... | collective-permute-start | bytes 3538952 | tf_op jit(solution)/shard_map/ppermute | solution.py:374
  971.6 107.5 %all-gather.13.cloned.1.call-start = ((), (), s32[]{:S(2)}) async-start(), calls=%async_computation.11 | async-start | bytes 3538944 | tf_op jit(solution)/shard_map/all_gather | solution.py:912
  (296 other events, 5814.2 us)
Sparse Core Ops, SparseCore 0:
  65.2 92.4 all-gather.6
  161.1 150.6 all-gather.8
  315.2 157.1 all-gather.10
  1046.6 32.4 all-gather.12
